TPU v7x, 32 devices: a whole 2x2x4 slice. The times are simulated.
32 devices in a mesh: groups: 2 (over y), dp: 8 (over z, x), tensor: 2 (over core).
Axes of the slice: x: 2, y: 2, z: 4, core: 2. Of those that a mesh axis runs over, the one named last changes fastest.
Arguments:
- layer_input: bfloat16 [8192, 4096], P(('groups', 'dp'), 'tensor'), parts along dimension 0, may hold values from -6 to 6
- gate_grad: bfloat16 [8192, 14336], P(('groups', 'dp'), 'tensor'), parts along dimension 0, may hold values from -6 to 6
- factor_in: bfloat16 [64, 4096], P(None, 'tensor'), may hold values from -0.09375 to 0.09375
- factor_out: bfloat16 [64, 14336], P(None, 'tensor'), may hold values from -0.046875 to 0.046875
- precondition: float32 [4096, 4096], P(('dp', 'tensor')), may hold values from -0.09375 to 0.09375
- query_grads: bfloat16 [1024, 4096], P(('dp', 'tensor')), may hold values from -6 to 6
Outputs:
- influence: float32 [16, 1024], P('groups', ('dp', 'tensor')), parts along dimension 0
There are 2 independent parts, one for each index of `groups`. A program takes and returns all parts, laid end to end along the dimension named above; an argument that names none is the same for every part. Nothing has to cross between parts.
All inputs are finite; a program needn't handle non-finite values.
Results may differ from a plain program's by a relative error of at most 0.0029.
Values may be sent and summed in bfloat16 or wider, within the bound.
No kernel may reach another device: no remote copies, remote signals or barrier semaphores. Data moves between devices by JAX's collectives and lax.ppermute only.
A program may use at most 64 MiB of HBM per device.

v0:
```python
import math

import jax
import jax.numpy as jnp
from jax import lax
from jax.sharding import PartitionSpec as P


def contract_last(left, right):
    return lax.dot_general(
        left, right, (((1,), (1,)), ((), ())), preferred_element_type=jnp.float32
    )


def outer_sum(inner_side, outer_side, seq_length):
    product = jnp.dot(inner_side.T, outer_side, precision=lax.Precision.HIGHEST)
    return product.reshape(1, -1) / math.sqrt(seq_length)


def on_device(layer_input, gate_grad, factor_in, factor_out, precondition, query_grads):
    seq_length = layer_input.shape[0]
    pair_count = lax.axis_size("tensor")
    own_rows = precondition.shape[0]
    inner_part = contract_last(layer_input, factor_in)
    outer_part = contract_last(gate_grad, factor_out)
    inner_side, outer_side = (
        lax.psum_scatter(inner_part, "tensor", scatter_dimension=0, tiled=True),
        lax.psum_scatter(outer_part, "tensor", scatter_dimension=0, tiled=True),
    )
    sequence_part = outer_sum(inner_side, outer_side, seq_length)
    pieces = lax.all_to_all(
        sequence_part, ("dp", "tensor"), split_axis=1, concat_axis=0, tiled=True
    )
    col_block = pieces.reshape(-1, pair_count, own_rows).sum(axis=1)
    partial_value = jnp.dot(col_block, precondition, precision=lax.Precision.HIGHEST)
    rounded = lax.psum(partial_value, ("dp", "tensor")).astype(jnp.bfloat16)
    return contract_last(rounded, query_grads) / math.sqrt(precondition.shape[1])


def solution(mesh):
    in_specs = (
        P(("groups", "dp"), "tensor"),
        P(("groups", "dp"), "tensor"),
        P(None, "tensor"),
        P(None, "tensor"),
        P(("dp", "tensor"), None),
        P(("dp", "tensor"), None),
    )
    out_specs = P("groups", ("dp", "tensor"))
    return jax.shard_map(
        on_device, mesh=mesh, in_specs=in_specs, out_specs=out_specs, check_vma=False
    )
```

profile of v0, /device:TPU:0, one launch (start us, length us, event | category | flops | bytes accessed | tf_op | source)
XLA Modules:
  0.0 116.3 jit_solution(8532220011668995609)
XLA Ops:
  6.5 0.0 copy-start
  6.5 0.0 reduce-scatter.3.cloned.1.call-start
  6.5 1.6 %copy-done = bf16[512,2048]{1,0:T(8,128)(2,1)S(1)} copy-done((bf16[512,2048]{1,0:T(8,128)(2,1)S(1)}, bf16[512,2048]{1,0:T(8,128)(2,1)}, u32[]{:S(2)}) %copy-start) | copy-done | bytes 2097176
  8.1 2.3 %fusion.1 = f32[512,64]{1,0:T(8,128)} fusion(bf16[512,2048]{1,0:T(8,128)(2,1)S(1)} %copy-done, bf16[64,2048]{1,0:T(8,128)(2,1)} %param.8), kind=kOutput, calls=%fused_computation.3 | convolution fusion | flops 134217728 | bytes 2490368 | tf_op jit(solution)/shard_map/dot_general | solution.py:10
  10.5 0.0 reduce-scatter.3.cloned.1.call-update
  10.5 0.0 reduce-scatter.5.cloned.1.call-start
  10.5 6.0 %fusion.2 = f32[512,64]{1,0:T(8,128)} fusion(bf16[512,7168]{1,0:T(8,128)(2,1)} %param.7, bf16[64,7168]{1,0:T(8,128)(2,1)} %param.9), kind=kOutput, calls=%fused_computation.4 | convolution fusion | flops 469762048 | bytes 8388608 | tf_op jit(solution)/shard_map/dot_general | solution.py:10
  16.6 0.0 copy-start.1
  16.6 0.0 reduce-scatter.5.cloned.1.call-update
  16.6 4.4 %reduce-scatter.3.cloned.1.call-done = f32[256,64]{1,0:T(8,128)} async-done(((f32[512,64]{1,0:T(8,128)}), f32[256,64]{1,0:T(8,128)}) %reduce-scatter.3.cloned.1.call-update) | async-done | bytes 65552 | tf_op jit(solution)/shard_map/reduce_scatter | solution.py:27
  21.0 11.2 %reduce-scatter.5.cloned.1.call-done = f32[256,64]{1,0:T(8,128)} async-done(((f32[512,64]{1,0:T(8,128)}), f32[256,64]{1,0:T(8,128)}) %reduce-scatter.5.cloned.1.call-update) | async-done | bytes 65552 | tf_op jit(solution)/shard_map/reduce_scatter | solution.py:28
  32.2 1.3 %convolution_multiply_fusion = f32[64,64]{1,0:T(8,128)S(1)} fusion(f32[256,64]{1,0:T(8,128)} %reduce-scatter.3.cloned.1.call-done, f32[256,64]{1,0:T(8,128)} %reduce-scatter.5.cloned.1.call-done), kind=kOutput, calls=%fused_computation | convolution fusion | flops 12587008 | bytes 147456 | tf_op jit(solution)/shard_map/dot_general | solution.py:16
  33.5 0.1 div.19
  33.6 12.1 %all_to_all.10 = f32[1,16,256]{2,0,1:T(1,128)S(1)} all-to-all(f32[1,16,256]{2,0,1:T(1,128)S(1)} %div.19), channel_id=1, replica_groups=mesh['groups'=2,'dp'=8,'tensor'=2] {'dp','tensor'}, dimensions={1} | all-to-all | bytes 32768 | tf_op jit(solution)/shard_map/all_to_all | solution.py:31
  45.8 4.3 %fusion.3 = f32[8,4096]{1,0:T(8,128)S(1)} fusion(f32[8,256]{1,0:T(8,128)S(1)} %reduce_sum.9, f32[256,4096]{1,0:T(8,128)} %param.10), kind=kOutput, calls=%fused_computation.5 | convolution fusion | flops 100663296 | bytes 4333568 | tf_op jit(solution)/shard_map/dot_general | solution.py:35
  50.1 58.5 %all-reduce.1 = bf16[8,4096]{1,0:T(8,128)(2,1)S(1)} all-reduce(f32[8,4096]{1,0:T(8,128)S(1)} %fusion.3), channel_id=1, replica_groups=mesh['groups'=2,'dp'=8,'tensor'=2] {'dp','tensor'}, use_global_device_ids=true, to_apply=%region_3.0 | all-reduce | flops 32768 | bytes 196608 | tf_op jit(solution)/shard_map/psum | solution.py:36
  108.6 0.0 copy-done.1
  108.7 0.8 convolution_multiply_fusion.1
  (3 shorter events, 0.1 us)
Async XLA Ops:
  6.5 1.6 %copy-start = (bf16[512,2048]{1,0:T(8,128)(2,1)S(1)}, bf16[512,2048]{1,0:T(8,128)(2,1)}, u32[]{:S(2)}) copy-start(bf16[512,2048]{1,0:T(8,128)(2,1)} %param.6) | copy-start | bytes 6291460
  6.5 14.5 %reduce-scatter.3.cloned.1.call-start = ((), (), s32[]{:S(2)}) async-start(), calls=%async_computation.3 | async-start | bytes 393216 | tf_op jit(solution)/shard_map/reduce_scatter | solution.py:27
  10.5 21.7 %reduce-scatter.5.cloned.1.call-start = ((), (), s32[]{:S(2)}) async-start(), calls=%async_computation.4 | async-start | bytes 393216 | tf_op jit(solution)/shard_map/reduce_scatter | solution.py:28
  16.6 92.1 %copy-start.1 = (bf16[64,4096]{1,0:T(8,128)(2,1)S(1)}, bf16[64,4096]{1,0:T(8,128)(2,1)}, u32[]{:S(2)}) copy-start(bf16[64,4096]{1,0:T(8,128)(2,1)} %param.11) | copy-start | bytes 1572868
Sparse Core Ops, SparseCore 0:
  10.6 10.3 reduce-scatter.2
  23.3 8.8 reduce-scatter.4
where the time goes:
time: 117 us; the launch traced here: 116 us
  blocking collectives  70.7 us (60%)
  waiting for transfers between devices  15.6 us (13%)
  matrix products  14.8 us (13%)
  between operations  13.4 us (11%)
  local copies, waits for them, and re-layouts  1.69 us (1%)
    psum x1, blocking collectives, on_device(): rounded = lax.psum(partial_value, ('dp', 'tensor')).astype(jnp.bfloat16)  58.5 us
    all_to_all x1, blocking collectives, on_device(): lax.all_to_all(sequence_part, ('dp', 'tensor'), split_axis=1, concat_axis...  12.1 us
    reduce_scatter x1, waiting for transfers between devices, on_device(): lax.psum_scatter(outer_part, 'tensor', scatter_dimension=0, tiled=True)  11.2 us
    dot_general x3, matrix products, contract_last(): lax.dot_general(left, right, (((1,), (1,)), ((), ())), preferred_element_...  9.2 us
    reduce_scatter x1, waiting for transfers between devices, on_device(): lax.psum_scatter(inner_part, 'tensor', scatter_dimension=0, tiled=True)  4.43 us
    dot_general x1, matrix products, on_device(): jnp.dot(col_block, precondition, precision=lax.Precision.HIGHEST)  4.26 us
  transfers between devices with their start and end apart: 2, of which 2 were waited for; matrix products, arithmetic and copies ran while one was open for 5% of the time, Pallas kernels for 0%

commit v1 on v0

v1 whole, which is shorter than its diff:
```python
import math

import jax
import jax.numpy as jnp
from jax import lax
from jax.sharding import PartitionSpec as P


def contract_last(left, right, precision=None):
    return lax.dot_general(
        left,
        right,
        (((1,), (1,)), ((), ())),
        precision=precision,
        preferred_element_type=jnp.float32,
    )


def swap(value, axis, bit):
    size = lax.axis_size(axis)
    return lax.ppermute(value, axis, [(i, i ^ bit) for i in range(size)])


def steps(size):
    return [1 << i for i in range(size.bit_length() - 1)]


def ordered(first, mine, other, axis):
    return jnp.where(
        first,
        jnp.concatenate((mine, other), axis),
        jnp.concatenate((other, mine), axis),
    )


def on_device(layer_input, gate_grad, factor_in, factor_out, precondition, query_grads):
    seq_length = layer_input.shape[0]
    own_rows, width = precondition.shape
    dp, dp_size = lax.axis_index("dp"), lax.axis_size("dp")
    core = lax.axis_index("tensor")

    inner = contract_last(factor_in, layer_input)
    inner_other = swap(inner, "tensor", 1)
    outer = contract_last(factor_out, gate_grad)
    outer_other = swap(outer, "tensor", 1)
    gradient = contract_last(
        inner + inner_other, outer + outer_other, lax.Precision.HIGHEST
    ) * (1 / math.sqrt(seq_length))

    blocks = gradient.reshape(dp_size, 2, own_rows)
    blocks = lax.dynamic_index_in_dim(blocks, core, 1, keepdims=False)[None]
    for bit in steps(dp_size):
        other = swap(blocks, "dp", bit)
        blocks = ordered((dp & bit) == 0, blocks, other, 0)
    col_block = lax.dynamic_index_in_dim(blocks, dp, 1, keepdims=False)

    partial = jnp.dot(col_block, precondition, precision=lax.Precision.HIGHEST)

    low, high = partial[:, : width // 2], partial[:, width // 2 :]
    given = jnp.where(core == 0, high, low)
    total = jnp.where(core == 0, low, high) + swap(given, "tensor", 1)
    for bit in steps(dp_size):
        total = total + swap(total, "dp", bit)

    rounded = total.astype(jnp.bfloat16)
    rounded = ordered(core == 0, rounded, swap(rounded, "tensor", 1), 1)
    return contract_last(rounded, query_grads) * (1 / math.sqrt(width))


def solution(mesh):
    in_specs = (
        P(("groups", "dp"), "tensor"),
        P(("groups", "dp"), "tensor"),
        P(None, "tensor"),
        P(None, "tensor"),
        P(("dp", "tensor"), None),
        P(("dp", "tensor"), None),
    )
    out_specs = P("groups", ("dp", "tensor"))
    return jax.shard_map(
        on_device, mesh=mesh, in_specs=in_specs, out_specs=out_specs, check_vma=False
    )
```

time: 117 us -> 46.5 us (0.40)
  blocking collectives: 70.7 us -> 0 us
  starting transfers between devices: 0.04 us -> 15.6 us
  between operations: 13.4 us -> 0.08 us
  matrix products: 14.8 us -> 12.8 us
    psum x1 -> x0, blocking collectives: 58.5 us -> none  [on_device(): rounded = lax.psum(partial_value, ('dp', 'tensor')).astype(jnp.bfloat16)]
    ppermute x0 -> x10, waiting for transfers between devices: none -> 16 us  [swap(): return lax.ppermute(value, axis, [(i, i ^ bit) for i in range(size)])]
    ppermute x0 -> x10, starting transfers between devices: none -> 15.6 us  [swap(): return lax.ppermute(value, axis, [(i, i ^ bit) for i in range(size)])]
    reduce_scatter x2 -> x0, waiting for transfers between devices: 15.6 us -> none  [the longest x1 11.2 us: on_device(): lax.psum_scatter(outer_part, 'tensor', scatter_dimension=0, tiled=True)]
    all_to_all x1 -> x0, blocking collectives: 12.1 us -> none  [on_device(): lax.all_to_all(sequence_part, ('dp', 'tensor'), split_axis=1, concat_axis...]
    dot_general x5, matrix products: 14.8 us -> 12.8 us  [the longest x4 8.55 us: contract_last(): lax.dot_general(left, right, (((1,), (1,)), ((), ())), precision=precisio...]
  transfers between devices with their start and end apart: 2 -> 10, of which waited for: 2 -> 9; matrix products, arithmetic and copies ran while one was open for 5% -> 12% of each run, Pallas kernels for 0% -> 0%
where the time goes in v1:
time: 46.5 us; the launch traced here: 46.3 us
  waiting for transfers between devices  16 us (34%)
  starting transfers between devices  15.6 us (34%)
  matrix products  12.8 us (28%)
  local copies, waits for them, and re-layouts  1.69 us (4%)
    ppermute x10, waiting for transfers between devices, swap(): return lax.ppermute(value, axis, [(i, i ^ bit) for i in range(size)])  16 us
    ppermute x10, starting transfers between devices, swap(): return lax.ppermute(value, axis, [(i, i ^ bit) for i in range(size)])  15.6 us
    dot_general x4, matrix products, contract_last(): lax.dot_general(left, right, (((1,), (1,)), ((), ())), precision=precisio...  8.55 us
    dot_general x1, matrix products, on_device(): partial = jnp.dot(col_block, precondition, precision=lax.Precision.HIGHEST)  4.26 us
    unnamed x4, local copies, waits for them, and re-layouts  1.6 us
  transfers between devices with their start and end apart: 10, of which 9 were waited for; matrix products, arithmetic and copies ran while one was open for 12% of the time, Pallas kernels for 0%

profile of v1, /device:TPU:0, one launch (start us, length us, event | category | flops | bytes accessed | tf_op | source)
XLA Modules:
  0.0 46.3 jit_solution(2234746372633373382)
XLA Ops:
  0.0 0.0 copy-start
  0.0 1.6 %copy-done = bf16[512,2048]{1,0:T(8,128)(2,1)S(1)} copy-done((bf16[512,2048]{1,0:T(8,128)(2,1)S(1)}, bf16[512,2048]{1,0:T(8,128)(2,1)}, u32[]{:S(2)}) %copy-start) | copy-done | bytes 2097176
  1.6 1.7 %fusion.19 = f32[64,512]{1,0:T(8,128)S(1)} fusion(bf16[64,2048]{1,0:T(8,128)(2,1)} %param.8, bf16[512,2048]{1,0:T(8,128)(2,1)S(1)} %copy-done), kind=kOutput, calls=%fused_computation.30 | convolution fusion | flops 134217728 | bytes 2490368 | tf_op jit(solution)/shard_map/dot_general | solution.py:10
  3.3 0.5 %collective-permute-start = (f32[64,512]{1,0:T(8,128)S(1)}, f32[64,512]{1,0:T(8,128)S(1)}, u32[]{:S(2)}, u32[]{:S(2)}) collective-permute-start(f32[64,512]{1,0:T(8,128)S(1)} %fusion.19), channel_id=1, source_target_pairs={{0,1},{1,0},{2,3},{3,2},{4,5},{5,4},{6,7},{7,6},{8,9},{9,8},{10,11... | collective-permute-start | bytes 393224 | tf_op jit(solution)/shard_map/ppermute | solution.py:21
  3.8 5.7 %fusion.20 = f32[64,512]{1,0:T(8,128)S(1)} fusion(bf16[64,7168]{1,0:T(8,128)(2,1)} %param.9, bf16[512,7168]{1,0:T(8,128)(2,1)} %param.7), kind=kOutput, calls=%fused_computation.31 | convolution fusion | flops 469762048 | bytes 8388608 | tf_op jit(solution)/shard_map/dot_general | solution.py:10
  9.5 0.0 copy-start.1
  9.5 0.1 collective-permute-start.1
  9.7 0.0 collective-permute-done
  9.7 1.3 %collective-permute-done.1 = f32[64,512]{1,0:T(8,128)S(1)} collective-permute-done((f32[64,512]{1,0:T(8,128)S(1)}, f32[64,512]{1,0:T(8,128)S(1)}, u32[]{:S(2)}, u32[]{:S(2)}) %collective-permute-start.1) | collective-permute-done | bytes 131104 | tf_op jit(solution)/shard_map/ppermute | solution.py:21
  11.0 0.3 convolution_multiply_fusion
  11.2 0.1 reshape.4
  11.3 2.7 %collective-permute-start.2 = (f32[1,8,256]{2,0,1:T(1,128)S(1)}, f32[1,8,256]{2,0,1:T(1,128)S(1)}, u32[]{:S(2)}, u32[]{:S(2)}) collective-permute-start(f32[1,8,256]{2,0,1:T(1,128)S(1)} %dynamic-slice_bitcast_fusion), channel_id=1, source_target_pairs={{0,2},{2,0},{4,6},{6,4},{8,10},{10,8},{12,14},{14,12},{1,3},{3,1},... | collective-permute-start | bytes 24584 | tf_op jit(solution)/shard_map/ppermute | solution.py:21
  14.1 1.6 %collective-permute-done.2 = f32[1,8,256]{2,0,1:T(1,128)S(1)} collective-permute-done((f32[1,8,256]{2,0,1:T(1,128)S(1)}, f32[1,8,256]{2,0,1:T(1,128)S(1)}, u32[]{:S(2)}, u32[]{:S(2)}) %collective-permute-start.2) | collective-permute-done | bytes 8224 | tf_op jit(solution)/shard_map/ppermute | solution.py:21
  15.7 2.2 %collective-permute-start.3 = (f32[2,8,256]{2,0,1:T(2,128)S(1)}, f32[2,8,256]{2,0,1:T(2,128)S(1)}, u32[]{:S(2)}, u32[]{:S(2)}) collective-permute-start(f32[2,8,256]{2,0,1:T(2,128)S(1)} %maximum_select_fusion.3), channel_id=1, source_target_pairs={{0,4},{2,6},{4,0},{6,2},{8,12},{10,14},{12,8},{14,10},{1,5},{3,7},... | collective-permute-start | bytes 49160 | tf_op jit(solution)/shard_map/ppermute | solution.py:21
  17.9 1.7 %collective-permute-done.3 = f32[2,8,256]{2,0,1:T(2,128)S(1)} collective-permute-done((f32[2,8,256]{2,0,1:T(2,128)S(1)}, f32[2,8,256]{2,0,1:T(2,128)S(1)}, u32[]{:S(2)}, u32[]{:S(2)}) %collective-permute-start.3) | collective-permute-done | bytes 16416 | tf_op jit(solution)/shard_map/ppermute | solution.py:21
  19.6 3.1 %collective-permute-start.4 = (f32[4,8,256]{2,0,1:T(4,128)S(1)}, f32[4,8,256]{2,0,1:T(4,128)S(1)}, u32[]{:S(2)}, u32[]{:S(2)}) collective-permute-start(f32[4,8,256]{2,0,1:T(4,128)S(1)} %maximum_select_fusion.2), channel_id=1, source_target_pairs={{0,8},{2,10},{4,12},{6,14},{8,0},{10,2},{12,4},{14,6},{1,9},{3,11}... | collective-permute-start | bytes 98312 | tf_op jit(solution)/shard_map/ppermute | solution.py:21
  22.7 1.9 %collective-permute-done.4 = f32[4,8,256]{2,0,1:T(4,128)S(1)} collective-permute-done((f32[4,8,256]{2,0,1:T(4,128)S(1)}, f32[4,8,256]{2,0,1:T(4,128)S(1)}, u32[]{:S(2)}, u32[]{:S(2)}) %collective-permute-start.4) | collective-permute-done | bytes 32800 | tf_op jit(solution)/shard_map/ppermute | solution.py:21
  24.6 4.3 %fusion.11 = f32[8,4096]{1,0:T(8,128)S(1)} fusion(f32[256,4096]{1,0:T(8,128)} %param.10, s32[]{:T(128)S(6)} %select_n.61, f32[4,8,256]{2,0,1:T(4,128)S(1)} %collective-permute-done.4, f32[4,8,256]{2,0,1:T(4,128)S(1)} %maximum_select_fusion.2, pred[]{:T(512)S(6)} %eq.15), kind=kOutput, calls=%fused_computation.23 | convolution fusion | flops 100669440 | bytes 4390917 | tf_op jit(solution)/shard_map/dot_general | solution.py:57
  28.9 0.1 collective-permute-start.5
  29.0 1.2 %collective-permute-done.5 = f32[8,2048]{1,0:T(8,128)S(1)} collective-permute-done((f32[8,2048]{1,0:T(8,128)S(1)}, f32[8,2048]{1,0:T(8,128)S(1)}, u32[]{:S(2)}, u32[]{:S(2)}) %collective-permute-start.5) | collective-permute-done | bytes 65568 | tf_op jit(solution)/shard_map/ppermute | solution.py:21
  30.2 1.9 %collective-permute-start.6 = (f32[8,2048]{1,0:T(8,128)S(1)}, f32[8,2048]{1,0:T(8,128)S(1)}, u32[]{:S(2)}, u32[]{:S(2)}) collective-permute-start(f32[8,2048]{1,0:T(8,128)S(1)} %select_add_fusion), channel_id=1, source_target_pairs={{0,2},{2,0},{4,6},{6,4},{8,10},{10,8},{12,14},{14,12},{1,3},{3,1},... | collective-permute-start | bytes 196616 | tf_op jit(solution)/shard_map/ppermute | solution.py:21
  32.1 2.4 %collective-permute-done.6 = f32[8,2048]{1,0:T(8,128)S(1)} collective-permute-done((f32[8,2048]{1,0:T(8,128)S(1)}, f32[8,2048]{1,0:T(8,128)S(1)}, u32[]{:S(2)}, u32[]{:S(2)}) %collective-permute-start.6) | collective-permute-done | bytes 65568 | tf_op jit(solution)/shard_map/ppermute | solution.py:21
  34.6 2.0 %collective-permute-start.7 = (f32[8,2048]{1,0:T(8,128)S(1)}, f32[8,2048]{1,0:T(8,128)S(1)}, u32[]{:S(2)}, u32[]{:S(2)}) collective-permute-start(f32[8,2048]{1,0:T(8,128)S(1)} %add.31), channel_id=1, source_target_pairs={{0,4},{2,6},{4,0},{6,2},{8,12},{10,14},{12,8},{14,10},{1,5},{3,7},... | collective-permute-start | bytes 196616 | tf_op jit(solution)/shard_map/ppermute | solution.py:21
  36.6 2.4 %collective-permute-done.7 = f32[8,2048]{1,0:T(8,128)S(1)} collective-permute-done((f32[8,2048]{1,0:T(8,128)S(1)}, f32[8,2048]{1,0:T(8,128)S(1)}, u32[]{:S(2)}, u32[]{:S(2)}) %collective-permute-start.7) | collective-permute-done | bytes 65568 | tf_op jit(solution)/shard_map/ppermute | solution.py:21
  38.9 3.0 %collective-permute-start.8 = (f32[8,2048]{1,0:T(8,128)S(1)}, f32[8,2048]{1,0:T(8,128)S(1)}, u32[]{:S(2)}, u32[]{:S(2)}) collective-permute-start(f32[8,2048]{1,0:T(8,128)S(1)} %add.32), channel_id=1, source_target_pairs={{0,8},{2,10},{4,12},{6,14},{8,0},{10,2},{12,4},{14,6},{1,9},{3,11}... | collective-permute-start | bytes 196616 | tf_op jit(solution)/shard_map/ppermute | solution.py:21
  41.9 2.2 %collective-permute-done.8 = f32[8,2048]{1,0:T(8,128)S(1)} collective-permute-done((f32[8,2048]{1,0:T(8,128)S(1)}, f32[8,2048]{1,0:T(8,128)S(1)}, u32[]{:S(2)}, u32[]{:S(2)}) %collective-permute-start.8) | collective-permute-done | bytes 65568 | tf_op jit(solution)/shard_map/ppermute | solution.py:21
  44.2 0.1 collective-permute-start.9
  44.3 1.2 %collective-permute-done.9 = bf16[8,2048]{1,0:T(8,128)(2,1)S(1)} collective-permute-done((bf16[8,2048]{1,0:T(8,128)(2,1)S(1)}, bf16[8,2048]{1,0:T(8,128)(2,1)S(1)}, u32[]{:S(2)}, u32[]{:S(2)}) %collective-permute-start.9) | collective-permute-done | bytes 32800 | tf_op jit(solution)/shard_map/ppermute | solution.py:21
  45.5 0.0 copy-done.1
  45.5 0.8 %convolution_multiply_fusion.1 = f32[8,64]{1,0:T(8,128)} fusion(bf16[64,4096]{1,0:T(8,128)(2,1)S(1)} %copy-done.1, bf16[8,2048]{1,0:T(8,128)(2,1)S(1)} %collective-permute-done.9, bf16[8,2048]{1,0:T(8,128)(2,1)S(1)} %add_convert_fusion, pred[]{:T(512)S(6)} %eq.14), kind=kOutput, calls=%fused_computation.1 | convolution fusion | flops 4489728 | bytes 591873 | tf_op jit(solution)/shard_map/dot_general | solution.py:10
  (8 shorter events, 0.1 us)
Async XLA Ops:
  0.0 1.6 %copy-start = (bf16[512,2048]{1,0:T(8,128)(2,1)S(1)}, bf16[512,2048]{1,0:T(8,128)(2,1)}, u32[]{:S(2)}) copy-start(bf16[512,2048]{1,0:T(8,128)(2,1)} %param.6) | copy-start | bytes 6291460
  3.3 6.4 %collective-permute-start = (f32[64,512]{1,0:T(8,128)S(1)}, f32[64,512]{1,0:T(8,128)S(1)}, u32[]{:S(2)}, u32[]{:S(2)}) collective-permute-start(f32[64,512]{1,0:T(8,128)S(1)} %fusion.19), channel_id=1, source_target_pairs={{0,1},{1,0},{2,3},{3,2},{4,5},{5,4},{6,7},{7,6},{8,9},{9,8},{10,11... | collective-permute-start | bytes 393224 | tf_op jit(solution)/shard_map/ppermute | solution.py:21
  9.5 35.9 %copy-start.1 = (bf16[64,4096]{1,0:T(8,128)(2,1)S(1)}, bf16[64,4096]{1,0:T(8,128)(2,1)}, u32[]{:S(2)}) copy-start(bf16[64,4096]{1,0:T(8,128)(2,1)} %param.11) | copy-start | bytes 1572868
  9.5 1.4 %collective-permute-start.1 = (f32[64,512]{1,0:T(8,128)S(1)}, f32[64,512]{1,0:T(8,128)S(1)}, u32[]{:S(2)}, u32[]{:S(2)}) collective-permute-start(f32[64,512]{1,0:T(8,128)S(1)} %fusion.20), channel_id=1, source_target_pairs={{0,1},{1,0},{2,3},{3,2},{4,5},{5,4},{6,7},{7,6},{8,9},{9,8},{10,11... | collective-permute-start | bytes 393224 | tf_op jit(solution)/shard_map/ppermute | solution.py:21
  11.3 4.3 %collective-permute-start.2 = (f32[1,8,256]{2,0,1:T(1,128)S(1)}, f32[1,8,256]{2,0,1:T(1,128)S(1)}, u32[]{:S(2)}, u32[]{:S(2)}) collective-permute-start(f32[1,8,256]{2,0,1:T(1,128)S(1)} %dynamic-slice_bitcast_fusion), channel_id=1, source_target_pairs={{0,2},{2,0},{4,6},{6,4},{8,10},{10,8},{12,14},{14,12},{1,3},{3,1},... | collective-permute-start | bytes 24584 | tf_op jit(solution)/shard_map/ppermute | solution.py:21
  15.7 3.9 %collective-permute-start.3 = (f32[2,8,256]{2,0,1:T(2,128)S(1)}, f32[2,8,256]{2,0,1:T(2,128)S(1)}, u32[]{:S(2)}, u32[]{:S(2)}) collective-permute-start(f32[2,8,256]{2,0,1:T(2,128)S(1)} %maximum_select_fusion.3), channel_id=1, source_target_pairs={{0,4},{2,6},{4,0},{6,2},{8,12},{10,14},{12,8},{14,10},{1,5},{3,7},... | collective-permute-start | bytes 49160 | tf_op jit(solution)/shard_map/ppermute | solution.py:21
  19.6 5.0 %collective-permute-start.4 = (f32[4,8,256]{2,0,1:T(4,128)S(1)}, f32[4,8,256]{2,0,1:T(4,128)S(1)}, u32[]{:S(2)}, u32[]{:S(2)}) collective-permute-start(f32[4,8,256]{2,0,1:T(4,128)S(1)} %maximum_select_fusion.2), channel_id=1, source_target_pairs={{0,8},{2,10},{4,12},{6,14},{8,0},{10,2},{12,4},{14,6},{1,9},{3,11}... | collective-permute-start | bytes 98312 | tf_op jit(solution)/shard_map/ppermute | solution.py:21
  28.9 1.3 %collective-permute-start.5 = (f32[8,2048]{1,0:T(8,128)S(1)}, f32[8,2048]{1,0:T(8,128)S(1)}, u32[]{:S(2)}, u32[]{:S(2)}) collective-permute-start(f32[8,2048]{1,0:T(8,128)S(1)} %slice_select_fusion), channel_id=1, source_target_pairs={{0,1},{1,0},{2,3},{3,2},{4,5},{5,4},{6,7},{7,6},{8,9},{9,8},{10,11... | collective-permute-start | bytes 196616 | tf_op jit(solution)/shard_map/ppermute | solution.py:21
  30.2 4.3 %collective-permute-start.6 = (f32[8,2048]{1,0:T(8,128)S(1)}, f32[8,2048]{1,0:T(8,128)S(1)}, u32[]{:S(2)}, u32[]{:S(2)}) collective-permute-start(f32[8,2048]{1,0:T(8,128)S(1)} %select_add_fusion), channel_id=1, source_target_pairs={{0,2},{2,0},{4,6},{6,4},{8,10},{10,8},{12,14},{14,12},{1,3},{3,1},... | collective-permute-start | bytes 196616 | tf_op jit(solution)/shard_map/ppermute | solution.py:21
  34.6 4.3 %collective-permute-start.7 = (f32[8,2048]{1,0:T(8,128)S(1)}, f32[8,2048]{1,0:T(8,128)S(1)}, u32[]{:S(2)}, u32[]{:S(2)}) collective-permute-start(f32[8,2048]{1,0:T(8,128)S(1)} %add.31), channel_id=1, source_target_pairs={{0,4},{2,6},{4,0},{6,2},{8,12},{10,14},{12,8},{14,10},{1,5},{3,7},... | collective-permute-start | bytes 196616 | tf_op jit(solution)/shard_map/ppermute | solution.py:21
  38.9 5.3 %collective-permute-start.8 = (f32[8,2048]{1,0:T(8,128)S(1)}, f32[8,2048]{1,0:T(8,128)S(1)}, u32[]{:S(2)}, u32[]{:S(2)}) collective-permute-start(f32[8,2048]{1,0:T(8,128)S(1)} %add.32), channel_id=1, source_target_pairs={{0,8},{2,10},{4,12},{6,14},{8,0},{10,2},{12,4},{14,6},{1,9},{3,11}... | collective-permute-start | bytes 196616 | tf_op jit(solution)/shard_map/ppermute | solution.py:21
  44.2 1.3 %collective-permute-start.9 = (bf16[8,2048]{1,0:T(8,128)(2,1)S(1)}, bf16[8,2048]{1,0:T(8,128)(2,1)S(1)}, u32[]{:S(2)}, u32[]{:S(2)}) collective-permute-start(bf16[8,2048]{1,0:T(8,128)(2,1)S(1)} %add_convert_fusion), channel_id=1, source_target_pairs={{0,1},{1,0},{2,3},{3,2},{4,5},{5,4},{6,7},{7,6},{8,9},{9,8},{10,11... | collective-permute-start | bytes 98312 | tf_op jit(solution)/shard_map/ppermute | solution.py:21

commit v2 on v1

--- a/solution.py
+++ b/solution.py
@@ -3,17 +3,117 @@
 import jax
 import jax.numpy as jnp
 from jax import lax
+from jax.experimental import pallas as pl
+from jax.experimental.pallas import tpu as pltpu
 from jax.sharding import PartitionSpec as P
 
+CHUNK = 1024
+BAND = 512
+LAST = (((1,), (1,)), ((), ()))
 
-def contract_last(left, right, precision=None):
-    return lax.dot_general(
-        left,
-        right,
-        (((1,), (1,)), ((), ())),
-        precision=precision,
-        preferred_element_type=jnp.float32,
-    )
+
+def project_kernel(layer_ref, gate_ref, in_ref, out_ref, sides_ref, left, right, sems):
+    rank = in_ref.shape[0]
+    counts = (layer_ref.shape[1] // CHUNK, gate_ref.shape[1] // CHUNK)
+    copies = []
+    for part, (big, small) in enumerate(((layer_ref, in_ref), (gate_ref, out_ref))):
+        for c in range(counts[part]):
+            slot = len(copies)
+            cols = pl.ds(c * CHUNK, CHUNK)
+            copies.append(
+                (
+                    pltpu.make_async_copy(
+                        small.at[:, cols],
+                        right.at[slot, pl.ds(part * rank, rank)],
+                        sems.at[0, slot],
+                    ),
+                    pltpu.make_async_copy(
+                        big.at[:, cols], left.at[slot], sems.at[1, slot]
+                    ),
+                )
+            )
+    for pair in copies:
+        for copy in pair:
+            copy.start()
+    blank = jnp.zeros((rank, CHUNK), right.dtype)
+    for slot in range(len(copies)):
+        right[slot, pl.ds(rank if slot < counts[0] else 0, rank)] = blank
+    total = None
+    for slot, pair in enumerate(copies):
+        for copy in pair:
+            copy.wait()
+        term = lax.dot_general(
+            left[slot], right[slot], LAST, preferred_element_type=jnp.float32
+        )
+        total = term if total is None else total + term
+    sides_ref[...] = total
+
+
+def project(layer_input, gate_grad, factor_in, factor_out):
+    tokens, rank = layer_input.shape[0], factor_in.shape[0]
+    features = layer_input.shape[1] + gate_grad.shape[1]
+    slots = features // CHUNK
+    return pl.pallas_call(
+        project_kernel,
+        out_shape=jax.ShapeDtypeStruct((tokens, 2 * rank), jnp.float32),
+        in_specs=[pl.BlockSpec(memory_space=pl.ANY)] * 4,
+        out_specs=pl.BlockSpec(memory_space=pltpu.VMEM),
+        scratch_shapes=[
+            pltpu.VMEM((slots, tokens, CHUNK), layer_input.dtype),
+            pltpu.VMEM((slots, 2 * rank, CHUNK), factor_in.dtype),
+            pltpu.SemaphoreType.DMA((2, slots)),
+        ],
+        compiler_params=pltpu.CompilerParams(vmem_limit_bytes=24 << 20),
+        cost_estimate=pl.CostEstimate(
+            flops=2 * tokens * features * rank,
+            bytes_accessed=2 * (tokens + rank) * features,
+            transcendentals=0,
+        ),
+        name="project",
+    )(layer_input, gate_grad, factor_in, factor_out)
+
+
+def split(value, terms):
+    parts = []
+    for _ in range(terms):
+        part = value.astype(jnp.bfloat16)
+        value = value - part.astype(jnp.float32)
+        parts.append(part)
+    return parts
+
+
+def precondition_kernel(grads_ref, matrix_ref, result_ref):
+    seqs = grads_ref.shape[0]
+    grads = jnp.concatenate(split(grads_ref[...], 3), axis=0)
+    width = matrix_ref.shape[1]
+    for start in range(0, width, BAND):
+        high, low = split(matrix_ref[:, start : start + BAND], 2)
+        by_high = jnp.dot(grads, high, preferred_element_type=jnp.float32)
+        by_low = jnp.dot(grads[: 2 * seqs], low, preferred_element_type=jnp.float32)
+        small = by_high[2 * seqs :] + by_low[seqs:]
+        middle = by_high[seqs : 2 * seqs] + by_low[:seqs]
+        result_ref[:, start : start + BAND] = by_high[:seqs] + (middle + small)
+
+
+def precondition_rows(grads, matrix):
+    seqs, (rows, width) = grads.shape[0], matrix.shape
+    return pl.pallas_call(
+        precondition_kernel,
+        out_shape=jax.ShapeDtypeStruct((seqs, width), jnp.float32),
+        in_specs=[pl.BlockSpec(memory_space=pltpu.VMEM)] * 2,
+        out_specs=pl.BlockSpec(memory_space=pltpu.VMEM),
+        compiler_params=pltpu.CompilerParams(vmem_limit_bytes=24 << 20),
+        cost_estimate=pl.CostEstimate(
+            flops=2 * seqs * rows * width,
+            bytes_accessed=4 * rows * width,
+            transcendentals=0,
+        ),
+        name="precondition",
+    )(grads, matrix)
+
+
+def contract_last(left, right):
+    return lax.dot_general(left, right, LAST, preferred_element_type=jnp.float32)
 
 
 def swap(value, axis, bit):
@@ -34,17 +134,18 @@
 
 
 def on_device(layer_input, gate_grad, factor_in, factor_out, precondition, query_grads):
-    seq_length = layer_input.shape[0]
+    seq_length, rank = layer_input.shape[0], factor_in.shape[0]
     own_rows, width = precondition.shape
     dp, dp_size = lax.axis_index("dp"), lax.axis_size("dp")
     core = lax.axis_index("tensor")
 
-    inner = contract_last(factor_in, layer_input)
-    inner_other = swap(inner, "tensor", 1)
-    outer = contract_last(factor_out, gate_grad)
-    outer_other = swap(outer, "tensor", 1)
-    gradient = contract_last(
-        inner + inner_other, outer + outer_other, lax.Precision.HIGHEST
+    sides = project(layer_input, gate_grad, factor_in, factor_out)
+    sides = sides + swap(sides, "tensor", 1)
+    gradient = lax.dot_general(
+        sides[:, :rank],
+        sides[:, rank:],
+        (((0,), (0,)), ((), ())),
+        precision=lax.Precision.HIGHEST,
     ) * (1 / math.sqrt(seq_length))
 
     blocks = gradient.reshape(dp_size, 2, own_rows)
@@ -54,7 +155,7 @@
         blocks = ordered((dp & bit) == 0, blocks, other, 0)
     col_block = lax.dynamic_index_in_dim(blocks, dp, 1, keepdims=False)
 
-    partial = jnp.dot(col_block, precondition, precision=lax.Precision.HIGHEST)
+    partial = precondition_rows(col_block, precondition)
 
     low, high = partial[:, : width // 2], partial[:, width // 2 :]
     given = jnp.where(core == 0, high, low)

time: 46.5 us -> 50.6 us (1.088)
  matrix products: 12.8 us -> 1.52 us
  Pallas kernels: 0 us -> 7.82 us
  local copies, waits for them, and re-layouts: 1.69 us -> 9.14 us
    dot_general x5 -> x2, matrix products: 12.8 us -> 1.52 us  [the longest x1 0.85 us: contract_last(): lax.dot_general(left, right, LAST, preferred_element_type=jnp.float32)]
    pallas_call x0 -> x2, Pallas kernels: none -> 7.82 us  [the longest x1 6.97 us: project(): pl.pallas_call(project_kernel, out_shape=jax.ShapeDtypeStruct((tokens, 2...]
    unnamed x4 -> x12, local copies, waits for them, and re-layouts: 1.6 us -> 9.05 us
    ppermute x10 -> x9, waiting for transfers between devices: 16 us -> 15.9 us  [swap(): return lax.ppermute(value, axis, [(i, i ^ bit) for i in range(size)])]
    ppermute x10 -> x9, starting transfers between devices: 15.6 us -> 15.7 us  [swap(): return lax.ppermute(value, axis, [(i, i ^ bit) for i in range(size)])]
  transfers between devices with their start and end apart: 10 -> 9, of which waited for: 9 -> 9; matrix products, arithmetic and copies ran while one was open for 12% -> 0% of each run, Pallas kernels for 0% -> 0%
where the time goes in v2:
time: 50.6 us; the launch traced here: 50.4 us
  waiting for transfers between devices  15.9 us (31%)
  starting transfers between devices  15.7 us (31%)
  local copies, waits for them, and re-layouts  9.14 us (18%)
  Pallas kernels  7.82 us (15%)
  matrix products  1.52 us (3%)
    ppermute x9, waiting for transfers between devices, swap(): return lax.ppermute(value, axis, [(i, i ^ bit) for i in range(size)])  15.9 us
    ppermute x9, starting transfers between devices, swap(): return lax.ppermute(value, axis, [(i, i ^ bit) for i in range(size)])  15.7 us
    unnamed x12, local copies, waits for them, and re-layouts  9.05 us
    pallas_call x1, Pallas kernels, project(): pl.pallas_call(project_kernel, out_shape=jax.ShapeDtypeStruct((tokens, 2...  6.97 us
  transfers between devices with their start and end apart: 9, of which 9 were waited for; matrix products, arithmetic and copies ran while one was open for 0% of the time, Pallas kernels for 0%

profile of v2, /device:TPU:0, one launch (start us, length us, event | category | flops | bytes accessed | tf_op | source)
XLA Modules:
  0.0 50.4 jit_solution(1715271394393247051)
XLA Ops:
  0.0 0.0 copy-start
  0.0 0.0 copy-start.1
  0.0 3.1 %copy-done.1 = bf16[512,7168]{1,0:T(8,128)(2,1)S(1)} copy-done((bf16[512,7168]{1,0:T(8,128)(2,1)S(1)}, bf16[512,7168]{1,0:T(8,128)(2,1)}, u32[]{:S(2)}) %copy-start.1) | copy-done | bytes 7340056
  3.1 0.0 copy-start.3
  3.1 1.6 %copy-done.3 = bf16[512,2048]{1,0:T(8,128)(2,1)S(1)} copy-done((bf16[512,2048]{1,0:T(8,128)(2,1)S(1)}, bf16[512,2048]{1,0:T(8,128)(2,1)}, u32[]{:S(2)}) %copy-start.3) | copy-done | bytes 2097176
  4.7 0.0 copy-start.4
  4.7 1.2 %copy-done.4 = bf16[64,7168]{1,0:T(8,128)(2,1)S(1)} copy-done((bf16[64,7168]{1,0:T(8,128)(2,1)S(1)}, bf16[64,7168]{1,0:T(8,128)(2,1)}, u32[]{:S(2)}) %copy-start.4) | copy-done | bytes 917528
  5.9 0.0 copy-start.5
  5.9 0.9 %copy-done.5 = bf16[64,2048]{1,0:T(8,128)(2,1)S(1)} copy-done((bf16[64,2048]{1,0:T(8,128)(2,1)S(1)}, bf16[64,2048]{1,0:T(8,128)(2,1)}, u32[]{:S(2)}) %copy-start.5) | copy-done | bytes 262168
  6.9 7.0 %project.1 = f32[512,128]{1,0:T(8,128)S(1)} custom-call(bf16[512,2048]{1,0:T(8,128)(2,1)S(1)} %copy-done.3, bf16[512,7168]{1,0:T(8,128)(2,1)S(1)} %copy-done.1, bf16[64,2048]{1,0:T(8,128)(2,1)S(1)} %copy-done.5, bf16[64,7168]{1,0:T(8,128)(2,1)S(1)} %copy-done.4), custom_call_target="tpu_custom_call" | custom-call | flops 603979776 | bytes 10616832 | tf_op jit(solution)/shard_map/project/pallas_call | solution.py:56
  13.8 0.5 %collective-permute-start = (f32[512,128]{1,0:T(8,128)S(1)}, f32[512,128]{1,0:T(8,128)S(1)}, u32[]{:S(2)}, u32[]{:S(2)}) collective-permute-start(f32[512,128]{1,0:T(8,128)S(1)} %project.1), channel_id=1, source_target_pairs={{0,1},{1,0},{2,3},{3,2},{4,5},{5,4},{6,7},{7,6},{8,9},{9,8},{10,11... | collective-permute-start | bytes 786440 | tf_op jit(solution)/shard_map/ppermute | solution.py:121
  14.4 1.2 %collective-permute-done = f32[512,128]{1,0:T(8,128)S(1)} collective-permute-done((f32[512,128]{1,0:T(8,128)S(1)}, f32[512,128]{1,0:T(8,128)S(1)}, u32[]{:S(2)}, u32[]{:S(2)}) %collective-permute-start) | collective-permute-done | bytes 262176 | tf_op jit(solution)/shard_map/ppermute | solution.py:121
  15.6 0.7 %convolution_multiply_fusion = f32[64,64]{1,0:T(8,128)S(1)} fusion(f32[512,128]{1,0:T(8,128)S(1)} %add.23), kind=kOutput, calls=%fused_computation | convolution fusion | flops 25169920 | bytes 540672 | tf_op jit(solution)/shard_map/dot_general | solution.py:144
  16.2 0.1 reshape.4
  16.3 2.9 %collective-permute-start.1 = (f32[1,8,256]{2,0,1:T(1,128)S(1)}, f32[1,8,256]{2,0,1:T(1,128)S(1)}, u32[]{:S(2)}, u32[]{:S(2)}) collective-permute-start(f32[1,8,256]{2,0,1:T(1,128)S(1)} %dynamic-slice_bitcast_fusion), channel_id=1, source_target_pairs={{0,2},{2,0},{4,6},{6,4},{8,10},{10,8},{12,14},{14,12},{1,3},{3,1},... | collective-permute-start | bytes 24584 | tf_op jit(solution)/shard_map/ppermute | solution.py:121
  19.3 1.6 %collective-permute-done.1 = f32[1,8,256]{2,0,1:T(1,128)S(1)} collective-permute-done((f32[1,8,256]{2,0,1:T(1,128)S(1)}, f32[1,8,256]{2,0,1:T(1,128)S(1)}, u32[]{:S(2)}, u32[]{:S(2)}) %collective-permute-start.1) | collective-permute-done | bytes 8224 | tf_op jit(solution)/shard_map/ppermute | solution.py:121
  20.9 2.2 %collective-permute-start.2 = (f32[2,8,256]{2,0,1:T(2,128)S(1)}, f32[2,8,256]{2,0,1:T(2,128)S(1)}, u32[]{:S(2)}, u32[]{:S(2)}) collective-permute-start(f32[2,8,256]{2,0,1:T(2,128)S(1)} %maximum_select_fusion.3), channel_id=1, source_target_pairs={{0,4},{2,6},{4,0},{6,2},{8,12},{10,14},{12,8},{14,10},{1,5},{3,7},... | collective-permute-start | bytes 49160 | tf_op jit(solution)/shard_map/ppermute | solution.py:121
  23.1 1.7 %collective-permute-done.2 = f32[2,8,256]{2,0,1:T(2,128)S(1)} collective-permute-done((f32[2,8,256]{2,0,1:T(2,128)S(1)}, f32[2,8,256]{2,0,1:T(2,128)S(1)}, u32[]{:S(2)}, u32[]{:S(2)}) %collective-permute-start.2) | collective-permute-done | bytes 16416 | tf_op jit(solution)/shard_map/ppermute | solution.py:121
  24.9 3.1 %collective-permute-start.3 = (f32[4,8,256]{2,0,1:T(4,128)S(1)}, f32[4,8,256]{2,0,1:T(4,128)S(1)}, u32[]{:S(2)}, u32[]{:S(2)}) collective-permute-start(f32[4,8,256]{2,0,1:T(4,128)S(1)} %maximum_select_fusion.2), channel_id=1, source_target_pairs={{0,8},{2,10},{4,12},{6,14},{8,0},{10,2},{12,4},{14,6},{1,9},{3,11}... | collective-permute-start | bytes 98312 | tf_op jit(solution)/shard_map/ppermute | solution.py:121
  28.0 1.9 %collective-permute-done.3 = f32[4,8,256]{2,0,1:T(4,128)S(1)} collective-permute-done((f32[4,8,256]{2,0,1:T(4,128)S(1)}, f32[4,8,256]{2,0,1:T(4,128)S(1)}, u32[]{:S(2)}, u32[]{:S(2)}) %collective-permute-start.3) | collective-permute-done | bytes 32800 | tf_op jit(solution)/shard_map/ppermute | solution.py:121
  29.9 0.0 copy-start.2
  29.9 2.2 %copy-done.2 = f32[256,4096]{1,0:T(8,128)S(1)} copy-done((f32[256,4096]{1,0:T(8,128)S(1)}, f32[256,4096]{1,0:T(8,128)}, u32[]{:S(2)}) %copy-start.2) | copy-done | bytes 4194328
  32.1 0.9 %precondition.1 = f32[8,4096]{1,0:T(8,128)S(1)} custom-call(f32[8,256]{1,0:T(8,128)S(1)} %fusion.10.grads_ref, f32[256,4096]{1,0:T(8,128)S(1)} %copy-done.2), custom_call_target="tpu_custom_call" | custom-call | flops 16777216 | bytes 4194304 | tf_op jit(solution)/shard_map/precondition/pallas_call | solution.py:100
  33.0 0.1 collective-permute-start.4
  33.0 1.2 %collective-permute-done.4 = f32[8,2048]{1,0:T(8,128)S(1)} collective-permute-done((f32[8,2048]{1,0:T(8,128)S(1)}, f32[8,2048]{1,0:T(8,128)S(1)}, u32[]{:S(2)}, u32[]{:S(2)}) %collective-permute-start.4) | collective-permute-done | bytes 65568 | tf_op jit(solution)/shard_map/ppermute | solution.py:121
  34.3 1.9 %collective-permute-start.5 = (f32[8,2048]{1,0:T(8,128)S(1)}, f32[8,2048]{1,0:T(8,128)S(1)}, u32[]{:S(2)}, u32[]{:S(2)}) collective-permute-start(f32[8,2048]{1,0:T(8,128)S(1)} %select_add_fusion), channel_id=1, source_target_pairs={{0,2},{2,0},{4,6},{6,4},{8,10},{10,8},{12,14},{14,12},{1,3},{3,1},... | collective-permute-start | bytes 196616 | tf_op jit(solution)/shard_map/ppermute | solution.py:121
  36.2 2.4 %collective-permute-done.5 = f32[8,2048]{1,0:T(8,128)S(1)} collective-permute-done((f32[8,2048]{1,0:T(8,128)S(1)}, f32[8,2048]{1,0:T(8,128)S(1)}, u32[]{:S(2)}, u32[]{:S(2)}) %collective-permute-start.5) | collective-permute-done | bytes 65568 | tf_op jit(solution)/shard_map/ppermute | solution.py:121
  38.6 2.0 %collective-permute-start.6 = (f32[8,2048]{1,0:T(8,128)S(1)}, f32[8,2048]{1,0:T(8,128)S(1)}, u32[]{:S(2)}, u32[]{:S(2)}) collective-permute-start(f32[8,2048]{1,0:T(8,128)S(1)} %add.27), channel_id=1, source_target_pairs={{0,4},{2,6},{4,0},{6,2},{8,12},{10,14},{12,8},{14,10},{1,5},{3,7},... | collective-permute-start | bytes 196616 | tf_op jit(solution)/shard_map/ppermute | solution.py:121
  40.6 2.4 %collective-permute-done.6 = f32[8,2048]{1,0:T(8,128)S(1)} collective-permute-done((f32[8,2048]{1,0:T(8,128)S(1)}, f32[8,2048]{1,0:T(8,128)S(1)}, u32[]{:S(2)}, u32[]{:S(2)}) %collective-permute-start.6) | collective-permute-done | bytes 65568 | tf_op jit(solution)/shard_map/ppermute | solution.py:121
  43.0 3.0 %collective-permute-start.7 = (f32[8,2048]{1,0:T(8,128)S(1)}, f32[8,2048]{1,0:T(8,128)S(1)}, u32[]{:S(2)}, u32[]{:S(2)}) collective-permute-start(f32[8,2048]{1,0:T(8,128)S(1)} %add.28), channel_id=1, source_target_pairs={{0,8},{2,10},{4,12},{6,14},{8,0},{10,2},{12,4},{14,6},{1,9},{3,11}... | collective-permute-start | bytes 196616 | tf_op jit(solution)/shard_map/ppermute | solution.py:121
  46.0 2.2 %collective-permute-done.7 = f32[8,2048]{1,0:T(8,128)S(1)} collective-permute-done((f32[8,2048]{1,0:T(8,128)S(1)}, f32[8,2048]{1,0:T(8,128)S(1)}, u32[]{:S(2)}, u32[]{:S(2)}) %collective-permute-start.7) | collective-permute-done | bytes 65568 | tf_op jit(solution)/shard_map/ppermute | solution.py:121
  48.3 0.1 collective-permute-start.8
  48.3 1.2 %collective-permute-done.8 = bf16[8,2048]{1,0:T(8,128)(2,1)S(1)} collective-permute-done((bf16[8,2048]{1,0:T(8,128)(2,1)S(1)}, bf16[8,2048]{1,0:T(8,128)(2,1)S(1)}, u32[]{:S(2)}, u32[]{:S(2)}) %collective-permute-start.8) | collective-permute-done | bytes 32800 | tf_op jit(solution)/shard_map/ppermute | solution.py:121
  49.5 0.0 copy-done
  49.5 0.8 %convolution_multiply_fusion.1 = f32[8,64]{1,0:T(8,128)} fusion(bf16[64,4096]{1,0:T(8,128)(2,1)S(1)} %copy-done, bf16[8,2048]{1,0:T(8,128)(2,1)S(1)} %collective-permute-done.8, bf16[8,2048]{1,0:T(8,128)(2,1)S(1)} %add_convert_fusion, pred[]{:T(512)S(6)} %eq.14), kind=kOutput, calls=%fused_computation.1 | convolution fusion | flops 4489728 | bytes 591873 | tf_op jit(solution)/shard_map/dot_general | solution.py:116
  (10 shorter events, 0.2 us)
Async XLA Ops:
  0.0 49.5 %copy-start = (bf16[64,4096]{1,0:T(8,128)(2,1)S(1)}, bf16[64,4096]{1,0:T(8,128)(2,1)}, u32[]{:S(2)}) copy-start(bf16[64,4096]{1,0:T(8,128)(2,1)} %param.11) | copy-start | bytes 1572868
  0.0 3.1 %copy-start.1 = (bf16[512,7168]{1,0:T(8,128)(2,1)S(1)}, bf16[512,7168]{1,0:T(8,128)(2,1)}, u32[]{:S(2)}) copy-start(bf16[512,7168]{1,0:T(8,128)(2,1)} %gate_ref.1) | copy-start | bytes 22020100
  3.1 1.6 %copy-start.3 = (bf16[512,2048]{1,0:T(8,128)(2,1)S(1)}, bf16[512,2048]{1,0:T(8,128)(2,1)}, u32[]{:S(2)}) copy-start(bf16[512,2048]{1,0:T(8,128)(2,1)} %layer_ref.1) | copy-start | bytes 6291460
  4.7 1.2 %copy-start.4 = (bf16[64,7168]{1,0:T(8,128)(2,1)S(1)}, bf16[64,7168]{1,0:T(8,128)(2,1)}, u32[]{:S(2)}) copy-start(bf16[64,7168]{1,0:T(8,128)(2,1)} %out_ref.1) | copy-start | bytes 2752516
  5.9 0.9 %copy-start.5 = (bf16[64,2048]{1,0:T(8,128)(2,1)S(1)}, bf16[64,2048]{1,0:T(8,128)(2,1)}, u32[]{:S(2)}) copy-start(bf16[64,2048]{1,0:T(8,128)(2,1)} %in_ref.1) | copy-start | bytes 786436
  13.8 1.7 %collective-permute-start = (f32[512,128]{1,0:T(8,128)S(1)}, f32[512,128]{1,0:T(8,128)S(1)}, u32[]{:S(2)}, u32[]{:S(2)}) collective-permute-start(f32[512,128]{1,0:T(8,128)S(1)} %project.1), channel_id=1, source_target_pairs={{0,1},{1,0},{2,3},{3,2},{4,5},{5,4},{6,7},{7,6},{8,9},{9,8},{10,11... | collective-permute-start | bytes 786440 | tf_op jit(solution)/shard_map/ppermute | solution.py:121
  16.3 4.6 %collective-permute-start.1 = (f32[1,8,256]{2,0,1:T(1,128)S(1)}, f32[1,8,256]{2,0,1:T(1,128)S(1)}, u32[]{:S(2)}, u32[]{:S(2)}) collective-permute-start(f32[1,8,256]{2,0,1:T(1,128)S(1)} %dynamic-slice_bitcast_fusion), channel_id=1, source_target_pairs={{0,2},{2,0},{4,6},{6,4},{8,10},{10,8},{12,14},{14,12},{1,3},{3,1},... | collective-permute-start | bytes 24584 | tf_op jit(solution)/shard_map/ppermute | solution.py:121
  20.9 3.9 %collective-permute-start.2 = (f32[2,8,256]{2,0,1:T(2,128)S(1)}, f32[2,8,256]{2,0,1:T(2,128)S(1)}, u32[]{:S(2)}, u32[]{:S(2)}) collective-permute-start(f32[2,8,256]{2,0,1:T(2,128)S(1)} %maximum_select_fusion.3), channel_id=1, source_target_pairs={{0,4},{2,6},{4,0},{6,2},{8,12},{10,14},{12,8},{14,10},{1,5},{3,7},... | collective-permute-start | bytes 49160 | tf_op jit(solution)/shard_map/ppermute | solution.py:121
  24.9 5.0 %collective-permute-start.3 = (f32[4,8,256]{2,0,1:T(4,128)S(1)}, f32[4,8,256]{2,0,1:T(4,128)S(1)}, u32[]{:S(2)}, u32[]{:S(2)}) collective-permute-start(f32[4,8,256]{2,0,1:T(4,128)S(1)} %maximum_select_fusion.2), channel_id=1, source_target_pairs={{0,8},{2,10},{4,12},{6,14},{8,0},{10,2},{12,4},{14,6},{1,9},{3,11}... | collective-permute-start | bytes 98312 | tf_op jit(solution)/shard_map/ppermute | solution.py:121
  29.9 2.2 %copy-start.2 = (f32[256,4096]{1,0:T(8,128)S(1)}, f32[256,4096]{1,0:T(8,128)}, u32[]{:S(2)}) copy-start(f32[256,4096]{1,0:T(8,128)} %matrix_ref.1) | copy-start | bytes 12582916
  33.0 1.3 %collective-permute-start.4 = (f32[8,2048]{1,0:T(8,128)S(1)}, f32[8,2048]{1,0:T(8,128)S(1)}, u32[]{:S(2)}, u32[]{:S(2)}) collective-permute-start(f32[8,2048]{1,0:T(8,128)S(1)} %slice_select_fusion), channel_id=1, source_target_pairs={{0,1},{1,0},{2,3},{3,2},{4,5},{5,4},{6,7},{7,6},{8,9},{9,8},{10,11... | collective-permute-start | bytes 196616 | tf_op jit(solution)/shard_map/ppermute | solution.py:121
  34.3 4.3 %collective-permute-start.5 = (f32[8,2048]{1,0:T(8,128)S(1)}, f32[8,2048]{1,0:T(8,128)S(1)}, u32[]{:S(2)}, u32[]{:S(2)}) collective-permute-start(f32[8,2048]{1,0:T(8,128)S(1)} %select_add_fusion), channel_id=1, source_target_pairs={{0,2},{2,0},{4,6},{6,4},{8,10},{10,8},{12,14},{14,12},{1,3},{3,1},... | collective-permute-start | bytes 196616 | tf_op jit(solution)/shard_map/ppermute | solution.py:121
  38.6 4.3 %collective-permute-start.6 = (f32[8,2048]{1,0:T(8,128)S(1)}, f32[8,2048]{1,0:T(8,128)S(1)}, u32[]{:S(2)}, u32[]{:S(2)}) collective-permute-start(f32[8,2048]{1,0:T(8,128)S(1)} %add.27), channel_id=1, source_target_pairs={{0,4},{2,6},{4,0},{6,2},{8,12},{10,14},{12,8},{14,10},{1,5},{3,7},... | collective-permute-start | bytes 196616 | tf_op jit(solution)/shard_map/ppermute | solution.py:121
  43.0 5.2 %collective-permute-start.7 = (f32[8,2048]{1,0:T(8,128)S(1)}, f32[8,2048]{1,0:T(8,128)S(1)}, u32[]{:S(2)}, u32[]{:S(2)}) collective-permute-start(f32[8,2048]{1,0:T(8,128)S(1)} %add.28), channel_id=1, source_target_pairs={{0,8},{2,10},{4,12},{6,14},{8,0},{10,2},{12,4},{14,6},{1,9},{3,11}... | collective-permute-start | bytes 196616 | tf_op jit(solution)/shard_map/ppermute | solution.py:121
  48.3 1.3 %collective-permute-start.8 = (bf16[8,2048]{1,0:T(8,128)(2,1)S(1)}, bf16[8,2048]{1,0:T(8,128)(2,1)S(1)}, u32[]{:S(2)}, u32[]{:S(2)}) collective-permute-start(bf16[8,2048]{1,0:T(8,128)(2,1)S(1)} %add_convert_fusion), channel_id=1, source_target_pairs={{0,1},{1,0},{2,3},{3,2},{4,5},{5,4},{6,7},{7,6},{8,9},{9,8},{10,11... | collective-permute-start | bytes 98312 | tf_op jit(solution)/shard_map/ppermute | solution.py:121

commit v3 on v2

--- a/solution.py
+++ b/solution.py
@@ -1,3 +1,4 @@
+import functools
 import math
 
 import jax
@@ -9,11 +10,68 @@
 
 CHUNK = 1024
 BAND = 512
+SHARES = (1, 1)
 LAST = (((1,), (1,)), ((), ()))
 
+ROUNDS_OF_8 = (
+    ((1, 0, 4, 5, 2, 3, 7, 6), (3, 2, 6, 7, 0, 1, 5, 4)),
+    ((2, 3, 0, 1, 6, 7, 4, 5), (3, 2, 6, 7, 0, 1, 5, 4)),
+)
+
+
+def gather_rounds(size):
+    if size == 8:
+        return [(pair, True) for pair in ROUNDS_OF_8]
+    rounds = []
+    for bit in steps(size):
+        sources = tuple(i ^ bit for i in range(size))
+        rounds.append(((sources, sources), False))
+    return rounds
+
+
+def gather_slots(size):
+    held = [[[chip] for chip in range(size)] for _ in range(2)]
+    for sources, swaps in gather_rounds(size):
+        got = [[held[c][sources[c][i]] for i in range(size)] for c in range(2)]
+        held = [
+            [
+                held[c][i] + got[c][i] + (got[1 - c][i] if swaps else [])
+                for i in range(size)
+            ]
+            for c in range(2)
+        ]
+    return [[[row.index(s) for s in range(size)] for row in rows] for rows in held]
+
+
+def packed(values, bits):
+    word = sum(value << (bits * i) for i, value in enumerate(values))
+    return word - (1 << 32) if word >= 1 << 31 else word
+
+
+def unpacked(word, index, bits):
+    return (word >> (bits * index)) & ((1 << bits) - 1)
+
+
+def gather_target(sources, core, dp):
+    size = len(sources[0])
+    if size != 8:
+        return dp ^ sources[0][0]
+    words = [packed([row.index(i) for i in range(size)], 3) for row in sources]
+    return unpacked(jnp.where(core == 0, words[0], words[1]), dp, 3)
+
+
+def gather_slot(size):
+    core, dp = lax.axis_index("tensor"), lax.axis_index("dp")
+    if size != 8:
+        return lambda s: dp ^ s
+    place, word = core * size + dp, jnp.int32(0)
+    for k, row in enumerate(sum(gather_slots(size), [])):
+        word = jnp.where(place == k, jnp.int32(packed(row, 4)), word)
+    return lambda s: unpacked(word, s, 4)
+
 
 def project_kernel(layer_ref, gate_ref, in_ref, out_ref, sides_ref, left, right, sems):
-    rank = in_ref.shape[0]
+    rank, tokens = in_ref.shape[0], layer_ref.shape[0]
     counts = (layer_ref.shape[1] // CHUNK, gate_ref.shape[1] // CHUNK)
     copies = []
     for part, (big, small) in enumerate(((layer_ref, in_ref), (gate_ref, out_ref))):
@@ -38,15 +96,21 @@
     blank = jnp.zeros((rank, CHUNK), right.dtype)
     for slot in range(len(copies)):
         right[slot, pl.ds(rank if slot < counts[0] else 0, rank)] = blank
-    total = None
+    half = tokens // 2
+    totals = [None, None]
     for slot, pair in enumerate(copies):
         for copy in pair:
             copy.wait()
-        term = lax.dot_general(
-            left[slot], right[slot], LAST, preferred_element_type=jnp.float32
-        )
-        total = term if total is None else total + term
-    sides_ref[...] = total
+        for h in range(2):
+            term = lax.dot_general(
+                left[slot, h * half : (h + 1) * half],
+                right[slot],
+                LAST,
+                preferred_element_type=jnp.float32,
+            )
+            totals[h] = term if slot == 0 else totals[h] + term
+    for h in range(2):
+        sides_ref[h * half : (h + 1) * half] = totals[h]
 
 
 def project(layer_input, gate_grad, factor_in, factor_out):
@@ -63,7 +127,7 @@
             pltpu.VMEM((slots, 2 * rank, CHUNK), factor_in.dtype),
             pltpu.SemaphoreType.DMA((2, slots)),
         ],
-        compiler_params=pltpu.CompilerParams(vmem_limit_bytes=24 << 20),
+        compiler_params=pltpu.CompilerParams(vmem_limit_bytes=54784 << 10),
         cost_estimate=pl.CostEstimate(
             flops=2 * tokens * features * rank,
             bytes_accessed=2 * (tokens + rank) * features,
@@ -73,6 +137,42 @@
     )(layer_input, gate_grad, factor_in, factor_out)
 
 
+def bring_kernel(first, matrix_ref, *refs):
+    band_ref, here_ref, sems = refs[-3:]
+    copies = [
+        pltpu.make_async_copy(
+            matrix_ref.at[:, pl.ds(first + start, BAND)],
+            band_ref.at[:, pl.ds(start, BAND)],
+            sems.at[number],
+        )
+        for number, start in enumerate(range(0, band_ref.shape[1], BAND))
+    ]
+    for copy in copies:
+        copy.start()
+    here_ref[...] = jnp.zeros_like(here_ref)
+    for copy in copies:
+        copy.wait()
+
+
+def bring(matrix, first, width, *after):
+    rows = matrix.shape[0]
+    return pl.pallas_call(
+        lambda *refs: bring_kernel(first, *refs),
+        out_shape=(
+            jax.ShapeDtypeStruct((rows, width), matrix.dtype),
+            jax.ShapeDtypeStruct((8, 128), jnp.float32),
+        ),
+        in_specs=[pl.BlockSpec(memory_space=pl.ANY)] * (1 + len(after)),
+        out_specs=[pl.BlockSpec(memory_space=pltpu.VMEM)] * 2,
+        scratch_shapes=[pltpu.SemaphoreType.DMA((width // BAND,))],
+        compiler_params=pltpu.CompilerParams(vmem_limit_bytes=49 << 20),
+        cost_estimate=pl.CostEstimate(
+            flops=0, bytes_accessed=4 * rows * width, transcendentals=0
+        ),
+        name="bring",
+    )(matrix, *after)
+
+
 def split(value, terms):
     parts = []
     for _ in range(terms):
@@ -82,34 +182,53 @@
     return parts
 
 
-def precondition_kernel(grads_ref, matrix_ref, result_ref):
-    seqs = grads_ref.shape[0]
-    grads = jnp.concatenate(split(grads_ref[...], 3), axis=0)
-    width = matrix_ref.shape[1]
-    for start in range(0, width, BAND):
-        high, low = split(matrix_ref[:, start : start + BAND], 2)
-        by_high = jnp.dot(grads, high, preferred_element_type=jnp.float32)
-        by_low = jnp.dot(grads[: 2 * seqs], low, preferred_element_type=jnp.float32)
-        small = by_high[2 * seqs :] + by_low[seqs:]
-        middle = by_high[seqs : 2 * seqs] + by_low[:seqs]
-        result_ref[:, start : start + BAND] = by_high[:seqs] + (middle + small)
-
-
-def precondition_rows(grads, matrix):
-    seqs, (rows, width) = grads.shape[0], matrix.shape
+def precondition_kernel(parts, token_ref, *refs):
+    del token_ref
+    *refs, result_ref, held = refs
+    part_refs, bands = refs[:parts], refs[parts:]
+    seqs, rows = result_ref.shape[0], held.shape[1]
+    core, first = lax.axis_index("tensor"), 0
+    for part_ref in part_refs:
+        own = jnp.where(core == 0, part_ref[:, :rows], part_ref[:, rows:])
+        held[first : first + part_ref.shape[0]] = own
+        first += part_ref.shape[0]
+    slot = gather_slot(seqs)
+    grads = jnp.concatenate(
+        [held[pl.ds(slot(s), 1), :] for s in range(seqs)], axis=0
+    )
+    grads = jnp.concatenate(split(grads, 3), axis=0)
+    first = 0
+    for band_ref in bands:
+        for start in range(0, band_ref.shape[1], BAND):
+            high, low = split(band_ref[:, start : start + BAND], 2)
+            by_high = jnp.dot(grads, high, preferred_element_type=jnp.float32)
+            by_low = jnp.dot(grads[: 2 * seqs], low, preferred_element_type=jnp.float32)
+            small = by_high[2 * seqs :] + by_low[seqs:]
+            middle = by_high[seqs : 2 * seqs] + by_low[:seqs]
+            result_ref[:, first + start : first + start + BAND] = by_high[:seqs] + (
+                middle + small
+            )
+        first += band_ref.shape[1]
+
+
+def precondition_rows(parts, token, bands, seqs):
+    rows, width = bands[0].shape[0], sum(band.shape[1] for band in bands)
+    held = sum(part.shape[0] for part in parts)
     return pl.pallas_call(
-        precondition_kernel,
+        functools.partial(precondition_kernel, len(parts)),
         out_shape=jax.ShapeDtypeStruct((seqs, width), jnp.float32),
-        in_specs=[pl.BlockSpec(memory_space=pltpu.VMEM)] * 2,
+        in_specs=[pl.BlockSpec(memory_space=pl.ANY)]
+        + [pl.BlockSpec(memory_space=pltpu.VMEM)] * (len(parts) + len(bands)),
         out_specs=pl.BlockSpec(memory_space=pltpu.VMEM),
-        compiler_params=pltpu.CompilerParams(vmem_limit_bytes=24 << 20),
+        scratch_shapes=[pltpu.VMEM((held, rows), jnp.float32)],
+        compiler_params=pltpu.CompilerParams(vmem_limit_bytes=16 << 20),
         cost_estimate=pl.CostEstimate(
             flops=2 * seqs * rows * width,
             bytes_accessed=4 * rows * width,
             transcendentals=0,
         ),
         name="precondition",
-    )(grads, matrix)
+    )(token, *parts, *bands)
 
 
 def contract_last(left, right):
@@ -119,6 +238,15 @@
 def swap(value, axis, bit):
     size = lax.axis_size(axis)
     return lax.ppermute(value, axis, [(i, i ^ bit) for i in range(size)])
+
+
+def receive(value, sources):
+    pairs = [
+        (2 * source + core, 2 * chip + core)
+        for core in range(2)
+        for chip, source in enumerate(sources[core])
+    ]
+    return lax.ppermute(value, ("dp", "tensor"), pairs)
 
 
 def steps(size):
@@ -138,6 +266,18 @@
     own_rows, width = precondition.shape
     dp, dp_size = lax.axis_index("dp"), lax.axis_size("dp")
     core = lax.axis_index("tensor")
+
+    bands, tokens = [], []
+
+    def beside(given, got):
+        if len(bands) < len(SHARES):
+            first = sum(band.shape[1] for band in bands)
+            share = width * SHARES[len(bands)] // sum(SHARES)
+            band, token = bring(precondition, first, share, given, *tokens[-1:])
+            got, token = lax.optimization_barrier((got, token))
+            bands.append(band)
+            tokens.append(token)
+        return got
 
     sides = project(layer_input, gate_grad, factor_in, factor_out)
     sides = sides + swap(sides, "tensor", 1)
@@ -148,14 +288,21 @@
         precision=lax.Precision.HIGHEST,
     ) * (1 / math.sqrt(seq_length))
 
-    blocks = gradient.reshape(dp_size, 2, own_rows)
-    blocks = lax.dynamic_index_in_dim(blocks, core, 1, keepdims=False)[None]
-    for bit in steps(dp_size):
-        other = swap(blocks, "dp", bit)
-        blocks = ordered((dp & bit) == 0, blocks, other, 0)
-    col_block = lax.dynamic_index_in_dim(blocks, dp, 1, keepdims=False)
-
-    partial = precondition_rows(col_block, precondition)
+    held = gradient.reshape(1, dp_size, 2 * own_rows)
+    rounds = gather_rounds(dp_size)
+    for number, (sources, swaps) in enumerate(rounds):
+        given = held
+        if number == len(rounds) - 1:
+            target = gather_target(sources, core, dp)
+            given = lax.dynamic_index_in_dim(held, target, 1, keepdims=False)
+            held = lax.dynamic_index_in_dim(held, dp, 1, keepdims=False)
+        got = beside(given, receive(given, sources))
+        parts = [held, got] + ([swap(got, "tensor", 1)] if swaps else [])
+        if number < len(rounds) - 1:
+            held = jnp.concatenate(parts, axis=0)
+    *parts, token = lax.optimization_barrier((*parts, tokens[-1]))
+
+    partial = precondition_rows(parts, token, bands, dp_size)
 
     low, high = partial[:, : width // 2], partial[:, width // 2 :]
     given = jnp.where(core == 0, high, low)

time: 50.6 us -> 37.4 us (0.74)
  local copies, waits for them, and re-layouts: 9.14 us -> 0.1 us
  starting transfers between devices: 15.7 us -> 12.8 us
  waiting for transfers between devices: 15.9 us -> 13.8 us
  Pallas kernels: 7.82 us -> 8.83 us
    unnamed x12 -> x6, local copies, waits for them, and re-layouts: 9.05 us -> 0.01 us
    ppermute x9 -> x8, starting transfers between devices: 15.7 us -> 8.1 us  [swap(): return lax.ppermute(value, axis, [(i, i ^ bit) for i in range(size)])]
    ppermute x0 -> x2, starting transfers between devices: none -> 4.66 us  [receive(): return lax.ppermute(value, ('dp', 'tensor'), pairs)]
    pallas_call x1 -> x3, Pallas kernels: 0.85 us -> 3.99 us  [the longest x2 3.11 us: bring(): pl.pallas_call(lambda *refs: bring_kernel(first, *refs), out_shape=(jax.S...]
    ppermute x9 -> x8, waiting for transfers between devices: 15.9 us -> 13.3 us  [swap(): return lax.ppermute(value, axis, [(i, i ^ bit) for i in range(size)])]
    pallas_call x1, Pallas kernels: 6.97 us -> 4.85 us  [project(): pl.pallas_call(project_kernel, out_shape=jax.ShapeDtypeStruct((tokens, 2...]
  transfers between devices with their start and end apart: 9 -> 10, of which waited for: 9 -> 10; matrix products, arithmetic and copies ran while one was open for 0% -> 0% of each run, Pallas kernels for 0% -> 8%
where the time goes in v3:
time: 37.4 us; the launch traced here: 37.2 us
  waiting for transfers between devices  13.8 us (37%)
  starting transfers between devices  12.8 us (34%)
  Pallas kernels  8.83 us (24%)
  matrix products  1.52 us (4%)
    ppermute x8, waiting for transfers between devices, swap(): return lax.ppermute(value, axis, [(i, i ^ bit) for i in range(size)])  13.3 us
    ppermute x8, starting transfers between devices, swap(): return lax.ppermute(value, axis, [(i, i ^ bit) for i in range(size)])  8.1 us
    pallas_call x1, Pallas kernels, project(): pl.pallas_call(project_kernel, out_shape=jax.ShapeDtypeStruct((tokens, 2...  4.85 us
    ppermute x2, starting transfers between devices, receive(): return lax.ppermute(value, ('dp', 'tensor'), pairs)  4.66 us
    pallas_call x2, Pallas kernels, bring(): pl.pallas_call(lambda *refs: bring_kernel(first, *refs), out_shape=(jax.S...  3.11 us
    pallas_call x1, Pallas kernels, precondition_rows(): pl.pallas_call(functools.partial(precondition_kernel, len(parts)), out_sh...  0.88 us
    dot_general x1, matrix products, contract_last(): lax.dot_general(left, right, LAST, preferred_element_type=jnp.float32)  0.85 us
  transfers between devices with their start and end apart: 10, of which 10 were waited for; matrix products, arithmetic and copies ran while one was open for 0% of the time, Pallas kernels for 8%

profile of v3, /device:TPU:0, one launch (start us, length us, event | category | flops | bytes accessed | tf_op | source)
XLA Modules:
  0.0 37.2 jit_solution(7834330904086672644)
XLA Ops:
  0.0 0.0 copy-start
  0.0 4.8 %project.1 = f32[512,128]{1,0:T(8,128)S(1)} custom-call(bf16[512,2048]{1,0:T(8,128)(2,1)} %layer_ref.1, bf16[512,7168]{1,0:T(8,128)(2,1)} %gate_ref.1, bf16[64,2048]{1,0:T(8,128)(2,1)} %in_ref.1, bf16[64,7168]{1,0:T(8,128)(2,1)} %out_ref.1), custom_call_target="tpu_custom_call" | custom-call | flops 603979776 | bytes 10616832 | tf_op jit(solution)/shard_map/project/pallas_call | solution.py:120
  4.9 0.5 %collective-permute-start = (f32[512,128]{1,0:T(8,128)S(1)}, f32[512,128]{1,0:T(8,128)S(1)}, u32[]{:S(2)}, u32[]{:S(2)}) collective-permute-start(f32[512,128]{1,0:T(8,128)S(1)} %project.1), channel_id=1, source_target_pairs={{0,1},{1,0},{2,3},{3,2},{4,5},{5,4},{6,7},{7,6},{8,9},{9,8},{10,11... | collective-permute-start | bytes 786440 | tf_op jit(solution)/shard_map/ppermute | solution.py:240
  5.4 1.2 %collective-permute-done = f32[512,128]{1,0:T(8,128)S(1)} collective-permute-done((f32[512,128]{1,0:T(8,128)S(1)}, f32[512,128]{1,0:T(8,128)S(1)}, u32[]{:S(2)}, u32[]{:S(2)}) %collective-permute-start) | collective-permute-done | bytes 262176 | tf_op jit(solution)/shard_map/ppermute | solution.py:240
  6.6 0.7 %convolution_multiply_fusion = f32[64,64]{1,0:T(8,128)S(1)} fusion(f32[512,128]{1,0:T(8,128)S(1)} %add.22), kind=kOutput, calls=%fused_computation | convolution fusion | flops 25169920 | bytes 540672 | tf_op jit(solution)/shard_map/dot_general | solution.py:284
  7.2 0.1 reshape.3.refs_1_
  7.3 2.9 %collective-permute-start.1 = (f32[1,8,512]{2,1,0:T(8,128)S(1)}, f32[1,8,512]{2,1,0:T(8,128)S(1)}, u32[]{:S(2)}, u32[]{:S(2)}) collective-permute-start(f32[1,8,512]{2,1,0:T(8,128)S(1)} %reshape.3.refs_1_), channel_id=1, source_target_pairs={{2,0},{0,2},{8,4},{10,6},{4,8},{6,10},{14,12},{12,14},{7,1},{5,3},... | collective-permute-start | bytes 49160 | tf_op jit(solution)/shard_map/ppermute | solution.py:249
  10.2 1.6 %bring.2 = (f32[256,2048]{1,0:T(8,128)S(1)}, f32[8,128]{1,0:T(8,128)S(1)}) custom-call(f32[256,4096]{1,0:T(8,128)} %refs_0_.3, f32[1,8,512]{2,1,0:T(8,128)S(1)} %reshape.3.refs_1_), custom_call_target="tpu_custom_call" | custom-call | bytes 2097152 | tf_op jit(solution)/shard_map/bring/pallas_call | solution.py:159
  11.7 0.1 collective-permute-done.1
  11.9 0.9 %collective-permute-start.2 = (f32[1,8,512]{2,1,0:T(8,128)S(1)}, f32[1,8,512]{2,1,0:T(8,128)S(1)}, u32[]{:S(2)}, u32[]{:S(2)}) collective-permute-start(f32[1,8,512]{2,1,0:T(8,128)S(1)} %collective-permute-done.1), channel_id=1, source_target_pairs={{0,1},{1,0},{2,3},{3,2},{4,5},{5,4},{6,7},{7,6},{8,9},{9,8},{10,11... | collective-permute-start | bytes 49160 | tf_op jit(solution)/shard_map/ppermute | solution.py:240
  12.8 0.8 %collective-permute-done.2 = f32[1,8,512]{2,1,0:T(8,128)S(1)} collective-permute-done((f32[1,8,512]{2,1,0:T(8,128)S(1)}, f32[1,8,512]{2,1,0:T(8,128)S(1)}, u32[]{:S(2)}, u32[]{:S(2)}) %collective-permute-start.2) | collective-permute-done | bytes 16416 | tf_op jit(solution)/shard_map/ppermute | solution.py:240
  13.7 1.8 %collective-permute-start.3 = (f32[3,512]{1,0:T(4,128)S(1)}, f32[3,512]{1,0:T(4,128)S(1)}, u32[]{:S(2)}, u32[]{:S(2)}) collective-permute-start(f32[3,512]{1,0:T(4,128)S(1)} %bitcast.8), channel_id=1, source_target_pairs={{4,0},{6,2},{0,4},{2,6},{12,8},{14,10},{8,12},{10,14},{7,1},{5,3},... | collective-permute-start | bytes 18440 | tf_op jit(solution)/shard_map/ppermute | solution.py:249
  15.4 1.6 %bring.3 = (f32[256,2048]{1,0:T(8,128)S(1)}, f32[8,128]{1,0:T(8,128)S(1)}) custom-call(f32[256,4096]{1,0:T(8,128)} %refs_0_.3, f32[3,512]{1,0:T(4,128)S(1)} %bitcast.9, f32[8,128]{1,0:T(8,128)S(1)} %get-tuple-element.19.refs_2_), custom_call_target="tpu_custom_call" | custom-call | bytes 2097152 | tf_op jit(solution)/shard_map/bring/pallas_call | solution.py:159
  17.0 0.3 collective-permute-done.3.refs_1_
  17.4 0.6 %collective-permute-start.4 = (f32[3,512]{1,0:T(4,128)S(1)}, f32[3,512]{1,0:T(4,128)S(1)}, u32[]{:S(2)}, u32[]{:S(2)}) collective-permute-start(f32[3,512]{1,0:T(4,128)S(1)} %collective-permute-done.3.refs_1_), channel_id=1, source_target_pairs={{0,1},{1,0},{2,3},{3,2},{4,5},{5,4},{6,7},{7,6},{8,9},{9,8},{10,11... | collective-permute-start | bytes 18440 | tf_op jit(solution)/shard_map/ppermute | solution.py:240
  18.0 0.8 %collective-permute-done.4.refs_2_ = f32[3,512]{1,0:T(4,128)S(1)} collective-permute-done((f32[3,512]{1,0:T(4,128)S(1)}, f32[3,512]{1,0:T(4,128)S(1)}, u32[]{:S(2)}, u32[]{:S(2)}) %collective-permute-start.4) | collective-permute-done | bytes 6176 | tf_op jit(solution)/shard_map/ppermute | solution.py:240
  18.8 0.9 %precondition.1 = f32[8,4096]{1,0:T(8,128)S(1)} custom-call(f32[8,128]{1,0:T(8,128)S(1)} %get-tuple-element.23.token_ref, f32[3,512]{1,0:T(4,128)S(1)} %bitcast.7, f32[3,512]{1,0:T(4,128)S(1)} %collective-permute-done.3.refs_1_, f32[3,512]{1,0:T(4,128)S(1)} %collective-permute-done.4.refs_2_, f32[256,2048]{1,0:T(8,128)S(1)} %get-tuple-element.27.refs_3_, ...), custom_call_target="tpu_custom_call" | custom-call | flops 16777216 | bytes 4194304 | tf_op jit(solution)/shard_map/precondition/pallas_call | solution.py:217
  19.8 0.4 %collective-permute-start.5 = (f32[8,2048]{1,0:T(8,128)S(1)}, f32[8,2048]{1,0:T(8,128)S(1)}, u32[]{:S(2)}, u32[]{:S(2)}) collective-permute-start(f32[8,2048]{1,0:T(8,128)S(1)} %slice_select_fusion), channel_id=1, source_target_pairs={{0,1},{1,0},{2,3},{3,2},{4,5},{5,4},{6,7},{7,6},{8,9},{9,8},{10,11... | collective-permute-start | bytes 196616 | tf_op jit(solution)/shard_map/ppermute | solution.py:240
  20.2 0.9 %collective-permute-done.5 = f32[8,2048]{1,0:T(8,128)S(1)} collective-permute-done((f32[8,2048]{1,0:T(8,128)S(1)}, f32[8,2048]{1,0:T(8,128)S(1)}, u32[]{:S(2)}, u32[]{:S(2)}) %collective-permute-start.5) | collective-permute-done | bytes 65568 | tf_op jit(solution)/shard_map/ppermute | solution.py:240
  21.1 1.6 %collective-permute-start.6 = (f32[8,2048]{1,0:T(8,128)S(1)}, f32[8,2048]{1,0:T(8,128)S(1)}, u32[]{:S(2)}, u32[]{:S(2)}) collective-permute-start(f32[8,2048]{1,0:T(8,128)S(1)} %select_add_fusion), channel_id=1, source_target_pairs={{0,2},{2,0},{4,6},{6,4},{8,10},{10,8},{12,14},{14,12},{1,3},{3,1},... | collective-permute-start | bytes 196616 | tf_op jit(solution)/shard_map/ppermute | solution.py:240
  22.7 2.8 %collective-permute-done.6 = f32[8,2048]{1,0:T(8,128)S(1)} collective-permute-done((f32[8,2048]{1,0:T(8,128)S(1)}, f32[8,2048]{1,0:T(8,128)S(1)}, u32[]{:S(2)}, u32[]{:S(2)}) %collective-permute-start.6) | collective-permute-done | bytes 65568 | tf_op jit(solution)/shard_map/ppermute | solution.py:240
  25.5 1.4 %collective-permute-start.7 = (f32[8,2048]{1,0:T(8,128)S(1)}, f32[8,2048]{1,0:T(8,128)S(1)}, u32[]{:S(2)}, u32[]{:S(2)}) collective-permute-start(f32[8,2048]{1,0:T(8,128)S(1)} %add.26), channel_id=1, source_target_pairs={{0,4},{2,6},{4,0},{6,2},{8,12},{10,14},{12,8},{14,10},{1,5},{3,7},... | collective-permute-start | bytes 196616 | tf_op jit(solution)/shard_map/ppermute | solution.py:240
  27.0 2.9 %collective-permute-done.7 = f32[8,2048]{1,0:T(8,128)S(1)} collective-permute-done((f32[8,2048]{1,0:T(8,128)S(1)}, f32[8,2048]{1,0:T(8,128)S(1)}, u32[]{:S(2)}, u32[]{:S(2)}) %collective-permute-start.7) | collective-permute-done | bytes 65568 | tf_op jit(solution)/shard_map/ppermute | solution.py:240
  29.9 2.6 %collective-permute-start.8 = (f32[8,2048]{1,0:T(8,128)S(1)}, f32[8,2048]{1,0:T(8,128)S(1)}, u32[]{:S(2)}, u32[]{:S(2)}) collective-permute-start(f32[8,2048]{1,0:T(8,128)S(1)} %add.27), channel_id=1, source_target_pairs={{0,8},{2,10},{4,12},{6,14},{8,0},{10,2},{12,4},{14,6},{1,9},{3,11}... | collective-permute-start | bytes 196616 | tf_op jit(solution)/shard_map/ppermute | solution.py:240
  32.4 2.7 %collective-permute-done.8 = f32[8,2048]{1,0:T(8,128)S(1)} collective-permute-done((f32[8,2048]{1,0:T(8,128)S(1)}, f32[8,2048]{1,0:T(8,128)S(1)}, u32[]{:S(2)}, u32[]{:S(2)}) %collective-permute-start.8) | collective-permute-done | bytes 65568 | tf_op jit(solution)/shard_map/ppermute | solution.py:240
  35.1 0.1 collective-permute-start.9
  35.2 1.2 %collective-permute-done.9 = bf16[8,2048]{1,0:T(8,128)(2,1)S(1)} collective-permute-done((bf16[8,2048]{1,0:T(8,128)(2,1)S(1)}, bf16[8,2048]{1,0:T(8,128)(2,1)S(1)}, u32[]{:S(2)}, u32[]{:S(2)}) %collective-permute-start.9) | collective-permute-done | bytes 32800 | tf_op jit(solution)/shard_map/ppermute | solution.py:240
  36.4 0.0 copy-done
  36.4 0.8 %convolution_multiply_fusion.1 = f32[8,64]{1,0:T(8,128)} fusion(bf16[64,4096]{1,0:T(8,128)(2,1)S(1)} %copy-done, bf16[8,2048]{1,0:T(8,128)(2,1)S(1)} %collective-permute-done.9, bf16[8,2048]{1,0:T(8,128)(2,1)S(1)} %add_convert_fusion, pred[]{:T(512)S(6)} %eq.2), kind=kOutput, calls=%fused_computation.1 | convolution fusion | flops 4489728 | bytes 591873 | tf_op jit(solution)/shard_map/dot_general | solution.py:235
  (12 shorter events, 0.1 us)
Async XLA Ops:
  0.0 36.4 %copy-start = (bf16[64,4096]{1,0:T(8,128)(2,1)S(1)}, bf16[64,4096]{1,0:T(8,128)(2,1)}, u32[]{:S(2)}) copy-start(bf16[64,4096]{1,0:T(8,128)(2,1)} %param.11) | copy-start | bytes 1572868
  4.9 1.7 %collective-permute-start = (f32[512,128]{1,0:T(8,128)S(1)}, f32[512,128]{1,0:T(8,128)S(1)}, u32[]{:S(2)}, u32[]{:S(2)}) collective-permute-start(f32[512,128]{1,0:T(8,128)S(1)} %project.1), channel_id=1, source_target_pairs={{0,1},{1,0},{2,3},{3,2},{4,5},{5,4},{6,7},{7,6},{8,9},{9,8},{10,11... | collective-permute-start | bytes 786440 | tf_op jit(solution)/shard_map/ppermute | solution.py:240
  7.3 4.6 %collective-permute-start.1 = (f32[1,8,512]{2,1,0:T(8,128)S(1)}, f32[1,8,512]{2,1,0:T(8,128)S(1)}, u32[]{:S(2)}, u32[]{:S(2)}) collective-permute-start(f32[1,8,512]{2,1,0:T(8,128)S(1)} %reshape.3.refs_1_), channel_id=1, source_target_pairs={{2,0},{0,2},{8,4},{10,6},{4,8},{6,10},{14,12},{12,14},{7,1},{5,3},... | collective-permute-start | bytes 49160 | tf_op jit(solution)/shard_map/ppermute | solution.py:249
  11.9 1.7 %collective-permute-start.2 = (f32[1,8,512]{2,1,0:T(8,128)S(1)}, f32[1,8,512]{2,1,0:T(8,128)S(1)}, u32[]{:S(2)}, u32[]{:S(2)}) collective-permute-start(f32[1,8,512]{2,1,0:T(8,128)S(1)} %collective-permute-done.1), channel_id=1, source_target_pairs={{0,1},{1,0},{2,3},{3,2},{4,5},{5,4},{6,7},{7,6},{8,9},{9,8},{10,11... | collective-permute-start | bytes 49160 | tf_op jit(solution)/shard_map/ppermute | solution.py:240
  13.7 3.7 %collective-permute-start.3 = (f32[3,512]{1,0:T(4,128)S(1)}, f32[3,512]{1,0:T(4,128)S(1)}, u32[]{:S(2)}, u32[]{:S(2)}) collective-permute-start(f32[3,512]{1,0:T(4,128)S(1)} %bitcast.8), channel_id=1, source_target_pairs={{4,0},{6,2},{0,4},{2,6},{12,8},{14,10},{8,12},{10,14},{7,1},{5,3},... | collective-permute-start | bytes 18440 | tf_op jit(solution)/shard_map/ppermute | solution.py:249
  17.4 1.5 %collective-permute-start.4 = (f32[3,512]{1,0:T(4,128)S(1)}, f32[3,512]{1,0:T(4,128)S(1)}, u32[]{:S(2)}, u32[]{:S(2)}) collective-permute-start(f32[3,512]{1,0:T(4,128)S(1)} %collective-permute-done.3.refs_1_), channel_id=1, source_target_pairs={{0,1},{1,0},{2,3},{3,2},{4,5},{5,4},{6,7},{7,6},{8,9},{9,8},{10,11... | collective-permute-start | bytes 18440 | tf_op jit(solution)/shard_map/ppermute | solution.py:240
  19.8 1.3 %collective-permute-start.5 = (f32[8,2048]{1,0:T(8,128)S(1)}, f32[8,2048]{1,0:T(8,128)S(1)}, u32[]{:S(2)}, u32[]{:S(2)}) collective-permute-start(f32[8,2048]{1,0:T(8,128)S(1)} %slice_select_fusion), channel_id=1, source_target_pairs={{0,1},{1,0},{2,3},{3,2},{4,5},{5,4},{6,7},{7,6},{8,9},{9,8},{10,11... | collective-permute-start | bytes 196616 | tf_op jit(solution)/shard_map/ppermute | solution.py:240
  21.1 4.4 %collective-permute-start.6 = (f32[8,2048]{1,0:T(8,128)S(1)}, f32[8,2048]{1,0:T(8,128)S(1)}, u32[]{:S(2)}, u32[]{:S(2)}) collective-permute-start(f32[8,2048]{1,0:T(8,128)S(1)} %select_add_fusion), channel_id=1, source_target_pairs={{0,2},{2,0},{4,6},{6,4},{8,10},{10,8},{12,14},{14,12},{1,3},{3,1},... | collective-permute-start | bytes 196616 | tf_op jit(solution)/shard_map/ppermute | solution.py:240
  25.5 4.3 %collective-permute-start.7 = (f32[8,2048]{1,0:T(8,128)S(1)}, f32[8,2048]{1,0:T(8,128)S(1)}, u32[]{:S(2)}, u32[]{:S(2)}) collective-permute-start(f32[8,2048]{1,0:T(8,128)S(1)} %add.26), channel_id=1, source_target_pairs={{0,4},{2,6},{4,0},{6,2},{8,12},{10,14},{12,8},{14,10},{1,5},{3,7},... | collective-permute-start | bytes 196616 | tf_op jit(solution)/shard_map/ppermute | solution.py:240
  29.9 5.2 %collective-permute-start.8 = (f32[8,2048]{1,0:T(8,128)S(1)}, f32[8,2048]{1,0:T(8,128)S(1)}, u32[]{:S(2)}, u32[]{:S(2)}) collective-permute-start(f32[8,2048]{1,0:T(8,128)S(1)} %add.27), channel_id=1, source_target_pairs={{0,8},{2,10},{4,12},{6,14},{8,0},{10,2},{12,4},{14,6},{1,9},{3,11}... | collective-permute-start | bytes 196616 | tf_op jit(solution)/shard_map/ppermute | solution.py:240
  35.1 1.3 %collective-permute-start.9 = (bf16[8,2048]{1,0:T(8,128)(2,1)S(1)}, bf16[8,2048]{1,0:T(8,128)(2,1)S(1)}, u32[]{:S(2)}, u32[]{:S(2)}) collective-permute-start(bf16[8,2048]{1,0:T(8,128)(2,1)S(1)} %add_convert_fusion), channel_id=1, source_target_pairs={{0,1},{1,0},{2,3},{3,2},{4,5},{5,4},{6,7},{7,6},{8,9},{9,8},{10,11... | collective-permute-start | bytes 98312 | tf_op jit(solution)/shard_map/ppermute | solution.py:240

commit v4 on v3

--- a/solution.py
+++ b/solution.py
@@ -10,12 +10,13 @@
 
 CHUNK = 1024
 BAND = 512
-SHARES = (1, 1)
+BESIDE = 128
+SHARES = (1, 1, 2)
 LAST = (((1,), (1,)), ((), ()))
 
 ROUNDS_OF_8 = (
-    ((1, 0, 4, 5, 2, 3, 7, 6), (3, 2, 6, 7, 0, 1, 5, 4)),
-    ((2, 3, 0, 1, 6, 7, 4, 5), (3, 2, 6, 7, 0, 1, 5, 4)),
+    ((2, 3, 0, 1, 6, 7, 4, 5), (4, 5, 1, 0, 7, 6, 2, 3)),
+    ((1, 0, 4, 5, 2, 3, 7, 6), (4, 5, 1, 0, 7, 6, 2, 3)),
 )
 
 
@@ -137,6 +138,44 @@
     )(layer_input, gate_grad, factor_in, factor_out)
 
 
+def gradient_kernel(mine_ref, other_ref, result_ref, square):
+    tokens, rank = mine_ref.shape[0], square.shape[0]
+    terms = jnp.concatenate(split(mine_ref[...] + other_ref[...], 3), axis=1)
+    product = lax.dot_general(
+        terms, terms, (((0,), (0,)), ((), ())), preferred_element_type=jnp.float32
+    )
+
+    def block(i, j):
+        rows = product[2 * rank * i : 2 * rank * i + rank]
+        return rows[:, 2 * rank * j : 2 * rank * (j + 1)]
+
+    small = block(0, 2) + block(2, 0) + block(1, 1)
+    full = block(0, 0) + (block(0, 1) + block(1, 0) + small)
+    square[...] = full[:, rank:] * (1 / math.sqrt(tokens))
+    rows = result_ref.shape[0]
+    each = rank // rows
+    for k in range(each):
+        result_ref[:, k * rank : (k + 1) * rank] = square[pl.ds(k, rows, each), :]
+
+
+def gradient_rows(mine, other, rows):
+    tokens, rank = mine.shape[0], mine.shape[1] // 2
+    return pl.pallas_call(
+        gradient_kernel,
+        out_shape=jax.ShapeDtypeStruct((rows, rank * rank // rows), jnp.float32),
+        in_specs=[pl.BlockSpec(memory_space=pltpu.VMEM)] * 2,
+        out_specs=pl.BlockSpec(memory_space=pltpu.VMEM),
+        scratch_shapes=[pltpu.VMEM((rank, rank), jnp.float32)],
+        compiler_params=pltpu.CompilerParams(vmem_limit_bytes=16 << 20),
+        cost_estimate=pl.CostEstimate(
+            flops=2 * tokens * rank * rank,
+            bytes_accessed=16 * tokens * rank,
+            transcendentals=0,
+        ),
+        name="gradient",
+    )(mine, other)
+
+
 def bring_kernel(first, matrix_ref, *refs):
     band_ref, here_ref, sems = refs[-3:]
     copies = [
@@ -209,6 +248,9 @@
                 middle + small
             )
         first += band_ref.shape[1]
+    top = jnp.max(jnp.abs(result_ref[:, :first]), axis=1, keepdims=True)
+    power = jnp.floor(jnp.log2(jnp.clip(top, 1e-30, 1e30))) - 14
+    result_ref[:, first:] = jnp.broadcast_to(power, (seqs, BESIDE))
 
 
 def precondition_rows(parts, token, bands, seqs):
@@ -216,7 +258,7 @@
     held = sum(part.shape[0] for part in parts)
     return pl.pallas_call(
         functools.partial(precondition_kernel, len(parts)),
-        out_shape=jax.ShapeDtypeStruct((seqs, width), jnp.float32),
+        out_shape=jax.ShapeDtypeStruct((seqs, width + BESIDE), jnp.float32),
         in_specs=[pl.BlockSpec(memory_space=pl.ANY)]
         + [pl.BlockSpec(memory_space=pltpu.VMEM)] * (len(parts) + len(bands)),
         out_specs=pl.BlockSpec(memory_space=pltpu.VMEM),
@@ -249,6 +291,21 @@
     return lax.ppermute(value, ("dp", "tensor"), pairs)
 
 
+def flip(value, steps):
+    size = lax.axis_size("dp")
+    pairs = []
+    for place in range(2 * size):
+        family = (place ^ odd(place >> 1)) & 1
+        pairs.append((place, place ^ (2 * steps[family] + 1)))
+    return lax.ppermute(value, ("dp", "tensor"), pairs)
+
+
+def odd(number):
+    for shift in (8, 4, 2, 1):
+        number = number ^ (number >> shift)
+    return number & 1
+
+
 def steps(size):
     return [1 << i for i in range(size.bit_length() - 1)]
 
@@ -261,8 +318,104 @@
     )
 
 
+def add_cores_kernel(mine_ref, other_ref, sum_ref, code_ref):
+    width = sum_ref.shape[1] - BESIDE
+    power = jnp.maximum(mine_ref[:, width:], other_ref[:, width:]) + 1
+    scale = jnp.exp2(-power)
+    for start in range(0, width, BESIDE):
+        lanes = slice(start, start + BESIDE)
+        total = mine_ref[:, lanes] + other_ref[:, lanes]
+        sum_ref[:, lanes] = total
+        code_ref[:, lanes] = total * scale
+    sum_ref[:, width:] = power
+    code_ref[:, width:] = power
+
+
+def add_first_kernel(mine_ref, got_ref, swapped_ref, sum_ref, code_ref):
+    width = sum_ref.shape[1]
+    powers = [ref[:, width:] for ref in (mine_ref, got_ref, swapped_ref)]
+    power = jnp.maximum(jnp.maximum(powers[0], powers[1]), powers[2]) + 2
+    got_scale, swapped_scale = jnp.exp2(powers[1]), jnp.exp2(powers[2])
+    scale = jnp.exp2(-power)
+    own = jnp.where(lax.axis_index("tensor") == 0, 1.0, 0.0)
+    for start in range(0, width, BESIDE):
+        lanes = slice(start, start + BESIDE)
+        first = got_ref[:, lanes] * got_scale + swapped_ref[:, lanes] * swapped_scale
+        mine = mine_ref[:, lanes]
+        sum_ref[:, lanes] = mine + first
+        code_ref[:, lanes] = (first + mine * own) * scale
+    code_ref[:, width:] = power
+
+
+def score_kernel(sum_ref, got_ref, swapped_ref, query_ref, result_ref, rounded):
+    width = sum_ref.shape[1]
+    got_scale = jnp.exp2(got_ref[:, width:])
+    swapped_scale = jnp.exp2(swapped_ref[:, width:])
+    for start in range(0, width, BESIDE):
+        lanes = slice(start, start + BESIDE)
+        second = got_ref[:, lanes] * got_scale + swapped_ref[:, lanes] * swapped_scale
+        rounded[:, lanes] = (sum_ref[:, lanes] + second).astype(rounded.dtype)
+    step = width // 4
+    total = sum(
+        contract_last(
+            rounded[:, start : start + step], query_ref[:, start : start + step]
+        )
+        for start in range(0, width, step)
+    )
+    result_ref[...] = total * (1 / math.sqrt(width))
+
+
+def small_kernel(kernel, name, operands, shapes, scratch=()):
+    return pl.pallas_call(
+        kernel,
+        out_shape=[jax.ShapeDtypeStruct(shape, jnp.float32) for shape in shapes],
+        in_specs=[pl.BlockSpec(memory_space=pltpu.VMEM)] * len(operands),
+        out_specs=[pl.BlockSpec(memory_space=pltpu.VMEM)] * len(shapes),
+        scratch_shapes=scratch,
+        compiler_params=pltpu.CompilerParams(vmem_limit_bytes=16 << 20),
+        name=name,
+    )(*operands)
+
+
+def score_by_rounds(partial, query_grads):
+    def heard(code, sources):
+        got = receive(code.astype(jnp.float16), sources)
+        swapped = swap(got, "tensor", 1)
+        return got.astype(jnp.float32), swapped.astype(jnp.float32)
+
+    seqs, extent = partial.shape
+    wide, narrow = (seqs, extent), (seqs, extent - BESIDE)
+    other = swap(partial, "tensor", 1)
+    mine, code = small_kernel(
+        add_cores_kernel, "add_cores", (partial, other), (wide, wide)
+    )
+    heard_first = heard(code, ROUNDS_OF_8[0])
+    total, code = small_kernel(
+        add_first_kernel, "add_first", (mine, *heard_first), (narrow, wide)
+    )
+    heard_second = heard(code, ROUNDS_OF_8[1])
+    return small_kernel(
+        score_kernel,
+        "score",
+        (total, *heard_second, query_grads),
+        ((seqs, query_grads.shape[0]),),
+        [pltpu.VMEM(narrow, jnp.bfloat16)],
+    )[0]
+
+
+def add_steps(partial):
+    half = (partial.shape[1] - BESIDE) // 2
+    even = lax.axis_index("tensor") == odd(lax.axis_index("dp"))
+    low, high = partial[:, :half], partial[:, half : 2 * half]
+    given = jnp.where(even, high, low)
+    total = jnp.where(even, low, high) + swap(given, "tensor", 1)
+    bits = steps(lax.axis_size("dp"))
+    for pair in zip(bits, bits[::-1]):
+        total = total + flip(total, pair)
+    return ordered(even, total, swap(total, "tensor", 1), 1)
+
+
 def on_device(layer_input, gate_grad, factor_in, factor_out, precondition, query_grads):
-    seq_length, rank = layer_input.shape[0], factor_in.shape[0]
     own_rows, width = precondition.shape
     dp, dp_size = lax.axis_index("dp"), lax.axis_size("dp")
     core = lax.axis_index("tensor")
@@ -280,15 +433,10 @@
         return got
 
     sides = project(layer_input, gate_grad, factor_in, factor_out)
-    sides = sides + swap(sides, "tensor", 1)
-    gradient = lax.dot_general(
-        sides[:, :rank],
-        sides[:, rank:],
-        (((0,), (0,)), ((), ())),
-        precision=lax.Precision.HIGHEST,
-    ) * (1 / math.sqrt(seq_length))
-
-    held = gradient.reshape(1, dp_size, 2 * own_rows)
+    other = beside(sides, swap(sides, "tensor", 1))
+    gradient = gradient_rows(sides, other, dp_size)
+
+    held = gradient[None]
     rounds = gather_rounds(dp_size)
     for number, (sources, swaps) in enumerate(rounds):
         given = held
@@ -304,14 +452,9 @@
 
     partial = precondition_rows(parts, token, bands, dp_size)
 
-    low, high = partial[:, : width // 2], partial[:, width // 2 :]
-    given = jnp.where(core == 0, high, low)
-    total = jnp.where(core == 0, low, high) + swap(given, "tensor", 1)
-    for bit in steps(dp_size):
-        total = total + swap(total, "dp", bit)
-
-    rounded = total.astype(jnp.bfloat16)
-    rounded = ordered(core == 0, rounded, swap(rounded, "tensor", 1), 1)
+    if dp_size == 8:
+        return score_by_rounds(partial, query_grads)
+    rounded = add_steps(partial).astype(jnp.bfloat16)
     return contract_last(rounded, query_grads) * (1 / math.sqrt(width))
 
 

time: 37.4 us -> 33.8 us (0.904)
  starting transfers between devices: 12.8 us -> 10.1 us
  Pallas kernels: 8.83 us -> 11.2 us
  waiting for transfers between devices: 13.8 us -> 12 us
  matrix products: 1.52 us -> 0 us
    ppermute x8 -> x6, waiting for transfers between devices: 13.3 us -> 5.15 us  [swap(): return lax.ppermute(value, axis, [(i, i ^ bit) for i in range(size)])]
    ppermute x2 -> x4, waiting for transfers between devices: 0.49 us -> 6.89 us  [receive(): return lax.ppermute(value, ('dp', 'tensor'), pairs)]
    ppermute x8 -> x6, starting transfers between devices: 8.1 us -> 2.09 us  [swap(): return lax.ppermute(value, axis, [(i, i ^ bit) for i in range(size)])]
    ppermute x2 -> x4, starting transfers between devices: 4.66 us -> 8.02 us  [receive(): return lax.ppermute(value, ('dp', 'tensor'), pairs)]
    dot_general x2 -> x0, matrix products: 1.52 us -> none  [the longest x1 0.85 us: contract_last(): lax.dot_general(left, right, LAST, preferred_element_type=jnp.float32)]
    pallas_call x0 -> x4, Pallas kernels: none -> 1.46 us  [the longest x3 0.94 us: small_kernel(): pl.pallas_call(kernel, out_shape=[jax.ShapeDtypeStruct(shape, jnp.float32...]
    pallas_call x2 -> x3, Pallas kernels: 3.11 us -> 3.99 us  [bring(): pl.pallas_call(lambda *refs: bring_kernel(first, *refs), out_shape=(jax.S...]
  transfers between devices with their start and end apart: 10 -> 10, of which waited for: 10 -> 9; matrix products, arithmetic and copies ran while one was open for 0% -> 0% of each run, Pallas kernels for 8% -> 12%
where the time goes in v4:
time: 33.8 us; the launch traced here: 33.6 us
  waiting for transfers between devices  12 us (36%)
  Pallas kernels  11.2 us (33%)
  starting transfers between devices  10.1 us (30%)
    ppermute x4, starting transfers between devices, receive(): return lax.ppermute(value, ('dp', 'tensor'), pairs)  8.02 us
    ppermute x4, waiting for transfers between devices, receive(): return lax.ppermute(value, ('dp', 'tensor'), pairs)  6.89 us
    ppermute x6, waiting for transfers between devices, swap(): return lax.ppermute(value, axis, [(i, i ^ bit) for i in range(size)])  5.15 us
    pallas_call x1, Pallas kernels, project(): pl.pallas_call(project_kernel, out_shape=jax.ShapeDtypeStruct((tokens, 2...  4.8 us
    pallas_call x3, Pallas kernels, bring(): pl.pallas_call(lambda *refs: bring_kernel(first, *refs), out_shape=(jax.S...  3.99 us
    ppermute x6, starting transfers between devices, swap(): return lax.ppermute(value, axis, [(i, i ^ bit) for i in range(size)])  2.09 us
    pallas_call x1, Pallas kernels, precondition_rows(): pl.pallas_call(functools.partial(precondition_kernel, len(parts)), out_sh...  0.97 us
    pallas_call x3, Pallas kernels, small_kernel(): pl.pallas_call(kernel, out_shape=[jax.ShapeDtypeStruct(shape, jnp.float32...  0.94 us
  transfers between devices with their start and end apart: 10, of which 9 were waited for; matrix products, arithmetic and copies ran while one was open for 0% of the time, Pallas kernels for 12%

profile of v4, /device:TPU:0, one launch (start us, length us, event | category | flops | bytes accessed | tf_op | source)
XLA Modules:
  0.0 33.6 jit_solution(738371647074241360)
XLA Ops:
  0.0 4.8 %project.1.refs_1_.mine_ref = f32[512,128]{1,0:T(8,128)S(1)} custom-call(bf16[512,2048]{1,0:T(8,128)(2,1)} %layer_ref.1, bf16[512,7168]{1,0:T(8,128)(2,1)} %gate_ref.1, bf16[64,2048]{1,0:T(8,128)(2,1)} %in_ref.1, bf16[64,7168]{1,0:T(8,128)(2,1)} %out_ref.1), custom_call_target="tpu_custom_call" | custom-call | flops 603979776 | bytes 10616832 | tf_op jit(solution)/shard_map/project/pallas_call | solution.py:121
  4.8 0.5 %collective-permute-start = (f32[512,128]{1,0:T(8,128)S(1)}, f32[512,128]{1,0:T(8,128)S(1)}, u32[]{:S(2)}, u32[]{:S(2)}) collective-permute-start(f32[512,128]{1,0:T(8,128)S(1)} %project.1.refs_1_.mine_ref), channel_id=1, source_target_pairs={{0,1},{1,0},{2,3},{3,2},{4,5},{5,4},{6,7},{7,6},{8,9},{9,8},{10,11... | collective-permute-start | bytes 786440 | tf_op jit(solution)/shard_map/ppermute | solution.py:282
  5.3 1.2 %bring.3 = (f32[256,1024]{1,0:T(8,128)S(1)}, f32[8,128]{1,0:T(8,128)S(1)}) custom-call(f32[256,4096]{1,0:T(8,128)} %refs_0_.5, f32[512,128]{1,0:T(8,128)S(1)} %project.1.refs_1_.mine_ref), custom_call_target="tpu_custom_call" | custom-call | bytes 1048576 | tf_op jit(solution)/shard_map/bring/pallas_call | solution.py:198
  6.5 0.0 collective-permute-done.other_ref
  6.6 0.5 %gradient.1 = f32[8,512]{1,0:T(8,128)S(1)} custom-call(f32[512,128]{1,0:T(8,128)S(1)} %project.1.refs_1_.mine_ref, f32[512,128]{1,0:T(8,128)S(1)} %collective-permute-done.other_ref), custom_call_target="tpu_custom_call" | custom-call | flops 4194304 | bytes 524288 | tf_op jit(solution)/shard_map/gradient/pallas_call | solution.py:163
  7.1 2.9 %collective-permute-start.1 = (f32[1,8,512]{2,1,0:T(8,128)S(1)}, f32[1,8,512]{2,1,0:T(8,128)S(1)}, u32[]{:S(2)}, u32[]{:S(2)}) collective-permute-start(f32[1,8,512]{2,1,0:T(8,128)S(1)} %bitcast.7), channel_id=1, source_target_pairs={{4,0},{6,2},{0,4},{2,6},{12,8},{14,10},{8,12},{10,14},{9,1},{11,3}... | collective-permute-start | bytes 49160 | tf_op jit(solution)/shard_map/ppermute | solution.py:291
  10.0 1.2 %bring.4 = (f32[256,1024]{1,0:T(8,128)S(1)}, f32[8,128]{1,0:T(8,128)S(1)}) custom-call(f32[256,4096]{1,0:T(8,128)} %refs_0_.5, f32[1,8,512]{2,1,0:T(8,128)S(1)} %bitcast.8, f32[8,128]{1,0:T(8,128)S(1)} %get-tuple-element.27.refs_2_), custom_call_target="tpu_custom_call" | custom-call | bytes 1048576 | tf_op jit(solution)/shard_map/bring/pallas_call | solution.py:198
  11.2 0.5 %collective-permute-done.1 = f32[1,8,512]{2,1,0:T(8,128)S(1)} collective-permute-done((f32[1,8,512]{2,1,0:T(8,128)S(1)}, f32[1,8,512]{2,1,0:T(8,128)S(1)}, u32[]{:S(2)}, u32[]{:S(2)}) %collective-permute-start.1) | collective-permute-done | bytes 16416 | tf_op jit(solution)/shard_map/ppermute | solution.py:291
  11.7 0.4 %collective-permute-start.2 = (f32[1,8,512]{2,1,0:T(8,128)S(1)}, f32[1,8,512]{2,1,0:T(8,128)S(1)}, u32[]{:S(2)}, u32[]{:S(2)}) collective-permute-start(f32[1,8,512]{2,1,0:T(8,128)S(1)} %collective-permute-done.1), channel_id=1, source_target_pairs={{0,1},{1,0},{2,3},{3,2},{4,5},{5,4},{6,7},{7,6},{8,9},{9,8},{10,11... | collective-permute-start | bytes 49160 | tf_op jit(solution)/shard_map/ppermute | solution.py:282
  12.1 0.8 %collective-permute-done.2 = f32[1,8,512]{2,1,0:T(8,128)S(1)} collective-permute-done((f32[1,8,512]{2,1,0:T(8,128)S(1)}, f32[1,8,512]{2,1,0:T(8,128)S(1)}, u32[]{:S(2)}, u32[]{:S(2)}) %collective-permute-start.2) | collective-permute-done | bytes 16416 | tf_op jit(solution)/shard_map/ppermute | solution.py:282
  13.0 0.0 copy-start
  13.0 1.9 %collective-permute-start.3 = (f32[3,512]{1,0:T(4,128)S(1)}, f32[3,512]{1,0:T(4,128)S(1)}, u32[]{:S(2)}, u32[]{:S(2)}) collective-permute-start(f32[3,512]{1,0:T(4,128)S(1)} %bitcast.11), channel_id=1, source_target_pairs={{2,0},{0,2},{8,4},{10,6},{4,8},{6,10},{14,12},{12,14},{9,1},{11,3}... | collective-permute-start | bytes 18440 | tf_op jit(solution)/shard_map/ppermute | solution.py:291
  14.9 1.6 %bring.5 = (f32[256,2048]{1,0:T(8,128)S(1)}, f32[8,128]{1,0:T(8,128)S(1)}) custom-call(f32[256,4096]{1,0:T(8,128)} %refs_0_.5, f32[3,512]{1,0:T(4,128)S(1)} %bitcast.12, f32[8,128]{1,0:T(8,128)S(1)} %get-tuple-element.30.refs_2_), custom_call_target="tpu_custom_call" | custom-call | bytes 2097152 | tf_op jit(solution)/shard_map/bring/pallas_call | solution.py:198
  16.5 0.2 collective-permute-done.3.refs_1_
  16.7 0.7 %collective-permute-start.4 = (f32[3,512]{1,0:T(4,128)S(1)}, f32[3,512]{1,0:T(4,128)S(1)}, u32[]{:S(2)}, u32[]{:S(2)}) collective-permute-start(f32[3,512]{1,0:T(4,128)S(1)} %collective-permute-done.3.refs_1_), channel_id=1, source_target_pairs={{0,1},{1,0},{2,3},{3,2},{4,5},{5,4},{6,7},{7,6},{8,9},{9,8},{10,11... | collective-permute-start | bytes 18440 | tf_op jit(solution)/shard_map/ppermute | solution.py:282
  17.4 0.8 %collective-permute-done.4.refs_2_ = f32[3,512]{1,0:T(4,128)S(1)} collective-permute-done((f32[3,512]{1,0:T(4,128)S(1)}, f32[3,512]{1,0:T(4,128)S(1)}, u32[]{:S(2)}, u32[]{:S(2)}) %collective-permute-start.4) | collective-permute-done | bytes 6176 | tf_op jit(solution)/shard_map/ppermute | solution.py:282
  18.3 1.0 %precondition.1.mine_ref = f32[8,4224]{1,0:T(8,128)S(1)} custom-call(f32[8,128]{1,0:T(8,128)S(1)} %get-tuple-element.34.token_ref, f32[3,512]{1,0:T(4,128)S(1)} %bitcast.10, f32[3,512]{1,0:T(4,128)S(1)} %collective-permute-done.3.refs_1_, f32[3,512]{1,0:T(4,128)S(1)} %collective-permute-done.4.refs_2_, f32[256,1024]{1,0:T(8,128)S(1)} %get-tuple-element.38.refs_3_, ...), custom_call_target="tpu_custom_call" | custom-call | flops 16777216 | bytes 4194304 | tf_op jit(solution)/shard_map/precondition/pallas_call | solution.py:259
  19.2 0.4 %collective-permute-start.5 = (f32[8,4224]{1,0:T(8,128)S(1)}, f32[8,4224]{1,0:T(8,128)S(1)}, u32[]{:S(2)}, u32[]{:S(2)}) collective-permute-start(f32[8,4224]{1,0:T(8,128)S(1)} %precondition.1.mine_ref), channel_id=1, source_target_pairs={{0,1},{1,0},{2,3},{3,2},{4,5},{5,4},{6,7},{7,6},{8,9},{9,8},{10,11... | collective-permute-start | bytes 405512 | tf_op jit(solution)/shard_map/ppermute | solution.py:282
  19.6 1.0 %collective-permute-done.5.other_ref = f32[8,4224]{1,0:T(8,128)S(1)} collective-permute-done((f32[8,4224]{1,0:T(8,128)S(1)}, f32[8,4224]{1,0:T(8,128)S(1)}, u32[]{:S(2)}, u32[]{:S(2)}) %collective-permute-start.5) | collective-permute-done | bytes 135200 | tf_op jit(solution)/shard_map/ppermute | solution.py:282
  20.7 1.7 %collective-permute-start.6 = (f16[8,4224]{1,0:T(8,128)(2,1)S(1)}, f16[8,4224]{1,0:T(8,128)(2,1)S(1)}, u32[]{:S(2)}, u32[]{:S(2)}) collective-permute-start(f16[8,4224]{1,0:T(8,128)(2,1)S(1)} %convert_element_type.18), channel_id=1, source_target_pairs={{4,0},{6,2},{0,4},{2,6},{12,8},{14,10},{8,12},{10,14},{9,1},{11,3}... | collective-permute-start | bytes 202760 | tf_op jit(solution)/shard_map/ppermute | solution.py:291
  22.4 3.3 %collective-permute-done.6 = f16[8,4224]{1,0:T(8,128)(2,1)S(1)} collective-permute-done((f16[8,4224]{1,0:T(8,128)(2,1)S(1)}, f16[8,4224]{1,0:T(8,128)(2,1)S(1)}, u32[]{:S(2)}, u32[]{:S(2)}) %collective-permute-start.6) | collective-permute-done | bytes 67616 | tf_op jit(solution)/shard_map/ppermute | solution.py:291
  25.8 0.0 collective-permute-start.7
  25.8 1.2 %collective-permute-done.7 = f16[8,4224]{1,0:T(8,128)(2,1)S(1)} collective-permute-done((f16[8,4224]{1,0:T(8,128)(2,1)S(1)}, f16[8,4224]{1,0:T(8,128)(2,1)S(1)}, u32[]{:S(2)}, u32[]{:S(2)}) %collective-permute-start.7) | collective-permute-done | bytes 67616 | tf_op jit(solution)/shard_map/ppermute | solution.py:282
  27.1 1.5 %collective-permute-start.8 = (f16[8,4224]{1,0:T(8,128)(2,1)S(1)}, f16[8,4224]{1,0:T(8,128)(2,1)S(1)}, u32[]{:S(2)}, u32[]{:S(2)}) collective-permute-start(f16[8,4224]{1,0:T(8,128)(2,1)S(1)} %convert_element_type.21), channel_id=1, source_target_pairs={{2,0},{0,2},{8,4},{10,6},{4,8},{6,10},{14,12},{12,14},{9,1},{11,3}... | collective-permute-start | bytes 202760 | tf_op jit(solution)/shard_map/ppermute | solution.py:291
  28.6 2.8 %collective-permute-done.8 = f16[8,4224]{1,0:T(8,128)(2,1)S(1)} collective-permute-done((f16[8,4224]{1,0:T(8,128)(2,1)S(1)}, f16[8,4224]{1,0:T(8,128)(2,1)S(1)}, u32[]{:S(2)}, u32[]{:S(2)}) %collective-permute-start.8) | collective-permute-done | bytes 67616 | tf_op jit(solution)/shard_map/ppermute | solution.py:291
  31.4 0.0 collective-permute-start.9
  31.5 1.2 %collective-permute-done.9 = f16[8,4224]{1,0:T(8,128)(2,1)S(1)} collective-permute-done((f16[8,4224]{1,0:T(8,128)(2,1)S(1)}, f16[8,4224]{1,0:T(8,128)(2,1)S(1)}, u32[]{:S(2)}, u32[]{:S(2)}) %collective-permute-start.9) | collective-permute-done | bytes 67616 | tf_op jit(solution)/shard_map/ppermute | solution.py:282
  32.7 0.0 copy-done
  32.7 0.9 %score.1 = f32[8,64]{1,0:T(8,128)} custom-call(f32[8,4096]{1,0:T(8,128)S(1)} %get-tuple-element.43.sum_ref, f32[8,4224]{1,0:T(8,128)S(1)} %convert_element_type.22.got_ref, f32[8,4224]{1,0:T(8,128)S(1)} %convert_element_type.23.swapped_ref, bf16[64,4096]{1,0:T(8,128)(2,1)S(1)} %copy-done), custom_call_target="tpu_custom_call" | custom-call | tf_op jit(solution)/shard_map/score/pallas_call | solution.py:369
  (12 shorter events, 0.2 us)
Async XLA Ops:
  4.8 1.7 %collective-permute-start = (f32[512,128]{1,0:T(8,128)S(1)}, f32[512,128]{1,0:T(8,128)S(1)}, u32[]{:S(2)}, u32[]{:S(2)}) collective-permute-start(f32[512,128]{1,0:T(8,128)S(1)} %project.1.refs_1_.mine_ref), channel_id=1, source_target_pairs={{0,1},{1,0},{2,3},{3,2},{4,5},{5,4},{6,7},{7,6},{8,9},{9,8},{10,11... | collective-permute-start | bytes 786440 | tf_op jit(solution)/shard_map/ppermute | solution.py:282
  7.1 4.6 %collective-permute-start.1 = (f32[1,8,512]{2,1,0:T(8,128)S(1)}, f32[1,8,512]{2,1,0:T(8,128)S(1)}, u32[]{:S(2)}, u32[]{:S(2)}) collective-permute-start(f32[1,8,512]{2,1,0:T(8,128)S(1)} %bitcast.7), channel_id=1, source_target_pairs={{4,0},{6,2},{0,4},{2,6},{12,8},{14,10},{8,12},{10,14},{9,1},{11,3}... | collective-permute-start | bytes 49160 | tf_op jit(solution)/shard_map/ppermute | solution.py:291
  11.7 1.3 %collective-permute-start.2 = (f32[1,8,512]{2,1,0:T(8,128)S(1)}, f32[1,8,512]{2,1,0:T(8,128)S(1)}, u32[]{:S(2)}, u32[]{:S(2)}) collective-permute-start(f32[1,8,512]{2,1,0:T(8,128)S(1)} %collective-permute-done.1), channel_id=1, source_target_pairs={{0,1},{1,0},{2,3},{3,2},{4,5},{5,4},{6,7},{7,6},{8,9},{9,8},{10,11... | collective-permute-start | bytes 49160 | tf_op jit(solution)/shard_map/ppermute | solution.py:282
  13.0 19.7 %copy-start = (bf16[64,4096]{1,0:T(8,128)(2,1)S(1)}, bf16[64,4096]{1,0:T(8,128)(2,1)}, u32[]{:S(2)}) copy-start(bf16[64,4096]{1,0:T(8,128)(2,1)} %query_ref.1) | copy-start | bytes 1572868
  13.0 3.7 %collective-permute-start.3 = (f32[3,512]{1,0:T(4,128)S(1)}, f32[3,512]{1,0:T(4,128)S(1)}, u32[]{:S(2)}, u32[]{:S(2)}) collective-permute-start(f32[3,512]{1,0:T(4,128)S(1)} %bitcast.11), channel_id=1, source_target_pairs={{2,0},{0,2},{8,4},{10,6},{4,8},{6,10},{14,12},{12,14},{9,1},{11,3}... | collective-permute-start | bytes 18440 | tf_op jit(solution)/shard_map/ppermute | solution.py:291
  16.7 1.6 %collective-permute-start.4 = (f32[3,512]{1,0:T(4,128)S(1)}, f32[3,512]{1,0:T(4,128)S(1)}, u32[]{:S(2)}, u32[]{:S(2)}) collective-permute-start(f32[3,512]{1,0:T(4,128)S(1)} %collective-permute-done.3.refs_1_), channel_id=1, source_target_pairs={{0,1},{1,0},{2,3},{3,2},{4,5},{5,4},{6,7},{7,6},{8,9},{9,8},{10,11... | collective-permute-start | bytes 18440 | tf_op jit(solution)/shard_map/ppermute | solution.py:282
  19.2 1.4 %collective-permute-start.5 = (f32[8,4224]{1,0:T(8,128)S(1)}, f32[8,4224]{1,0:T(8,128)S(1)}, u32[]{:S(2)}, u32[]{:S(2)}) collective-permute-start(f32[8,4224]{1,0:T(8,128)S(1)} %precondition.1.mine_ref), channel_id=1, source_target_pairs={{0,1},{1,0},{2,3},{3,2},{4,5},{5,4},{6,7},{7,6},{8,9},{9,8},{10,11... | collective-permute-start | bytes 405512 | tf_op jit(solution)/shard_map/ppermute | solution.py:282
  20.7 5.1 %collective-permute-start.6 = (f16[8,4224]{1,0:T(8,128)(2,1)S(1)}, f16[8,4224]{1,0:T(8,128)(2,1)S(1)}, u32[]{:S(2)}, u32[]{:S(2)}) collective-permute-start(f16[8,4224]{1,0:T(8,128)(2,1)S(1)} %convert_element_type.18), channel_id=1, source_target_pairs={{4,0},{6,2},{0,4},{2,6},{12,8},{14,10},{8,12},{10,14},{9,1},{11,3}... | collective-permute-start | bytes 202760 | tf_op jit(solution)/shard_map/ppermute | solution.py:291
  25.8 1.3 %collective-permute-start.7 = (f16[8,4224]{1,0:T(8,128)(2,1)S(1)}, f16[8,4224]{1,0:T(8,128)(2,1)S(1)}, u32[]{:S(2)}, u32[]{:S(2)}) collective-permute-start(f16[8,4224]{1,0:T(8,128)(2,1)S(1)} %collective-permute-done.6), channel_id=1, source_target_pairs={{0,1},{1,0},{2,3},{3,2},{4,5},{5,4},{6,7},{7,6},{8,9},{9,8},{10,11... | collective-permute-start | bytes 202760 | tf_op jit(solution)/shard_map/ppermute | solution.py:282
  27.1 4.3 %collective-permute-start.8 = (f16[8,4224]{1,0:T(8,128)(2,1)S(1)}, f16[8,4224]{1,0:T(8,128)(2,1)S(1)}, u32[]{:S(2)}, u32[]{:S(2)}) collective-permute-start(f16[8,4224]{1,0:T(8,128)(2,1)S(1)} %convert_element_type.21), channel_id=1, source_target_pairs={{2,0},{0,2},{8,4},{10,6},{4,8},{6,10},{14,12},{12,14},{9,1},{11,3}... | collective-permute-start | bytes 202760 | tf_op jit(solution)/shard_map/ppermute | solution.py:291
  31.4 1.3 %collective-permute-start.9 = (f16[8,4224]{1,0:T(8,128)(2,1)S(1)}, f16[8,4224]{1,0:T(8,128)(2,1)S(1)}, u32[]{:S(2)}, u32[]{:S(2)}) collective-permute-start(f16[8,4224]{1,0:T(8,128)(2,1)S(1)} %collective-permute-done.8), channel_id=1, source_target_pairs={{0,1},{1,0},{2,3},{3,2},{4,5},{5,4},{6,7},{7,6},{8,9},{9,8},{10,11... | collective-permute-start | bytes 202760 | tf_op jit(solution)/shard_map/ppermute | solution.py:282

commit v5 on v4

--- a/solution.py
+++ b/solution.py
@@ -11,7 +11,6 @@
 CHUNK = 1024
 BAND = 512
 BESIDE = 128
-SHARES = (1, 1, 2)
 LAST = (((1,), (1,)), ((), ()))
 
 ROUNDS_OF_8 = (
@@ -140,7 +139,7 @@
 
 def gradient_kernel(mine_ref, other_ref, result_ref, square):
     tokens, rank = mine_ref.shape[0], square.shape[0]
-    terms = jnp.concatenate(split(mine_ref[...] + other_ref[...], 3), axis=1)
+    terms = jnp.concatenate(split(mine_ref[...] + other_ref[...], 2), axis=1)
     product = lax.dot_general(
         terms, terms, (((0,), (0,)), ((), ())), preferred_element_type=jnp.float32
     )
@@ -149,8 +148,7 @@
         rows = product[2 * rank * i : 2 * rank * i + rank]
         return rows[:, 2 * rank * j : 2 * rank * (j + 1)]
 
-    small = block(0, 2) + block(2, 0) + block(1, 1)
-    full = block(0, 0) + (block(0, 1) + block(1, 0) + small)
+    full = block(0, 0) + (block(0, 1) + block(1, 0) + block(1, 1))
     square[...] = full[:, rank:] * (1 / math.sqrt(tokens))
     rows = result_ref.shape[0]
     each = rank // rows
@@ -176,42 +174,6 @@
     )(mine, other)
 
 
-def bring_kernel(first, matrix_ref, *refs):
-    band_ref, here_ref, sems = refs[-3:]
-    copies = [
-        pltpu.make_async_copy(
-            matrix_ref.at[:, pl.ds(first + start, BAND)],
-            band_ref.at[:, pl.ds(start, BAND)],
-            sems.at[number],
-        )
-        for number, start in enumerate(range(0, band_ref.shape[1], BAND))
-    ]
-    for copy in copies:
-        copy.start()
-    here_ref[...] = jnp.zeros_like(here_ref)
-    for copy in copies:
-        copy.wait()
-
-
-def bring(matrix, first, width, *after):
-    rows = matrix.shape[0]
-    return pl.pallas_call(
-        lambda *refs: bring_kernel(first, *refs),
-        out_shape=(
-            jax.ShapeDtypeStruct((rows, width), matrix.dtype),
-            jax.ShapeDtypeStruct((8, 128), jnp.float32),
-        ),
-        in_specs=[pl.BlockSpec(memory_space=pl.ANY)] * (1 + len(after)),
-        out_specs=[pl.BlockSpec(memory_space=pltpu.VMEM)] * 2,
-        scratch_shapes=[pltpu.SemaphoreType.DMA((width // BAND,))],
-        compiler_params=pltpu.CompilerParams(vmem_limit_bytes=49 << 20),
-        cost_estimate=pl.CostEstimate(
-            flops=0, bytes_accessed=4 * rows * width, transcendentals=0
-        ),
-        name="bring",
-    )(matrix, *after)
-
-
 def split(value, terms):
     parts = []
     for _ in range(terms):
@@ -221,10 +183,59 @@
     return parts
 
 
-def precondition_kernel(parts, token_ref, *refs):
+def pack_kernel(sources, *refs):
+    *held_refs, given_ref, kept_ref = refs
+    core, dp = lax.axis_index("tensor"), lax.axis_index("dp")
+    target = gather_target(sources, core, dp)
+    for row, ref in enumerate(held_refs):
+        given_ref[row : row + 1] = ref[pl.ds(target, 1), :]
+        kept_ref[row : row + 1] = ref[pl.ds(dp, 1), :]
+
+
+def pack(held, sources):
+    return pl.pallas_call(
+        functools.partial(pack_kernel, sources),
+        out_shape=[jax.ShapeDtypeStruct((len(held), held[0].shape[1]), jnp.float32)] * 2,
+        in_specs=[pl.BlockSpec(memory_space=pltpu.VMEM)] * len(held),
+        out_specs=[pl.BlockSpec(memory_space=pltpu.VMEM)] * 2,
+        compiler_params=pltpu.CompilerParams(vmem_limit_bytes=16 << 20),
+        name="pack",
+    )(*held)
+
+
+def split_kernel(after_ref, *refs):
+    del after_ref
+    *bands, high_ref, low_ref = refs
+    first = 0
+    for band_ref in bands:
+        for start in range(0, band_ref.shape[1], BAND):
+            lanes = slice(first + start, first + start + BAND)
+            high_ref[:, lanes], low_ref[:, lanes] = split(
+                band_ref[:, start : start + BAND], 2
+            )
+        first += band_ref.shape[1]
+
+
+def split_bands(bands, after):
+    shape = (bands[0].shape[0], sum(band.shape[1] for band in bands))
+    return pl.pallas_call(
+        split_kernel,
+        out_shape=[jax.ShapeDtypeStruct(shape, jnp.bfloat16)] * 2,
+        in_specs=[pl.BlockSpec(memory_space=pl.ANY)]
+        + [pl.BlockSpec(memory_space=pltpu.VMEM)] * len(bands),
+        out_specs=[pl.BlockSpec(memory_space=pltpu.VMEM)] * 2,
+        compiler_params=pltpu.CompilerParams(vmem_limit_bytes=16 << 20),
+        cost_estimate=pl.CostEstimate(
+            flops=0, bytes_accessed=8 * shape[0] * shape[1], transcendentals=0
+        ),
+        name="split",
+    )(after, *bands)
+
+
+def precondition_kernel(token_ref, *refs):
     del token_ref
     *refs, result_ref, held = refs
-    part_refs, bands = refs[:parts], refs[parts:]
+    *part_refs, high_ref, low_ref = refs
     seqs, rows = result_ref.shape[0], held.shape[1]
     core, first = lax.axis_index("tensor"), 0
     for part_ref in part_refs:
@@ -235,32 +246,29 @@
     grads = jnp.concatenate(
         [held[pl.ds(slot(s), 1), :] for s in range(seqs)], axis=0
     )
-    grads = jnp.concatenate(split(grads, 3), axis=0)
-    first = 0
-    for band_ref in bands:
-        for start in range(0, band_ref.shape[1], BAND):
-            high, low = split(band_ref[:, start : start + BAND], 2)
-            by_high = jnp.dot(grads, high, preferred_element_type=jnp.float32)
-            by_low = jnp.dot(grads[: 2 * seqs], low, preferred_element_type=jnp.float32)
-            small = by_high[2 * seqs :] + by_low[seqs:]
-            middle = by_high[seqs : 2 * seqs] + by_low[:seqs]
-            result_ref[:, first + start : first + start + BAND] = by_high[:seqs] + (
-                middle + small
-            )
-        first += band_ref.shape[1]
-    top = jnp.max(jnp.abs(result_ref[:, :first]), axis=1, keepdims=True)
+    grads = jnp.concatenate(split(grads, 2), axis=0)
+    width = high_ref.shape[1]
+    for start in range(0, width, BAND):
+        lanes = slice(start, start + BAND)
+        by_high, by_low = (
+            jnp.dot(grads, ref[:, lanes], preferred_element_type=jnp.float32)
+            for ref in (high_ref, low_ref)
+        )
+        small = by_high[seqs:] + by_low[:seqs] + by_low[seqs:]
+        result_ref[:, lanes] = by_high[:seqs] + small
+    top = jnp.max(jnp.abs(result_ref[:, :width]), axis=1, keepdims=True)
     power = jnp.floor(jnp.log2(jnp.clip(top, 1e-30, 1e30))) - 14
-    result_ref[:, first:] = jnp.broadcast_to(power, (seqs, BESIDE))
-
-
-def precondition_rows(parts, token, bands, seqs):
-    rows, width = bands[0].shape[0], sum(band.shape[1] for band in bands)
+    result_ref[:, width:] = jnp.broadcast_to(power, (seqs, BESIDE))
+
+
+def precondition_rows(parts, token, matrices, seqs):
+    rows, width = matrices[0].shape
     held = sum(part.shape[0] for part in parts)
     return pl.pallas_call(
-        functools.partial(precondition_kernel, len(parts)),
+        precondition_kernel,
         out_shape=jax.ShapeDtypeStruct((seqs, width + BESIDE), jnp.float32),
         in_specs=[pl.BlockSpec(memory_space=pl.ANY)]
-        + [pl.BlockSpec(memory_space=pltpu.VMEM)] * (len(parts) + len(bands)),
+        + [pl.BlockSpec(memory_space=pltpu.VMEM)] * (len(parts) + len(matrices)),
         out_specs=pl.BlockSpec(memory_space=pltpu.VMEM),
         scratch_shapes=[pltpu.VMEM((held, rows), jnp.float32)],
         compiler_params=pltpu.CompilerParams(vmem_limit_bytes=16 << 20),
@@ -270,7 +278,7 @@
             transcendentals=0,
         ),
         name="precondition",
-    )(token, *parts, *bands)
+    )(token, *parts, *matrices)
 
 
 def contract_last(left, right):
@@ -282,9 +290,9 @@
     return lax.ppermute(value, axis, [(i, i ^ bit) for i in range(size)])
 
 
-def receive(value, sources):
+def receive(value, sources, across=0):
     pairs = [
-        (2 * source + core, 2 * chip + core)
+        (2 * source + (core ^ across), 2 * chip + core)
         for core in range(2)
         for chip, source in enumerate(sources[core])
     ]
@@ -378,8 +386,8 @@
 
 
 def score_by_rounds(partial, query_grads):
-    def heard(code, sources):
-        got = receive(code.astype(jnp.float16), sources)
+    def heard(code, sources, across):
+        got = receive(code.astype(jnp.float16), sources, across)
         swapped = swap(got, "tensor", 1)
         return got.astype(jnp.float32), swapped.astype(jnp.float32)
 
@@ -389,11 +397,11 @@
     mine, code = small_kernel(
         add_cores_kernel, "add_cores", (partial, other), (wide, wide)
     )
-    heard_first = heard(code, ROUNDS_OF_8[0])
+    heard_first = heard(code, ROUNDS_OF_8[0][::-1], 1)
     total, code = small_kernel(
         add_first_kernel, "add_first", (mine, *heard_first), (narrow, wide)
     )
-    heard_second = heard(code, ROUNDS_OF_8[1])
+    heard_second = heard(code, ROUNDS_OF_8[1], 0)
     return small_kernel(
         score_kernel,
         "score",
@@ -418,39 +426,26 @@
 def on_device(layer_input, gate_grad, factor_in, factor_out, precondition, query_grads):
     own_rows, width = precondition.shape
     dp, dp_size = lax.axis_index("dp"), lax.axis_size("dp")
-    core = lax.axis_index("tensor")
-
-    bands, tokens = [], []
-
-    def beside(given, got):
-        if len(bands) < len(SHARES):
-            first = sum(band.shape[1] for band in bands)
-            share = width * SHARES[len(bands)] // sum(SHARES)
-            band, token = bring(precondition, first, share, given, *tokens[-1:])
-            got, token = lax.optimization_barrier((got, token))
-            bands.append(band)
-            tokens.append(token)
-        return got
 
     sides = project(layer_input, gate_grad, factor_in, factor_out)
-    other = beside(sides, swap(sides, "tensor", 1))
+    other = swap(sides, "tensor", 1)
     gradient = gradient_rows(sides, other, dp_size)
 
-    held = gradient[None]
+    held = [gradient]
     rounds = gather_rounds(dp_size)
     for number, (sources, swaps) in enumerate(rounds):
-        given = held
         if number == len(rounds) - 1:
-            target = gather_target(sources, core, dp)
-            given = lax.dynamic_index_in_dim(held, target, 1, keepdims=False)
-            held = lax.dynamic_index_in_dim(held, dp, 1, keepdims=False)
-        got = beside(given, receive(given, sources))
-        parts = [held, got] + ([swap(got, "tensor", 1)] if swaps else [])
-        if number < len(rounds) - 1:
-            held = jnp.concatenate(parts, axis=0)
-    *parts, token = lax.optimization_barrier((*parts, tokens[-1]))
-
-    partial = precondition_rows(parts, token, bands, dp_size)
+            given, kept = pack(held, sources)
+            got = receive(given, sources)
+            parts = [kept, got] + ([swap(got, "tensor", 1)] if swaps else [])
+        else:
+            given = held[0] if number == 0 else jnp.stack(held)
+            got = receive(given, sources)
+            heard = [got] + ([swap(got, "tensor", 1)] if swaps else [])
+            held += [row for rows in heard for row in (rows if number else [rows])]
+    matrices = split_bands([precondition], got)
+
+    partial = precondition_rows(parts, got, matrices, dp_size)
 
     if dp_size == 8:
         return score_by_rounds(partial, query_grads)

time: 33.8 us -> 33 us (0.976)
  Pallas kernels: 11.2 us -> 7.74 us
  waiting for transfers between devices: 12 us -> 14.2 us
  starting transfers between devices: 10.1 us -> 10.7 us
    pallas_call x4 -> x3, Pallas kernels: 4.96 us -> 1.47 us  [the longest x1 0.76 us: split_bands(): pl.pallas_call(split_kernel, out_shape=[jax.ShapeDtypeStruct(shape, jnp.b...]
    ppermute x4, waiting for transfers between devices: 6.89 us -> 8.86 us  [receive(): return lax.ppermute(value, ('dp', 'tensor'), pairs)]
    ppermute x4, starting transfers between devices: 8.02 us -> 8.81 us  [receive(): return lax.ppermute(value, ('dp', 'tensor'), pairs)]
  transfers between devices with their start and end apart: 10 -> 10, of which waited for: 9 -> 10; matrix products, arithmetic and copies ran while one was open for 0% -> 0% of each run, Pallas kernels for 12% -> 2%
where the time goes in v5:
time: 33 us; the launch traced here: 32.8 us
  waiting for transfers between devices  14.2 us (43%)
  starting transfers between devices  10.7 us (32%)
  Pallas kernels  7.74 us (23%)
    ppermute x4, waiting for transfers between devices, receive(): return lax.ppermute(value, ('dp', 'tensor'), pairs)  8.86 us
    ppermute x4, starting transfers between devices, receive(): return lax.ppermute(value, ('dp', 'tensor'), pairs)  8.81 us
    ppermute x6, waiting for transfers between devices, swap(): return lax.ppermute(value, axis, [(i, i ^ bit) for i in range(size)])  5.35 us
    pallas_call x1, Pallas kernels, project(): pl.pallas_call(project_kernel, out_shape=jax.ShapeDtypeStruct((tokens, 2...  4.93 us
    ppermute x6, starting transfers between devices, swap(): return lax.ppermute(value, axis, [(i, i ^ bit) for i in range(size)])  1.92 us
    pallas_call x3, Pallas kernels, small_kernel(): pl.pallas_call(kernel, out_shape=[jax.ShapeDtypeStruct(shape, jnp.float32...  0.94 us
    pallas_call x1, Pallas kernels, split_bands(): pl.pallas_call(split_kernel, out_shape=[jax.ShapeDtypeStruct(shape, jnp.b...  0.76 us
    pallas_call x1, Pallas kernels, precondition_rows(): pl.pallas_call(precondition_kernel, out_shape=jax.ShapeDtypeStruct((seqs,...  0.7 us
  transfers between devices with their start and end apart: 10, of which 10 were waited for; matrix products, arithmetic and copies ran while one was open for 0% of the time, Pallas kernels for 2%

profile of v5, /device:TPU:0, one launch (start us, length us, event | category | flops | bytes accessed | tf_op | source)
XLA Modules:
  0.0 32.8 jit_solution(2227067178672569065)
XLA Ops:
  0.0 0.0 copy-start
  0.0 4.9 %project.1.mine_ref = f32[512,128]{1,0:T(8,128)S(1)} custom-call(bf16[512,2048]{1,0:T(8,128)(2,1)} %layer_ref.1, bf16[512,7168]{1,0:T(8,128)(2,1)} %gate_ref.1, bf16[64,2048]{1,0:T(8,128)(2,1)} %in_ref.1, bf16[64,7168]{1,0:T(8,128)(2,1)} %out_ref.1), custom_call_target="tpu_custom_call" | custom-call | flops 603979776 | bytes 10616832 | tf_op jit(solution)/shard_map/project/pallas_call | solution.py:120
  4.9 0.5 %collective-permute-start = (f32[512,128]{1,0:T(8,128)S(1)}, f32[512,128]{1,0:T(8,128)S(1)}, u32[]{:S(2)}, u32[]{:S(2)}) collective-permute-start(f32[512,128]{1,0:T(8,128)S(1)} %project.1.mine_ref), channel_id=1, source_target_pairs={{0,1},{1,0},{2,3},{3,2},{4,5},{5,4},{6,7},{7,6},{8,9},{9,8},{10,11... | collective-permute-start | bytes 786440 | tf_op jit(solution)/shard_map/ppermute | solution.py:290
  5.5 1.2 %collective-permute-done.other_ref = f32[512,128]{1,0:T(8,128)S(1)} collective-permute-done((f32[512,128]{1,0:T(8,128)S(1)}, f32[512,128]{1,0:T(8,128)S(1)}, u32[]{:S(2)}, u32[]{:S(2)}) %collective-permute-start) | collective-permute-done | bytes 262176 | tf_op jit(solution)/shard_map/ppermute | solution.py:290
  6.6 0.4 %gradient.1.refs_0_ = f32[8,512]{1,0:T(8,128)S(1)} custom-call(f32[512,128]{1,0:T(8,128)S(1)} %project.1.mine_ref, f32[512,128]{1,0:T(8,128)S(1)} %collective-permute-done.other_ref), custom_call_target="tpu_custom_call" | custom-call | flops 4194304 | bytes 524288 | tf_op jit(solution)/shard_map/gradient/pallas_call | solution.py:161
  7.0 2.9 %collective-permute-start.1 = (f32[8,512]{1,0:T(8,128)S(1)}, f32[8,512]{1,0:T(8,128)S(1)}, u32[]{:S(2)}, u32[]{:S(2)}) collective-permute-start(f32[8,512]{1,0:T(8,128)S(1)} %gradient.1.refs_0_), channel_id=1, source_target_pairs={{4,0},{6,2},{0,4},{2,6},{12,8},{14,10},{8,12},{10,14},{9,1},{11,3}... | collective-permute-start | bytes 49160 | tf_op jit(solution)/shard_map/ppermute | solution.py:299
  10.0 1.7 %collective-permute-done.1.refs_1_ = f32[8,512]{1,0:T(8,128)S(1)} collective-permute-done((f32[8,512]{1,0:T(8,128)S(1)}, f32[8,512]{1,0:T(8,128)S(1)}, u32[]{:S(2)}, u32[]{:S(2)}) %collective-permute-start.1) | collective-permute-done | bytes 16416 | tf_op jit(solution)/shard_map/ppermute | solution.py:299
  11.7 0.3 collective-permute-start.2
  12.0 0.9 %collective-permute-done.2.refs_2_ = f32[8,512]{1,0:T(8,128)S(1)} collective-permute-done((f32[8,512]{1,0:T(8,128)S(1)}, f32[8,512]{1,0:T(8,128)S(1)}, u32[]{:S(2)}, u32[]{:S(2)}) %collective-permute-start.2) | collective-permute-done | bytes 16416 | tf_op jit(solution)/shard_map/ppermute | solution.py:290
  12.9 2.1 %collective-permute-start.3 = (f32[3,512]{1,0:T(4,128)S(1)}, f32[3,512]{1,0:T(4,128)S(1)}, u32[]{:S(2)}, u32[]{:S(2)}) collective-permute-start(f32[3,512]{1,0:T(4,128)S(1)} %get-tuple-element.13), channel_id=1, source_target_pairs={{2,0},{0,2},{8,4},{10,6},{4,8},{6,10},{14,12},{12,14},{9,1},{11,3}... | collective-permute-start | bytes 18440 | tf_op jit(solution)/shard_map/ppermute | solution.py:299
  15.0 1.6 %collective-permute-done.3.after_ref.token_ref.refs_1_ = f32[3,512]{1,0:T(4,128)S(1)} collective-permute-done((f32[3,512]{1,0:T(4,128)S(1)}, f32[3,512]{1,0:T(4,128)S(1)}, u32[]{:S(2)}, u32[]{:S(2)}) %collective-permute-start.3) | collective-permute-done | bytes 6176 | tf_op jit(solution)/shard_map/ppermute | solution.py:299
  16.6 0.3 collective-permute-start.4
  16.9 0.0 copy-done
  16.9 0.8 %split.1 = (bf16[256,4096]{1,0:T(8,128)(2,1)S(1)}, bf16[256,4096]{1,0:T(8,128)(2,1)S(1)}) custom-call(f32[3,512]{1,0:T(4,128)S(1)} %collective-permute-done.3.after_ref.token_ref.refs_1_, f32[256,4096]{1,0:T(8,128)S(1)} %copy-done), custom_call_target="tpu_custom_call" | custom-call | bytes 8388608 | tf_op jit(solution)/shard_map/split/pallas_call | solution.py:221
  17.7 0.1 collective-permute-done.4.refs_2_
  17.8 0.0 copy-start.1
  17.8 0.7 %precondition.1.mine_ref = f32[8,4224]{1,0:T(8,128)S(1)} custom-call(f32[3,512]{1,0:T(4,128)S(1)} %collective-permute-done.3.after_ref.token_ref.refs_1_, f32[3,512]{1,0:T(4,128)S(1)} %get-tuple-element.14.refs_0_, f32[3,512]{1,0:T(4,128)S(1)} %collective-permute-done.3.after_ref.token_ref.refs_1_, f32[3,512]{1,0:T(4,128)S(1)} %collective-permute-done.4.refs_2_, ...), custom_call_target="tpu_custom_call" | custom-call | flops 16777216 | bytes 4194304 | tf_op jit(solution)/shard_map/precondition/pallas_call | solution.py:267
  18.5 0.4 %collective-permute-start.5 = (f32[8,4224]{1,0:T(8,128)S(1)}, f32[8,4224]{1,0:T(8,128)S(1)}, u32[]{:S(2)}, u32[]{:S(2)}) collective-permute-start(f32[8,4224]{1,0:T(8,128)S(1)} %precondition.1.mine_ref), channel_id=1, source_target_pairs={{0,1},{1,0},{2,3},{3,2},{4,5},{5,4},{6,7},{7,6},{8,9},{9,8},{10,11... | collective-permute-start | bytes 405512 | tf_op jit(solution)/shard_map/ppermute | solution.py:290
  18.9 1.1 %collective-permute-done.5.other_ref = f32[8,4224]{1,0:T(8,128)S(1)} collective-permute-done((f32[8,4224]{1,0:T(8,128)S(1)}, f32[8,4224]{1,0:T(8,128)S(1)}, u32[]{:S(2)}, u32[]{:S(2)}) %collective-permute-start.5) | collective-permute-done | bytes 135200 | tf_op jit(solution)/shard_map/ppermute | solution.py:290
  20.0 1.8 %collective-permute-start.6 = (f16[8,4224]{1,0:T(8,128)(2,1)S(1)}, f16[8,4224]{1,0:T(8,128)(2,1)S(1)}, u32[]{:S(2)}, u32[]{:S(2)}) collective-permute-start(f16[8,4224]{1,0:T(8,128)(2,1)S(1)} %convert_element_type.18), channel_id=1, source_target_pairs={{9,0},{11,2},{3,4},{1,6},{15,8},{13,10},{5,12},{7,14},{4,1},{6,3},... | collective-permute-start | bytes 202760 | tf_op jit(solution)/shard_map/ppermute | solution.py:299
  21.8 3.1 %collective-permute-done.6 = f16[8,4224]{1,0:T(8,128)(2,1)S(1)} collective-permute-done((f16[8,4224]{1,0:T(8,128)(2,1)S(1)}, f16[8,4224]{1,0:T(8,128)(2,1)S(1)}, u32[]{:S(2)}, u32[]{:S(2)}) %collective-permute-start.6) | collective-permute-done | bytes 67616 | tf_op jit(solution)/shard_map/ppermute | solution.py:299
  24.9 0.0 collective-permute-start.7
  24.9 1.2 %collective-permute-done.7 = f16[8,4224]{1,0:T(8,128)(2,1)S(1)} collective-permute-done((f16[8,4224]{1,0:T(8,128)(2,1)S(1)}, f16[8,4224]{1,0:T(8,128)(2,1)S(1)}, u32[]{:S(2)}, u32[]{:S(2)}) %collective-permute-start.7) | collective-permute-done | bytes 67616 | tf_op jit(solution)/shard_map/ppermute | solution.py:290
  26.2 1.9 %collective-permute-start.8 = (f16[8,4224]{1,0:T(8,128)(2,1)S(1)}, f16[8,4224]{1,0:T(8,128)(2,1)S(1)}, u32[]{:S(2)}, u32[]{:S(2)}) collective-permute-start(f16[8,4224]{1,0:T(8,128)(2,1)S(1)} %convert_element_type.21), channel_id=1, source_target_pairs={{2,0},{0,2},{8,4},{10,6},{4,8},{6,10},{14,12},{12,14},{9,1},{11,3}... | collective-permute-start | bytes 202760 | tf_op jit(solution)/shard_map/ppermute | solution.py:299
  28.2 2.4 %collective-permute-done.8 = f16[8,4224]{1,0:T(8,128)(2,1)S(1)} collective-permute-done((f16[8,4224]{1,0:T(8,128)(2,1)S(1)}, f16[8,4224]{1,0:T(8,128)(2,1)S(1)}, u32[]{:S(2)}, u32[]{:S(2)}) %collective-permute-start.8) | collective-permute-done | bytes 67616 | tf_op jit(solution)/shard_map/ppermute | solution.py:299
  30.6 0.5 %collective-permute-start.9 = (f16[8,4224]{1,0:T(8,128)(2,1)S(1)}, f16[8,4224]{1,0:T(8,128)(2,1)S(1)}, u32[]{:S(2)}, u32[]{:S(2)}) collective-permute-start(f16[8,4224]{1,0:T(8,128)(2,1)S(1)} %collective-permute-done.8), channel_id=1, source_target_pairs={{0,1},{1,0},{2,3},{3,2},{4,5},{5,4},{6,7},{7,6},{8,9},{9,8},{10,11... | collective-permute-start | bytes 202760 | tf_op jit(solution)/shard_map/ppermute | solution.py:290
  31.1 0.9 %collective-permute-done.9 = f16[8,4224]{1,0:T(8,128)(2,1)S(1)} collective-permute-done((f16[8,4224]{1,0:T(8,128)(2,1)S(1)}, f16[8,4224]{1,0:T(8,128)(2,1)S(1)}, u32[]{:S(2)}, u32[]{:S(2)}) %collective-permute-start.9) | collective-permute-done | bytes 67616 | tf_op jit(solution)/shard_map/ppermute | solution.py:290
  32.0 0.0 copy-done.1
  32.0 0.9 %score.1 = f32[8,64]{1,0:T(8,128)} custom-call(f32[8,4096]{1,0:T(8,128)S(1)} %get-tuple-element.19.sum_ref, f32[8,4224]{1,0:T(8,128)S(1)} %convert_element_type.22.got_ref, f32[8,4224]{1,0:T(8,128)S(1)} %convert_element_type.23.swapped_ref, bf16[64,4096]{1,0:T(8,128)(2,1)S(1)} %copy-done.1), custom_call_target="tpu_custom_call" | custom-call | tf_op jit(solution)/shard_map/score/pallas_call | solution.py:377
  (9 shorter events, 0.2 us)
Async XLA Ops:
  0.0 16.9 %copy-start = (f32[256,4096]{1,0:T(8,128)S(1)}, f32[256,4096]{1,0:T(8,128)}, u32[]{:S(2)}) copy-start(f32[256,4096]{1,0:T(8,128)} %refs_0_.1) | copy-start | bytes 12582916
  4.9 1.7 %collective-permute-start = (f32[512,128]{1,0:T(8,128)S(1)}, f32[512,128]{1,0:T(8,128)S(1)}, u32[]{:S(2)}, u32[]{:S(2)}) collective-permute-start(f32[512,128]{1,0:T(8,128)S(1)} %project.1.mine_ref), channel_id=1, source_target_pairs={{0,1},{1,0},{2,3},{3,2},{4,5},{5,4},{6,7},{7,6},{8,9},{9,8},{10,11... | collective-permute-start | bytes 786440 | tf_op jit(solution)/shard_map/ppermute | solution.py:290
  7.0 4.7 %collective-permute-start.1 = (f32[8,512]{1,0:T(8,128)S(1)}, f32[8,512]{1,0:T(8,128)S(1)}, u32[]{:S(2)}, u32[]{:S(2)}) collective-permute-start(f32[8,512]{1,0:T(8,128)S(1)} %gradient.1.refs_0_), channel_id=1, source_target_pairs={{4,0},{6,2},{0,4},{2,6},{12,8},{14,10},{8,12},{10,14},{9,1},{11,3}... | collective-permute-start | bytes 49160 | tf_op jit(solution)/shard_map/ppermute | solution.py:299
  11.7 1.2 %collective-permute-start.2 = (f32[8,512]{1,0:T(8,128)S(1)}, f32[8,512]{1,0:T(8,128)S(1)}, u32[]{:S(2)}, u32[]{:S(2)}) collective-permute-start(f32[8,512]{1,0:T(8,128)S(1)} %collective-permute-done.1.refs_1_), channel_id=1, source_target_pairs={{0,1},{1,0},{2,3},{3,2},{4,5},{5,4},{6,7},{7,6},{8,9},{9,8},{10,11... | collective-permute-start | bytes 49160 | tf_op jit(solution)/shard_map/ppermute | solution.py:290
  12.9 3.7 %collective-permute-start.3 = (f32[3,512]{1,0:T(4,128)S(1)}, f32[3,512]{1,0:T(4,128)S(1)}, u32[]{:S(2)}, u32[]{:S(2)}) collective-permute-start(f32[3,512]{1,0:T(4,128)S(1)} %get-tuple-element.13), channel_id=1, source_target_pairs={{2,0},{0,2},{8,4},{10,6},{4,8},{6,10},{14,12},{12,14},{9,1},{11,3}... | collective-permute-start | bytes 18440 | tf_op jit(solution)/shard_map/ppermute | solution.py:299
  16.6 1.2 %collective-permute-start.4 = (f32[3,512]{1,0:T(4,128)S(1)}, f32[3,512]{1,0:T(4,128)S(1)}, u32[]{:S(2)}, u32[]{:S(2)}) collective-permute-start(f32[3,512]{1,0:T(4,128)S(1)} %collective-permute-done.3.after_ref.token_ref.refs_1_), channel_id=1, source_target_pairs={{0,1},{1,0},{2,3},{3,2},{4,5},{5,4},{6,7},{7,6},{8,9},{9,8},{10,11... | collective-permute-start | bytes 18440 | tf_op jit(solution)/shard_map/ppermute | solution.py:290
  17.8 14.2 %copy-start.1 = (bf16[64,4096]{1,0:T(8,128)(2,1)S(1)}, bf16[64,4096]{1,0:T(8,128)(2,1)}, u32[]{:S(2)}) copy-start(bf16[64,4096]{1,0:T(8,128)(2,1)} %query_ref.1) | copy-start | bytes 1572868
  18.5 1.4 %collective-permute-start.5 = (f32[8,4224]{1,0:T(8,128)S(1)}, f32[8,4224]{1,0:T(8,128)S(1)}, u32[]{:S(2)}, u32[]{:S(2)}) collective-permute-start(f32[8,4224]{1,0:T(8,128)S(1)} %precondition.1.mine_ref), channel_id=1, source_target_pairs={{0,1},{1,0},{2,3},{3,2},{4,5},{5,4},{6,7},{7,6},{8,9},{9,8},{10,11... | collective-permute-start | bytes 405512 | tf_op jit(solution)/shard_map/ppermute | solution.py:290
  20.0 4.9 %collective-permute-start.6 = (f16[8,4224]{1,0:T(8,128)(2,1)S(1)}, f16[8,4224]{1,0:T(8,128)(2,1)S(1)}, u32[]{:S(2)}, u32[]{:S(2)}) collective-permute-start(f16[8,4224]{1,0:T(8,128)(2,1)S(1)} %convert_element_type.18), channel_id=1, source_target_pairs={{9,0},{11,2},{3,4},{1,6},{15,8},{13,10},{5,12},{7,14},{4,1},{6,3},... | collective-permute-start | bytes 202760 | tf_op jit(solution)/shard_map/ppermute | solution.py:299
  24.9 1.3 %collective-permute-start.7 = (f16[8,4224]{1,0:T(8,128)(2,1)S(1)}, f16[8,4224]{1,0:T(8,128)(2,1)S(1)}, u32[]{:S(2)}, u32[]{:S(2)}) collective-permute-start(f16[8,4224]{1,0:T(8,128)(2,1)S(1)} %collective-permute-done.6), channel_id=1, source_target_pairs={{0,1},{1,0},{2,3},{3,2},{4,5},{5,4},{6,7},{7,6},{8,9},{9,8},{10,11... | collective-permute-start | bytes 202760 | tf_op jit(solution)/shard_map/ppermute | solution.py:290
  26.2 4.3 %collective-permute-start.8 = (f16[8,4224]{1,0:T(8,128)(2,1)S(1)}, f16[8,4224]{1,0:T(8,128)(2,1)S(1)}, u32[]{:S(2)}, u32[]{:S(2)}) collective-permute-start(f16[8,4224]{1,0:T(8,128)(2,1)S(1)} %convert_element_type.21), channel_id=1, source_target_pairs={{2,0},{0,2},{8,4},{10,6},{4,8},{6,10},{14,12},{12,14},{9,1},{11,3}... | collective-permute-start | bytes 202760 | tf_op jit(solution)/shard_map/ppermute | solution.py:299
  30.6 1.4 %collective-permute-start.9 = (f16[8,4224]{1,0:T(8,128)(2,1)S(1)}, f16[8,4224]{1,0:T(8,128)(2,1)S(1)}, u32[]{:S(2)}, u32[]{:S(2)}) collective-permute-start(f16[8,4224]{1,0:T(8,128)(2,1)S(1)} %collective-permute-done.8), channel_id=1, source_target_pairs={{0,1},{1,0},{2,3},{3,2},{4,5},{5,4},{6,7},{7,6},{8,9},{9,8},{10,11... | collective-permute-start | bytes 202760 | tf_op jit(solution)/shard_map/ppermute | solution.py:290

commit v6 on v5

--- a/solution.py
+++ b/solution.py
@@ -139,7 +139,8 @@
 
 def gradient_kernel(mine_ref, other_ref, result_ref, square):
     tokens, rank = mine_ref.shape[0], square.shape[0]
-    terms = jnp.concatenate(split(mine_ref[...] + other_ref[...], 2), axis=1)
+    terms = jnp.concatenate(split(mine_ref[...] + other_ref[...]), axis=1)
+    terms = terms.astype(jnp.bfloat16)
     product = lax.dot_general(
         terms, terms, (((0,), (0,)), ((), ())), preferred_element_type=jnp.float32
     )
@@ -174,13 +175,9 @@
     )(mine, other)
 
 
-def split(value, terms):
-    parts = []
-    for _ in range(terms):
-        part = value.astype(jnp.bfloat16)
-        value = value - part.astype(jnp.float32)
-        parts.append(part)
-    return parts
+def split(value):
+    high = value.astype(jnp.bfloat16).astype(jnp.float32)
+    return high, value - high
 
 
 def pack_kernel(sources, *refs):
@@ -210,9 +207,9 @@
     for band_ref in bands:
         for start in range(0, band_ref.shape[1], BAND):
             lanes = slice(first + start, first + start + BAND)
-            high_ref[:, lanes], low_ref[:, lanes] = split(
-                band_ref[:, start : start + BAND], 2
-            )
+            high, low = split(band_ref[:, start : start + BAND])
+            high_ref[:, lanes] = high.astype(jnp.bfloat16)
+            low_ref[:, lanes] = low.astype(jnp.bfloat16)
         first += band_ref.shape[1]
 
 
@@ -246,7 +243,7 @@
     grads = jnp.concatenate(
         [held[pl.ds(slot(s), 1), :] for s in range(seqs)], axis=0
     )
-    grads = jnp.concatenate(split(grads, 2), axis=0)
+    grads = jnp.concatenate(split(grads), axis=0).astype(jnp.bfloat16)
     width = high_ref.shape[1]
     for start in range(0, width, BAND):
         lanes = slice(start, start + BAND)
@@ -355,22 +352,16 @@
     code_ref[:, width:] = power
 
 
-def score_kernel(sum_ref, got_ref, swapped_ref, query_ref, result_ref, rounded):
+def score_kernel(sum_ref, got_ref, swapped_ref, query_ref, result_ref, whole):
     width = sum_ref.shape[1]
     got_scale = jnp.exp2(got_ref[:, width:])
     swapped_scale = jnp.exp2(swapped_ref[:, width:])
     for start in range(0, width, BESIDE):
         lanes = slice(start, start + BESIDE)
         second = got_ref[:, lanes] * got_scale + swapped_ref[:, lanes] * swapped_scale
-        rounded[:, lanes] = (sum_ref[:, lanes] + second).astype(rounded.dtype)
-    step = width // 4
-    total = sum(
-        contract_last(
-            rounded[:, start : start + step], query_ref[:, start : start + step]
-        )
-        for start in range(0, width, step)
-    )
-    result_ref[...] = total * (1 / math.sqrt(width))
+        whole[:, lanes] = sum_ref[:, lanes] + second
+    scores = contract_last(whole[...].astype(query_ref.dtype), query_ref[...])
+    result_ref[...] = scores * (1 / math.sqrt(width))
 
 
 def small_kernel(kernel, name, operands, shapes, scratch=()):
@@ -407,7 +398,7 @@
         "score",
         (total, *heard_second, query_grads),
         ((seqs, query_grads.shape[0]),),
-        [pltpu.VMEM(narrow, jnp.bfloat16)],
+        [pltpu.VMEM(narrow, jnp.float32)],
     )[0]
 
 

time: 33 us -> 33 us (level)
  no operation moved by 1% of the time
where the time goes in v6:
time: 33 us; the launch traced here: 32.8 us
  waiting for transfers between devices  14.2 us (43%)
  starting transfers between devices  10.7 us (32%)
  Pallas kernels  7.73 us (23%)
    ppermute x4, waiting for transfers between devices, receive(): return lax.ppermute(value, ('dp', 'tensor'), pairs)  8.86 us
    ppermute x4, starting transfers between devices, receive(): return lax.ppermute(value, ('dp', 'tensor'), pairs)  8.81 us
    ppermute x6, waiting for transfers between devices, swap(): return lax.ppermute(value, axis, [(i, i ^ bit) for i in range(size)])  5.35 us
    pallas_call x1, Pallas kernels, project(): pl.pallas_call(project_kernel, out_shape=jax.ShapeDtypeStruct((tokens, 2...  4.93 us
    ppermute x6, starting transfers between devices, swap(): return lax.ppermute(value, axis, [(i, i ^ bit) for i in range(size)])  1.92 us
    pallas_call x3, Pallas kernels, small_kernel(): pl.pallas_call(kernel, out_shape=[jax.ShapeDtypeStruct(shape, jnp.float32...  0.93 us
    pallas_call x1, Pallas kernels, split_bands(): pl.pallas_call(split_kernel, out_shape=[jax.ShapeDtypeStruct(shape, jnp.b...  0.76 us
    pallas_call x1, Pallas kernels, precondition_rows(): pl.pallas_call(precondition_kernel, out_shape=jax.ShapeDtypeStruct((seqs,...  0.7 us
  transfers between devices with their start and end apart: 10, of which 10 were waited for; matrix products, arithmetic and copies ran while one was open for 0% of the time, Pallas kernels for 2%

profile of v6, /device:TPU:0, one launch (start us, length us, event | category | flops | bytes accessed | tf_op | source)
XLA Modules:
  0.0 32.8 jit_solution(13466524250021839913)
XLA Ops:
  0.0 0.0 copy-start
  0.0 4.9 %project.1.mine_ref = f32[512,128]{1,0:T(8,128)S(1)} custom-call(bf16[512,2048]{1,0:T(8,128)(2,1)} %layer_ref.1, bf16[512,7168]{1,0:T(8,128)(2,1)} %gate_ref.1, bf16[64,2048]{1,0:T(8,128)(2,1)} %in_ref.1, bf16[64,7168]{1,0:T(8,128)(2,1)} %out_ref.1), custom_call_target="tpu_custom_call" | custom-call | flops 603979776 | bytes 10616832 | tf_op jit(solution)/shard_map/project/pallas_call | solution.py:120
  4.9 0.5 %collective-permute-start = (f32[512,128]{1,0:T(8,128)S(1)}, f32[512,128]{1,0:T(8,128)S(1)}, u32[]{:S(2)}, u32[]{:S(2)}) collective-permute-start(f32[512,128]{1,0:T(8,128)S(1)} %project.1.mine_ref), channel_id=1, source_target_pairs={{0,1},{1,0},{2,3},{3,2},{4,5},{5,4},{6,7},{7,6},{8,9},{9,8},{10,11... | collective-permute-start | bytes 786440 | tf_op jit(solution)/shard_map/ppermute | solution.py:287
  5.5 1.2 %collective-permute-done.other_ref = f32[512,128]{1,0:T(8,128)S(1)} collective-permute-done((f32[512,128]{1,0:T(8,128)S(1)}, f32[512,128]{1,0:T(8,128)S(1)}, u32[]{:S(2)}, u32[]{:S(2)}) %collective-permute-start) | collective-permute-done | bytes 262176 | tf_op jit(solution)/shard_map/ppermute | solution.py:287
  6.6 0.4 %gradient.1.refs_0_ = f32[8,512]{1,0:T(8,128)S(1)} custom-call(f32[512,128]{1,0:T(8,128)S(1)} %project.1.mine_ref, f32[512,128]{1,0:T(8,128)S(1)} %collective-permute-done.other_ref), custom_call_target="tpu_custom_call" | custom-call | flops 4194304 | bytes 524288 | tf_op jit(solution)/shard_map/gradient/pallas_call | solution.py:162
  7.0 2.9 %collective-permute-start.1 = (f32[8,512]{1,0:T(8,128)S(1)}, f32[8,512]{1,0:T(8,128)S(1)}, u32[]{:S(2)}, u32[]{:S(2)}) collective-permute-start(f32[8,512]{1,0:T(8,128)S(1)} %gradient.1.refs_0_), channel_id=1, source_target_pairs={{4,0},{6,2},{0,4},{2,6},{12,8},{14,10},{8,12},{10,14},{9,1},{11,3}... | collective-permute-start | bytes 49160 | tf_op jit(solution)/shard_map/ppermute | solution.py:296
  10.0 1.7 %collective-permute-done.1.refs_1_ = f32[8,512]{1,0:T(8,128)S(1)} collective-permute-done((f32[8,512]{1,0:T(8,128)S(1)}, f32[8,512]{1,0:T(8,128)S(1)}, u32[]{:S(2)}, u32[]{:S(2)}) %collective-permute-start.1) | collective-permute-done | bytes 16416 | tf_op jit(solution)/shard_map/ppermute | solution.py:296
  11.7 0.3 collective-permute-start.2
  12.0 0.9 %collective-permute-done.2.refs_2_ = f32[8,512]{1,0:T(8,128)S(1)} collective-permute-done((f32[8,512]{1,0:T(8,128)S(1)}, f32[8,512]{1,0:T(8,128)S(1)}, u32[]{:S(2)}, u32[]{:S(2)}) %collective-permute-start.2) | collective-permute-done | bytes 16416 | tf_op jit(solution)/shard_map/ppermute | solution.py:287
  12.9 2.1 %collective-permute-start.3 = (f32[3,512]{1,0:T(4,128)S(1)}, f32[3,512]{1,0:T(4,128)S(1)}, u32[]{:S(2)}, u32[]{:S(2)}) collective-permute-start(f32[3,512]{1,0:T(4,128)S(1)} %get-tuple-element.13), channel_id=1, source_target_pairs={{2,0},{0,2},{8,4},{10,6},{4,8},{6,10},{14,12},{12,14},{9,1},{11,3}... | collective-permute-start | bytes 18440 | tf_op jit(solution)/shard_map/ppermute | solution.py:296
  15.0 1.6 %collective-permute-done.3.after_ref.token_ref.refs_1_ = f32[3,512]{1,0:T(4,128)S(1)} collective-permute-done((f32[3,512]{1,0:T(4,128)S(1)}, f32[3,512]{1,0:T(4,128)S(1)}, u32[]{:S(2)}, u32[]{:S(2)}) %collective-permute-start.3) | collective-permute-done | bytes 6176 | tf_op jit(solution)/shard_map/ppermute | solution.py:296
  16.6 0.3 collective-permute-start.4
  16.9 0.0 copy-done
  16.9 0.8 %split.1 = (bf16[256,4096]{1,0:T(8,128)(2,1)S(1)}, bf16[256,4096]{1,0:T(8,128)(2,1)S(1)}) custom-call(f32[3,512]{1,0:T(4,128)S(1)} %collective-permute-done.3.after_ref.token_ref.refs_1_, f32[256,4096]{1,0:T(8,128)S(1)} %copy-done), custom_call_target="tpu_custom_call" | custom-call | bytes 8388608 | tf_op jit(solution)/shard_map/split/pallas_call | solution.py:218
  17.7 0.1 collective-permute-done.4.refs_2_
  17.8 0.0 copy-start.1
  17.8 0.7 %precondition.1.mine_ref = f32[8,4224]{1,0:T(8,128)S(1)} custom-call(f32[3,512]{1,0:T(4,128)S(1)} %collective-permute-done.3.after_ref.token_ref.refs_1_, f32[3,512]{1,0:T(4,128)S(1)} %get-tuple-element.14.refs_0_, f32[3,512]{1,0:T(4,128)S(1)} %collective-permute-done.3.after_ref.token_ref.refs_1_, f32[3,512]{1,0:T(4,128)S(1)} %collective-permute-done.4.refs_2_, ...), custom_call_target="tpu_custom_call" | custom-call | flops 16777216 | bytes 4194304 | tf_op jit(solution)/shard_map/precondition/pallas_call | solution.py:264
  18.5 0.4 %collective-permute-start.5 = (f32[8,4224]{1,0:T(8,128)S(1)}, f32[8,4224]{1,0:T(8,128)S(1)}, u32[]{:S(2)}, u32[]{:S(2)}) collective-permute-start(f32[8,4224]{1,0:T(8,128)S(1)} %precondition.1.mine_ref), channel_id=1, source_target_pairs={{0,1},{1,0},{2,3},{3,2},{4,5},{5,4},{6,7},{7,6},{8,9},{9,8},{10,11... | collective-permute-start | bytes 405512 | tf_op jit(solution)/shard_map/ppermute | solution.py:287
  18.9 1.1 %collective-permute-done.5.other_ref = f32[8,4224]{1,0:T(8,128)S(1)} collective-permute-done((f32[8,4224]{1,0:T(8,128)S(1)}, f32[8,4224]{1,0:T(8,128)S(1)}, u32[]{:S(2)}, u32[]{:S(2)}) %collective-permute-start.5) | collective-permute-done | bytes 135200 | tf_op jit(solution)/shard_map/ppermute | solution.py:287
  20.0 1.8 %collective-permute-start.6 = (f16[8,4224]{1,0:T(8,128)(2,1)S(1)}, f16[8,4224]{1,0:T(8,128)(2,1)S(1)}, u32[]{:S(2)}, u32[]{:S(2)}) collective-permute-start(f16[8,4224]{1,0:T(8,128)(2,1)S(1)} %convert_element_type.18), channel_id=1, source_target_pairs={{9,0},{11,2},{3,4},{1,6},{15,8},{13,10},{5,12},{7,14},{4,1},{6,3},... | collective-permute-start | bytes 202760 | tf_op jit(solution)/shard_map/ppermute | solution.py:296
  21.8 3.1 %collective-permute-done.6 = f16[8,4224]{1,0:T(8,128)(2,1)S(1)} collective-permute-done((f16[8,4224]{1,0:T(8,128)(2,1)S(1)}, f16[8,4224]{1,0:T(8,128)(2,1)S(1)}, u32[]{:S(2)}, u32[]{:S(2)}) %collective-permute-start.6) | collective-permute-done | bytes 67616 | tf_op jit(solution)/shard_map/ppermute | solution.py:296
  24.9 0.0 collective-permute-start.7
  24.9 1.2 %collective-permute-done.7 = f16[8,4224]{1,0:T(8,128)(2,1)S(1)} collective-permute-done((f16[8,4224]{1,0:T(8,128)(2,1)S(1)}, f16[8,4224]{1,0:T(8,128)(2,1)S(1)}, u32[]{:S(2)}, u32[]{:S(2)}) %collective-permute-start.7) | collective-permute-done | bytes 67616 | tf_op jit(solution)/shard_map/ppermute | solution.py:287
  26.2 1.9 %collective-permute-start.8 = (f16[8,4224]{1,0:T(8,128)(2,1)S(1)}, f16[8,4224]{1,0:T(8,128)(2,1)S(1)}, u32[]{:S(2)}, u32[]{:S(2)}) collective-permute-start(f16[8,4224]{1,0:T(8,128)(2,1)S(1)} %convert_element_type.21), channel_id=1, source_target_pairs={{2,0},{0,2},{8,4},{10,6},{4,8},{6,10},{14,12},{12,14},{9,1},{11,3}... | collective-permute-start | bytes 202760 | tf_op jit(solution)/shard_map/ppermute | solution.py:296
  28.2 2.4 %collective-permute-done.8 = f16[8,4224]{1,0:T(8,128)(2,1)S(1)} collective-permute-done((f16[8,4224]{1,0:T(8,128)(2,1)S(1)}, f16[8,4224]{1,0:T(8,128)(2,1)S(1)}, u32[]{:S(2)}, u32[]{:S(2)}) %collective-permute-start.8) | collective-permute-done | bytes 67616 | tf_op jit(solution)/shard_map/ppermute | solution.py:296
  30.6 0.5 %collective-permute-start.9 = (f16[8,4224]{1,0:T(8,128)(2,1)S(1)}, f16[8,4224]{1,0:T(8,128)(2,1)S(1)}, u32[]{:S(2)}, u32[]{:S(2)}) collective-permute-start(f16[8,4224]{1,0:T(8,128)(2,1)S(1)} %collective-permute-done.8), channel_id=1, source_target_pairs={{0,1},{1,0},{2,3},{3,2},{4,5},{5,4},{6,7},{7,6},{8,9},{9,8},{10,11... | collective-permute-start | bytes 202760 | tf_op jit(solution)/shard_map/ppermute | solution.py:287
  31.1 0.9 %collective-permute-done.9 = f16[8,4224]{1,0:T(8,128)(2,1)S(1)} collective-permute-done((f16[8,4224]{1,0:T(8,128)(2,1)S(1)}, f16[8,4224]{1,0:T(8,128)(2,1)S(1)}, u32[]{:S(2)}, u32[]{:S(2)}) %collective-permute-start.9) | collective-permute-done | bytes 67616 | tf_op jit(solution)/shard_map/ppermute | solution.py:287
  32.0 0.0 copy-done.1
  32.0 0.9 %score.1 = f32[8,64]{1,0:T(8,128)} custom-call(f32[8,4096]{1,0:T(8,128)S(1)} %get-tuple-element.19.sum_ref, f32[8,4224]{1,0:T(8,128)S(1)} %convert_element_type.22.got_ref, f32[8,4224]{1,0:T(8,128)S(1)} %convert_element_type.23.swapped_ref, bf16[64,4096]{1,0:T(8,128)(2,1)S(1)} %copy-done.1), custom_call_target="tpu_custom_call" | custom-call | tf_op jit(solution)/shard_map/score/pallas_call | solution.py:368
  (9 shorter events, 0.2 us)
Async XLA Ops:
  0.0 16.9 %copy-start = (f32[256,4096]{1,0:T(8,128)S(1)}, f32[256,4096]{1,0:T(8,128)}, u32[]{:S(2)}) copy-start(f32[256,4096]{1,0:T(8,128)} %refs_0_.1) | copy-start | bytes 12582916
  4.9 1.7 %collective-permute-start = (f32[512,128]{1,0:T(8,128)S(1)}, f32[512,128]{1,0:T(8,128)S(1)}, u32[]{:S(2)}, u32[]{:S(2)}) collective-permute-start(f32[512,128]{1,0:T(8,128)S(1)} %project.1.mine_ref), channel_id=1, source_target_pairs={{0,1},{1,0},{2,3},{3,2},{4,5},{5,4},{6,7},{7,6},{8,9},{9,8},{10,11... | collective-permute-start | bytes 786440 | tf_op jit(solution)/shard_map/ppermute | solution.py:287
  7.0 4.7 %collective-permute-start.1 = (f32[8,512]{1,0:T(8,128)S(1)}, f32[8,512]{1,0:T(8,128)S(1)}, u32[]{:S(2)}, u32[]{:S(2)}) collective-permute-start(f32[8,512]{1,0:T(8,128)S(1)} %gradient.1.refs_0_), channel_id=1, source_target_pairs={{4,0},{6,2},{0,4},{2,6},{12,8},{14,10},{8,12},{10,14},{9,1},{11,3}... | collective-permute-start | bytes 49160 | tf_op jit(solution)/shard_map/ppermute | solution.py:296
  11.7 1.2 %collective-permute-start.2 = (f32[8,512]{1,0:T(8,128)S(1)}, f32[8,512]{1,0:T(8,128)S(1)}, u32[]{:S(2)}, u32[]{:S(2)}) collective-permute-start(f32[8,512]{1,0:T(8,128)S(1)} %collective-permute-done.1.refs_1_), channel_id=1, source_target_pairs={{0,1},{1,0},{2,3},{3,2},{4,5},{5,4},{6,7},{7,6},{8,9},{9,8},{10,11... | collective-permute-start | bytes 49160 | tf_op jit(solution)/shard_map/ppermute | solution.py:287
  12.9 3.7 %collective-permute-start.3 = (f32[3,512]{1,0:T(4,128)S(1)}, f32[3,512]{1,0:T(4,128)S(1)}, u32[]{:S(2)}, u32[]{:S(2)}) collective-permute-start(f32[3,512]{1,0:T(4,128)S(1)} %get-tuple-element.13), channel_id=1, source_target_pairs={{2,0},{0,2},{8,4},{10,6},{4,8},{6,10},{14,12},{12,14},{9,1},{11,3}... | collective-permute-start | bytes 18440 | tf_op jit(solution)/shard_map/ppermute | solution.py:296
  16.6 1.2 %collective-permute-start.4 = (f32[3,512]{1,0:T(4,128)S(1)}, f32[3,512]{1,0:T(4,128)S(1)}, u32[]{:S(2)}, u32[]{:S(2)}) collective-permute-start(f32[3,512]{1,0:T(4,128)S(1)} %collective-permute-done.3.after_ref.token_ref.refs_1_), channel_id=1, source_target_pairs={{0,1},{1,0},{2,3},{3,2},{4,5},{5,4},{6,7},{7,6},{8,9},{9,8},{10,11... | collective-permute-start | bytes 18440 | tf_op jit(solution)/shard_map/ppermute | solution.py:287
  17.8 14.2 %copy-start.1 = (bf16[64,4096]{1,0:T(8,128)(2,1)S(1)}, bf16[64,4096]{1,0:T(8,128)(2,1)}, u32[]{:S(2)}) copy-start(bf16[64,4096]{1,0:T(8,128)(2,1)} %query_ref.1) | copy-start | bytes 1572868
  18.5 1.4 %collective-permute-start.5 = (f32[8,4224]{1,0:T(8,128)S(1)}, f32[8,4224]{1,0:T(8,128)S(1)}, u32[]{:S(2)}, u32[]{:S(2)}) collective-permute-start(f32[8,4224]{1,0:T(8,128)S(1)} %precondition.1.mine_ref), channel_id=1, source_target_pairs={{0,1},{1,0},{2,3},{3,2},{4,5},{5,4},{6,7},{7,6},{8,9},{9,8},{10,11... | collective-permute-start | bytes 405512 | tf_op jit(solution)/shard_map/ppermute | solution.py:287
  20.0 4.9 %collective-permute-start.6 = (f16[8,4224]{1,0:T(8,128)(2,1)S(1)}, f16[8,4224]{1,0:T(8,128)(2,1)S(1)}, u32[]{:S(2)}, u32[]{:S(2)}) collective-permute-start(f16[8,4224]{1,0:T(8,128)(2,1)S(1)} %convert_element_type.18), channel_id=1, source_target_pairs={{9,0},{11,2},{3,4},{1,6},{15,8},{13,10},{5,12},{7,14},{4,1},{6,3},... | collective-permute-start | bytes 202760 | tf_op jit(solution)/shard_map/ppermute | solution.py:296
  24.9 1.3 %collective-permute-start.7 = (f16[8,4224]{1,0:T(8,128)(2,1)S(1)}, f16[8,4224]{1,0:T(8,128)(2,1)S(1)}, u32[]{:S(2)}, u32[]{:S(2)}) collective-permute-start(f16[8,4224]{1,0:T(8,128)(2,1)S(1)} %collective-permute-done.6), channel_id=1, source_target_pairs={{0,1},{1,0},{2,3},{3,2},{4,5},{5,4},{6,7},{7,6},{8,9},{9,8},{10,11... | collective-permute-start | bytes 202760 | tf_op jit(solution)/shard_map/ppermute | solution.py:287
  26.2 4.3 %collective-permute-start.8 = (f16[8,4224]{1,0:T(8,128)(2,1)S(1)}, f16[8,4224]{1,0:T(8,128)(2,1)S(1)}, u32[]{:S(2)}, u32[]{:S(2)}) collective-permute-start(f16[8,4224]{1,0:T(8,128)(2,1)S(1)} %convert_element_type.21), channel_id=1, source_target_pairs={{2,0},{0,2},{8,4},{10,6},{4,8},{6,10},{14,12},{12,14},{9,1},{11,3}... | collective-permute-start | bytes 202760 | tf_op jit(solution)/shard_map/ppermute | solution.py:296
  30.6 1.4 %collective-permute-start.9 = (f16[8,4224]{1,0:T(8,128)(2,1)S(1)}, f16[8,4224]{1,0:T(8,128)(2,1)S(1)}, u32[]{:S(2)}, u32[]{:S(2)}) collective-permute-start(f16[8,4224]{1,0:T(8,128)(2,1)S(1)} %collective-permute-done.8), channel_id=1, source_target_pairs={{0,1},{1,0},{2,3},{3,2},{4,5},{5,4},{6,7},{7,6},{8,9},{9,8},{10,11... | collective-permute-start | bytes 202760 | tf_op jit(solution)/shard_map/ppermute | solution.py:287

commit v7 on v6

--- a/solution.py
+++ b/solution.py
@@ -9,7 +9,7 @@
 from jax.sharding import PartitionSpec as P
 
 CHUNK = 1024
-BAND = 512
+BAND = 1024
 BESIDE = 128
 LAST = (((1,), (1,)), ((), ()))
 
@@ -434,7 +434,8 @@
             got = receive(given, sources)
             heard = [got] + ([swap(got, "tensor", 1)] if swaps else [])
             held += [row for rows in heard for row in (rows if number else [rows])]
-    matrices = split_bands([precondition], got)
+    rows, _ = lax.optimization_barrier((precondition, sides))
+    matrices = split_bands([rows], got)
 
     partial = precondition_rows(parts, got, matrices, dp_size)
 

time: 33 us -> 33 us (level)
  no operation moved by 1% of the time
where the time goes in v7:
time: 33 us; the launch traced here: 32.8 us
  waiting for transfers between devices  14.4 us (44%)
  starting transfers between devices  10.7 us (32%)
  Pallas kernels  7.55 us (23%)
    ppermute x4, waiting for transfers between devices, receive(): return lax.ppermute(value, ('dp', 'tensor'), pairs)  8.85 us
    ppermute x4, starting transfers between devices, receive(): return lax.ppermute(value, ('dp', 'tensor'), pairs)  8.82 us
    ppermute x6, waiting for transfers between devices, swap(): return lax.ppermute(value, axis, [(i, i ^ bit) for i in range(size)])  5.55 us
    pallas_call x1, Pallas kernels, project(): pl.pallas_call(project_kernel, out_shape=jax.ShapeDtypeStruct((tokens, 2...  4.93 us
    ppermute x6, starting transfers between devices, swap(): return lax.ppermute(value, axis, [(i, i ^ bit) for i in range(size)])  1.9 us
    pallas_call x3, Pallas kernels, small_kernel(): pl.pallas_call(kernel, out_shape=[jax.ShapeDtypeStruct(shape, jnp.float32...  0.93 us
    pallas_call x1, Pallas kernels, precondition_rows(): pl.pallas_call(precondition_kernel, out_shape=jax.ShapeDtypeStruct((seqs,...  0.72 us
  transfers between devices with their start and end apart: 10, of which 10 were waited for; matrix products, arithmetic and copies ran while one was open for 0% of the time, Pallas kernels for 2%

profile of v7, /device:TPU:0, one launch (start us, length us, event | category | flops | bytes accessed | tf_op | source)
XLA Modules:
  0.0 32.8 jit_solution(2841213405906303334)
XLA Ops:
  0.0 0.0 copy-start
  0.0 4.9 %project.1.mine_ref = f32[512,128]{1,0:T(8,128)S(1)} custom-call(bf16[512,2048]{1,0:T(8,128)(2,1)} %layer_ref.1, bf16[512,7168]{1,0:T(8,128)(2,1)} %gate_ref.1, bf16[64,2048]{1,0:T(8,128)(2,1)} %in_ref.1, bf16[64,7168]{1,0:T(8,128)(2,1)} %out_ref.1), custom_call_target="tpu_custom_call" | custom-call | flops 603979776 | bytes 10616832 | tf_op jit(solution)/shard_map/project/pallas_call | solution.py:120
  4.9 0.5 %collective-permute-start = (f32[512,128]{1,0:T(8,128)S(1)}, f32[512,128]{1,0:T(8,128)S(1)}, u32[]{:S(2)}, u32[]{:S(2)}) collective-permute-start(f32[512,128]{1,0:T(8,128)S(1)} %project.1.mine_ref), channel_id=1, source_target_pairs={{0,1},{1,0},{2,3},{3,2},{4,5},{5,4},{6,7},{7,6},{8,9},{9,8},{10,11... | collective-permute-start | bytes 786440 | tf_op jit(solution)/shard_map/ppermute | solution.py:287
  5.5 1.2 %collective-permute-done.other_ref = f32[512,128]{1,0:T(8,128)S(1)} collective-permute-done((f32[512,128]{1,0:T(8,128)S(1)}, f32[512,128]{1,0:T(8,128)S(1)}, u32[]{:S(2)}, u32[]{:S(2)}) %collective-permute-start) | collective-permute-done | bytes 262176 | tf_op jit(solution)/shard_map/ppermute | solution.py:287
  6.6 0.4 %gradient.1.refs_0_ = f32[8,512]{1,0:T(8,128)S(1)} custom-call(f32[512,128]{1,0:T(8,128)S(1)} %project.1.mine_ref, f32[512,128]{1,0:T(8,128)S(1)} %collective-permute-done.other_ref), custom_call_target="tpu_custom_call" | custom-call | flops 4194304 | bytes 524288 | tf_op jit(solution)/shard_map/gradient/pallas_call | solution.py:162
  7.0 2.9 %collective-permute-start.1 = (f32[8,512]{1,0:T(8,128)S(1)}, f32[8,512]{1,0:T(8,128)S(1)}, u32[]{:S(2)}, u32[]{:S(2)}) collective-permute-start(f32[8,512]{1,0:T(8,128)S(1)} %gradient.1.refs_0_), channel_id=1, source_target_pairs={{4,0},{6,2},{0,4},{2,6},{12,8},{14,10},{8,12},{10,14},{9,1},{11,3}... | collective-permute-start | bytes 49160 | tf_op jit(solution)/shard_map/ppermute | solution.py:296
  10.0 1.7 %collective-permute-done.1.refs_1_ = f32[8,512]{1,0:T(8,128)S(1)} collective-permute-done((f32[8,512]{1,0:T(8,128)S(1)}, f32[8,512]{1,0:T(8,128)S(1)}, u32[]{:S(2)}, u32[]{:S(2)}) %collective-permute-start.1) | collective-permute-done | bytes 16416 | tf_op jit(solution)/shard_map/ppermute | solution.py:296
  11.7 0.3 collective-permute-start.2
  12.0 0.9 %collective-permute-done.2.refs_2_ = f32[8,512]{1,0:T(8,128)S(1)} collective-permute-done((f32[8,512]{1,0:T(8,128)S(1)}, f32[8,512]{1,0:T(8,128)S(1)}, u32[]{:S(2)}, u32[]{:S(2)}) %collective-permute-start.2) | collective-permute-done | bytes 16416 | tf_op jit(solution)/shard_map/ppermute | solution.py:287
  12.9 2.1 %collective-permute-start.3 = (f32[3,512]{1,0:T(4,128)S(1)}, f32[3,512]{1,0:T(4,128)S(1)}, u32[]{:S(2)}, u32[]{:S(2)}) collective-permute-start(f32[3,512]{1,0:T(4,128)S(1)} %get-tuple-element.14), channel_id=1, source_target_pairs={{2,0},{0,2},{8,4},{10,6},{4,8},{6,10},{14,12},{12,14},{9,1},{11,3}... | collective-permute-start | bytes 18440 | tf_op jit(solution)/shard_map/ppermute | solution.py:296
  15.0 1.6 %collective-permute-done.3.after_ref.token_ref.refs_1_ = f32[3,512]{1,0:T(4,128)S(1)} collective-permute-done((f32[3,512]{1,0:T(4,128)S(1)}, f32[3,512]{1,0:T(4,128)S(1)}, u32[]{:S(2)}, u32[]{:S(2)}) %collective-permute-start.3) | collective-permute-done | bytes 6176 | tf_op jit(solution)/shard_map/ppermute | solution.py:296
  16.6 0.3 collective-permute-start.4
  16.9 0.0 copy-done
  16.9 0.6 %split.1 = (bf16[256,4096]{1,0:T(8,128)(2,1)S(1)}, bf16[256,4096]{1,0:T(8,128)(2,1)S(1)}) custom-call(f32[3,512]{1,0:T(4,128)S(1)} %collective-permute-done.3.after_ref.token_ref.refs_1_, f32[256,4096]{1,0:T(8,128)S(1)} %copy-done), custom_call_target="tpu_custom_call" | custom-call | bytes 8388608 | tf_op jit(solution)/shard_map/split/pallas_call | solution.py:218
  17.5 0.3 collective-permute-done.4.refs_2_
  17.8 0.0 copy-start.1
  17.8 0.7 %precondition.1.mine_ref = f32[8,4224]{1,0:T(8,128)S(1)} custom-call(f32[3,512]{1,0:T(4,128)S(1)} %collective-permute-done.3.after_ref.token_ref.refs_1_, f32[3,512]{1,0:T(4,128)S(1)} %get-tuple-element.15.refs_0_, f32[3,512]{1,0:T(4,128)S(1)} %collective-permute-done.3.after_ref.token_ref.refs_1_, f32[3,512]{1,0:T(4,128)S(1)} %collective-permute-done.4.refs_2_, ...), custom_call_target="tpu_custom_call" | custom-call | flops 16777216 | bytes 4194304 | tf_op jit(solution)/shard_map/precondition/pallas_call | solution.py:264
  18.5 0.3 %collective-permute-start.5 = (f32[8,4224]{1,0:T(8,128)S(1)}, f32[8,4224]{1,0:T(8,128)S(1)}, u32[]{:S(2)}, u32[]{:S(2)}) collective-permute-start(f32[8,4224]{1,0:T(8,128)S(1)} %precondition.1.mine_ref), channel_id=1, source_target_pairs={{0,1},{1,0},{2,3},{3,2},{4,5},{5,4},{6,7},{7,6},{8,9},{9,8},{10,11... | collective-permute-start | bytes 405512 | tf_op jit(solution)/shard_map/ppermute | solution.py:287
  18.9 1.1 %collective-permute-done.5.other_ref = f32[8,4224]{1,0:T(8,128)S(1)} collective-permute-done((f32[8,4224]{1,0:T(8,128)S(1)}, f32[8,4224]{1,0:T(8,128)S(1)}, u32[]{:S(2)}, u32[]{:S(2)}) %collective-permute-start.5) | collective-permute-done | bytes 135200 | tf_op jit(solution)/shard_map/ppermute | solution.py:287
  20.0 1.8 %collective-permute-start.6 = (f16[8,4224]{1,0:T(8,128)(2,1)S(1)}, f16[8,4224]{1,0:T(8,128)(2,1)S(1)}, u32[]{:S(2)}, u32[]{:S(2)}) collective-permute-start(f16[8,4224]{1,0:T(8,128)(2,1)S(1)} %convert_element_type.18), channel_id=1, source_target_pairs={{9,0},{11,2},{3,4},{1,6},{15,8},{13,10},{5,12},{7,14},{4,1},{6,3},... | collective-permute-start | bytes 202760 | tf_op jit(solution)/shard_map/ppermute | solution.py:296
  21.8 3.1 %collective-permute-done.6 = f16[8,4224]{1,0:T(8,128)(2,1)S(1)} collective-permute-done((f16[8,4224]{1,0:T(8,128)(2,1)S(1)}, f16[8,4224]{1,0:T(8,128)(2,1)S(1)}, u32[]{:S(2)}, u32[]{:S(2)}) %collective-permute-start.6) | collective-permute-done | bytes 67616 | tf_op jit(solution)/shard_map/ppermute | solution.py:296
  24.9 0.0 collective-permute-start.7
  24.9 1.2 %collective-permute-done.7 = f16[8,4224]{1,0:T(8,128)(2,1)S(1)} collective-permute-done((f16[8,4224]{1,0:T(8,128)(2,1)S(1)}, f16[8,4224]{1,0:T(8,128)(2,1)S(1)}, u32[]{:S(2)}, u32[]{:S(2)}) %collective-permute-start.7) | collective-permute-done | bytes 67616 | tf_op jit(solution)/shard_map/ppermute | solution.py:287
  26.2 1.9 %collective-permute-start.8 = (f16[8,4224]{1,0:T(8,128)(2,1)S(1)}, f16[8,4224]{1,0:T(8,128)(2,1)S(1)}, u32[]{:S(2)}, u32[]{:S(2)}) collective-permute-start(f16[8,4224]{1,0:T(8,128)(2,1)S(1)} %convert_element_type.21), channel_id=1, source_target_pairs={{2,0},{0,2},{8,4},{10,6},{4,8},{6,10},{14,12},{12,14},{9,1},{11,3}... | collective-permute-start | bytes 202760 | tf_op jit(solution)/shard_map/ppermute | solution.py:296
  28.2 2.4 %collective-permute-done.8 = f16[8,4224]{1,0:T(8,128)(2,1)S(1)} collective-permute-done((f16[8,4224]{1,0:T(8,128)(2,1)S(1)}, f16[8,4224]{1,0:T(8,128)(2,1)S(1)}, u32[]{:S(2)}, u32[]{:S(2)}) %collective-permute-start.8) | collective-permute-done | bytes 67616 | tf_op jit(solution)/shard_map/ppermute | solution.py:296
  30.6 0.5 %collective-permute-start.9 = (f16[8,4224]{1,0:T(8,128)(2,1)S(1)}, f16[8,4224]{1,0:T(8,128)(2,1)S(1)}, u32[]{:S(2)}, u32[]{:S(2)}) collective-permute-start(f16[8,4224]{1,0:T(8,128)(2,1)S(1)} %collective-permute-done.8), channel_id=1, source_target_pairs={{0,1},{1,0},{2,3},{3,2},{4,5},{5,4},{6,7},{7,6},{8,9},{9,8},{10,11... | collective-permute-start | bytes 202760 | tf_op jit(solution)/shard_map/ppermute | solution.py:287
  31.1 0.9 %collective-permute-done.9 = f16[8,4224]{1,0:T(8,128)(2,1)S(1)} collective-permute-done((f16[8,4224]{1,0:T(8,128)(2,1)S(1)}, f16[8,4224]{1,0:T(8,128)(2,1)S(1)}, u32[]{:S(2)}, u32[]{:S(2)}) %collective-permute-start.9) | collective-permute-done | bytes 67616 | tf_op jit(solution)/shard_map/ppermute | solution.py:287
  32.0 0.0 copy-done.1
  32.0 0.9 %score.1 = f32[8,64]{1,0:T(8,128)} custom-call(f32[8,4096]{1,0:T(8,128)S(1)} %get-tuple-element.21.sum_ref, f32[8,4224]{1,0:T(8,128)S(1)} %convert_element_type.22.got_ref, f32[8,4224]{1,0:T(8,128)S(1)} %convert_element_type.23.swapped_ref, bf16[64,4096]{1,0:T(8,128)(2,1)S(1)} %copy-done.1), custom_call_target="tpu_custom_call" | custom-call | tf_op jit(solution)/shard_map/score/pallas_call | solution.py:368
  (9 shorter events, 0.2 us)
Async XLA Ops:
  0.0 16.9 %copy-start = (f32[256,4096]{1,0:T(8,128)S(1)}, f32[256,4096]{1,0:T(8,128)}, u32[]{:S(2)}) copy-start(f32[256,4096]{1,0:T(8,128)} %refs_0_) | copy-start | bytes 12582916
  4.9 1.7 %collective-permute-start = (f32[512,128]{1,0:T(8,128)S(1)}, f32[512,128]{1,0:T(8,128)S(1)}, u32[]{:S(2)}, u32[]{:S(2)}) collective-permute-start(f32[512,128]{1,0:T(8,128)S(1)} %project.1.mine_ref), channel_id=1, source_target_pairs={{0,1},{1,0},{2,3},{3,2},{4,5},{5,4},{6,7},{7,6},{8,9},{9,8},{10,11... | collective-permute-start | bytes 786440 | tf_op jit(solution)/shard_map/ppermute | solution.py:287
  7.0 4.7 %collective-permute-start.1 = (f32[8,512]{1,0:T(8,128)S(1)}, f32[8,512]{1,0:T(8,128)S(1)}, u32[]{:S(2)}, u32[]{:S(2)}) collective-permute-start(f32[8,512]{1,0:T(8,128)S(1)} %gradient.1.refs_0_), channel_id=1, source_target_pairs={{4,0},{6,2},{0,4},{2,6},{12,8},{14,10},{8,12},{10,14},{9,1},{11,3}... | collective-permute-start | bytes 49160 | tf_op jit(solution)/shard_map/ppermute | solution.py:296
  11.7 1.2 %collective-permute-start.2 = (f32[8,512]{1,0:T(8,128)S(1)}, f32[8,512]{1,0:T(8,128)S(1)}, u32[]{:S(2)}, u32[]{:S(2)}) collective-permute-start(f32[8,512]{1,0:T(8,128)S(1)} %collective-permute-done.1.refs_1_), channel_id=1, source_target_pairs={{0,1},{1,0},{2,3},{3,2},{4,5},{5,4},{6,7},{7,6},{8,9},{9,8},{10,11... | collective-permute-start | bytes 49160 | tf_op jit(solution)/shard_map/ppermute | solution.py:287
  12.9 3.7 %collective-permute-start.3 = (f32[3,512]{1,0:T(4,128)S(1)}, f32[3,512]{1,0:T(4,128)S(1)}, u32[]{:S(2)}, u32[]{:S(2)}) collective-permute-start(f32[3,512]{1,0:T(4,128)S(1)} %get-tuple-element.14), channel_id=1, source_target_pairs={{2,0},{0,2},{8,4},{10,6},{4,8},{6,10},{14,12},{12,14},{9,1},{11,3}... | collective-permute-start | bytes 18440 | tf_op jit(solution)/shard_map/ppermute | solution.py:296
  16.6 1.2 %collective-permute-start.4 = (f32[3,512]{1,0:T(4,128)S(1)}, f32[3,512]{1,0:T(4,128)S(1)}, u32[]{:S(2)}, u32[]{:S(2)}) collective-permute-start(f32[3,512]{1,0:T(4,128)S(1)} %collective-permute-done.3.after_ref.token_ref.refs_1_), channel_id=1, source_target_pairs={{0,1},{1,0},{2,3},{3,2},{4,5},{5,4},{6,7},{7,6},{8,9},{9,8},{10,11... | collective-permute-start | bytes 18440 | tf_op jit(solution)/shard_map/ppermute | solution.py:287
  17.8 14.2 %copy-start.1 = (bf16[64,4096]{1,0:T(8,128)(2,1)S(1)}, bf16[64,4096]{1,0:T(8,128)(2,1)}, u32[]{:S(2)}) copy-start(bf16[64,4096]{1,0:T(8,128)(2,1)} %query_ref.1) | copy-start | bytes 1572868
  18.5 1.4 %collective-permute-start.5 = (f32[8,4224]{1,0:T(8,128)S(1)}, f32[8,4224]{1,0:T(8,128)S(1)}, u32[]{:S(2)}, u32[]{:S(2)}) collective-permute-start(f32[8,4224]{1,0:T(8,128)S(1)} %precondition.1.mine_ref), channel_id=1, source_target_pairs={{0,1},{1,0},{2,3},{3,2},{4,5},{5,4},{6,7},{7,6},{8,9},{9,8},{10,11... | collective-permute-start | bytes 405512 | tf_op jit(solution)/shard_map/ppermute | solution.py:287
  20.0 4.9 %collective-permute-start.6 = (f16[8,4224]{1,0:T(8,128)(2,1)S(1)}, f16[8,4224]{1,0:T(8,128)(2,1)S(1)}, u32[]{:S(2)}, u32[]{:S(2)}) collective-permute-start(f16[8,4224]{1,0:T(8,128)(2,1)S(1)} %convert_element_type.18), channel_id=1, source_target_pairs={{9,0},{11,2},{3,4},{1,6},{15,8},{13,10},{5,12},{7,14},{4,1},{6,3},... | collective-permute-start | bytes 202760 | tf_op jit(solution)/shard_map/ppermute | solution.py:296
  24.9 1.3 %collective-permute-start.7 = (f16[8,4224]{1,0:T(8,128)(2,1)S(1)}, f16[8,4224]{1,0:T(8,128)(2,1)S(1)}, u32[]{:S(2)}, u32[]{:S(2)}) collective-permute-start(f16[8,4224]{1,0:T(8,128)(2,1)S(1)} %collective-permute-done.6), channel_id=1, source_target_pairs={{0,1},{1,0},{2,3},{3,2},{4,5},{5,4},{6,7},{7,6},{8,9},{9,8},{10,11... | collective-permute-start | bytes 202760 | tf_op jit(solution)/shard_map/ppermute | solution.py:287
  26.2 4.3 %collective-permute-start.8 = (f16[8,4224]{1,0:T(8,128)(2,1)S(1)}, f16[8,4224]{1,0:T(8,128)(2,1)S(1)}, u32[]{:S(2)}, u32[]{:S(2)}) collective-permute-start(f16[8,4224]{1,0:T(8,128)(2,1)S(1)} %convert_element_type.21), channel_id=1, source_target_pairs={{2,0},{0,2},{8,4},{10,6},{4,8},{6,10},{14,12},{12,14},{9,1},{11,3}... | collective-permute-start | bytes 202760 | tf_op jit(solution)/shard_map/ppermute | solution.py:296
  30.6 1.4 %collective-permute-start.9 = (f16[8,4224]{1,0:T(8,128)(2,1)S(1)}, f16[8,4224]{1,0:T(8,128)(2,1)S(1)}, u32[]{:S(2)}, u32[]{:S(2)}) collective-permute-start(f16[8,4224]{1,0:T(8,128)(2,1)S(1)} %collective-permute-done.8), channel_id=1, source_target_pairs={{0,1},{1,0},{2,3},{3,2},{4,5},{5,4},{6,7},{7,6},{8,9},{9,8},{10,11... | collective-permute-start | bytes 202760 | tf_op jit(solution)/shard_map/ppermute | solution.py:287

commit v8 on v7

--- a/solution.py
+++ b/solution.py
@@ -58,6 +58,18 @@
         return dp ^ sources[0][0]
     words = [packed([row.index(i) for i in range(size)], 3) for row in sources]
     return unpacked(jnp.where(core == 0, words[0], words[1]), dp, 3)
+
+
+def first_targets(core, dp):
+    first, second = ROUNDS_OF_8
+    lists = []
+    for row in first:
+        targets = [row.index(i) for i in range(8)]
+        lists.append([targets] + [[s.index(i) for i in targets] for s in second])
+    return [
+        unpacked(jnp.where(core == 0, packed(own, 3), packed(other, 3)), dp, 3)
+        for own, other in zip(*lists)
+    ]
 
 
 def gather_slot(size):
@@ -137,7 +149,8 @@
     )(layer_input, gate_grad, factor_in, factor_out)
 
 
-def gradient_kernel(mine_ref, other_ref, result_ref, square):
+def gradient_kernel(mine_ref, other_ref, result_ref, *refs):
+    *given_refs, square = refs
     tokens, rank = mine_ref.shape[0], square.shape[0]
     terms = jnp.concatenate(split(mine_ref[...] + other_ref[...]), axis=1)
     terms = terms.astype(jnp.bfloat16)
@@ -155,15 +168,23 @@
     each = rank // rows
     for k in range(each):
         result_ref[:, k * rank : (k + 1) * rank] = square[pl.ds(k, rows, each), :]
+    for given_ref in given_refs:
+        chips = first_targets(lax.axis_index("tensor"), lax.axis_index("dp"))
+        for row, chip in enumerate(chips):
+            given_ref[row : row + 1] = result_ref[pl.ds(chip, 1), :]
 
 
 def gradient_rows(mine, other, rows):
     tokens, rank = mine.shape[0], mine.shape[1] // 2
+    counts = (rows, 3) if rows == 8 else (rows,)
     return pl.pallas_call(
         gradient_kernel,
-        out_shape=jax.ShapeDtypeStruct((rows, rank * rank // rows), jnp.float32),
+        out_shape=[
+            jax.ShapeDtypeStruct((count, rank * rank // rows), jnp.float32)
+            for count in counts
+        ],
         in_specs=[pl.BlockSpec(memory_space=pltpu.VMEM)] * 2,
-        out_specs=pl.BlockSpec(memory_space=pltpu.VMEM),
+        out_specs=[pl.BlockSpec(memory_space=pltpu.VMEM)] * len(counts),
         scratch_shapes=[pltpu.VMEM((rank, rank), jnp.float32)],
         compiler_params=pltpu.CompilerParams(vmem_limit_bytes=16 << 20),
         cost_estimate=pl.CostEstimate(
@@ -185,8 +206,9 @@
     core, dp = lax.axis_index("tensor"), lax.axis_index("dp")
     target = gather_target(sources, core, dp)
     for row, ref in enumerate(held_refs):
-        given_ref[row : row + 1] = ref[pl.ds(target, 1), :]
-        kept_ref[row : row + 1] = ref[pl.ds(dp, 1), :]
+        some = ref.shape[0] < len(sources[0])
+        given_ref[row : row + 1] = ref[pl.ds(1 + core if some else target, 1), :]
+        kept_ref[row : row + 1] = ref[pl.ds(0 if some else dp, 1), :]
 
 
 def pack(held, sources):
@@ -420,7 +442,7 @@
 
     sides = project(layer_input, gate_grad, factor_in, factor_out)
     other = swap(sides, "tensor", 1)
-    gradient = gradient_rows(sides, other, dp_size)
+    gradient, *firsts = gradient_rows(sides, other, dp_size)
 
     held = [gradient]
     rounds = gather_rounds(dp_size)
@@ -430,7 +452,7 @@
             got = receive(given, sources)
             parts = [kept, got] + ([swap(got, "tensor", 1)] if swaps else [])
         else:
-            given = held[0] if number == 0 else jnp.stack(held)
+            given = (*firsts, *held)[0] if number == 0 else jnp.stack(held)
             got = receive(given, sources)
             heard = [got] + ([swap(got, "tensor", 1)] if swaps else [])
             held += [row for rows in heard for row in (rows if number else [rows])]

time: 33 us -> 32.8 us (level)
  no operation moved by 1% of the time
where the time goes in v8:
time: 32.8 us; the launch traced here: 32.7 us
  waiting for transfers between devices  14.4 us (44%)
  starting transfers between devices  10.5 us (32%)
  Pallas kernels  7.56 us (23%)
    ppermute x4, waiting for transfers between devices, receive(): return lax.ppermute(value, ('dp', 'tensor'), pairs)  8.92 us
    ppermute x4, starting transfers between devices, receive(): return lax.ppermute(value, ('dp', 'tensor'), pairs)  8.59 us
    ppermute x6, waiting for transfers between devices, swap(): return lax.ppermute(value, axis, [(i, i ^ bit) for i in range(size)])  5.51 us
    pallas_call x1, Pallas kernels, project(): pl.pallas_call(project_kernel, out_shape=jax.ShapeDtypeStruct((tokens, 2...  4.93 us
    ppermute x6, starting transfers between devices, swap(): return lax.ppermute(value, axis, [(i, i ^ bit) for i in range(size)])  1.94 us
    pallas_call x3, Pallas kernels, small_kernel(): pl.pallas_call(kernel, out_shape=[jax.ShapeDtypeStruct(shape, jnp.float32...  0.93 us
    pallas_call x1, Pallas kernels, precondition_rows(): pl.pallas_call(precondition_kernel, out_shape=jax.ShapeDtypeStruct((seqs,...  0.72 us
  transfers between devices with their start and end apart: 10, of which 10 were waited for; matrix products, arithmetic and copies ran while one was open for 0% of the time, Pallas kernels for 2%

profile of v8, /device:TPU:0, one launch (start us, length us, event | category | flops | bytes accessed | tf_op | source)
XLA Modules:
  0.0 32.7 jit_solution(15526351454769976381)
XLA Ops:
  0.0 0.0 copy-start
  0.0 4.9 %project.1.mine_ref = f32[512,128]{1,0:T(8,128)S(1)} custom-call(bf16[512,2048]{1,0:T(8,128)(2,1)} %layer_ref.1, bf16[512,7168]{1,0:T(8,128)(2,1)} %gate_ref.1, bf16[64,2048]{1,0:T(8,128)(2,1)} %in_ref.1, bf16[64,7168]{1,0:T(8,128)(2,1)} %out_ref.1), custom_call_target="tpu_custom_call" | custom-call | flops 603979776 | bytes 10616832 | tf_op jit(solution)/shard_map/project/pallas_call | solution.py:132
  4.9 0.5 %collective-permute-start = (f32[512,128]{1,0:T(8,128)S(1)}, f32[512,128]{1,0:T(8,128)S(1)}, u32[]{:S(2)}, u32[]{:S(2)}) collective-permute-start(f32[512,128]{1,0:T(8,128)S(1)} %project.1.mine_ref), channel_id=1, source_target_pairs={{0,1},{1,0},{2,3},{3,2},{4,5},{5,4},{6,7},{7,6},{8,9},{9,8},{10,11... | collective-permute-start | bytes 786440 | tf_op jit(solution)/shard_map/ppermute | solution.py:309
  5.5 1.2 %collective-permute-done.other_ref = f32[512,128]{1,0:T(8,128)S(1)} collective-permute-done((f32[512,128]{1,0:T(8,128)S(1)}, f32[512,128]{1,0:T(8,128)S(1)}, u32[]{:S(2)}, u32[]{:S(2)}) %collective-permute-start) | collective-permute-done | bytes 262176 | tf_op jit(solution)/shard_map/ppermute | solution.py:309
  6.6 0.4 %gradient.1 = (f32[8,512]{1,0:T(8,128)S(1)}, f32[3,512]{1,0:T(4,128)S(1)}) custom-call(f32[512,128]{1,0:T(8,128)S(1)} %project.1.mine_ref, f32[512,128]{1,0:T(8,128)S(1)} %collective-permute-done.other_ref), custom_call_target="tpu_custom_call" | custom-call | flops 4194304 | bytes 524288 | tf_op jit(solution)/shard_map/gradient/pallas_call | solution.py:180
  7.0 2.9 %collective-permute-start.1 = (f32[3,512]{1,0:T(4,128)S(1)}, f32[3,512]{1,0:T(4,128)S(1)}, u32[]{:S(2)}, u32[]{:S(2)}) collective-permute-start(f32[3,512]{1,0:T(4,128)S(1)} %get-tuple-element.17), channel_id=1, source_target_pairs={{4,0},{6,2},{0,4},{2,6},{12,8},{14,10},{8,12},{10,14},{9,1},{11,3}... | collective-permute-start | bytes 18440 | tf_op jit(solution)/shard_map/ppermute | solution.py:318
  10.0 1.6 %collective-permute-done.1.refs_1_ = f32[3,512]{1,0:T(4,128)S(1)} collective-permute-done((f32[3,512]{1,0:T(4,128)S(1)}, f32[3,512]{1,0:T(4,128)S(1)}, u32[]{:S(2)}, u32[]{:S(2)}) %collective-permute-start.1) | collective-permute-done | bytes 6176 | tf_op jit(solution)/shard_map/ppermute | solution.py:318
  11.6 0.3 collective-permute-start.2
  11.9 0.9 %collective-permute-done.2.refs_2_ = f32[3,512]{1,0:T(4,128)S(1)} collective-permute-done((f32[3,512]{1,0:T(4,128)S(1)}, f32[3,512]{1,0:T(4,128)S(1)}, u32[]{:S(2)}, u32[]{:S(2)}) %collective-permute-start.2) | collective-permute-done | bytes 6176 | tf_op jit(solution)/shard_map/ppermute | solution.py:309
  12.8 2.0 %collective-permute-start.3 = (f32[3,512]{1,0:T(4,128)S(1)}, f32[3,512]{1,0:T(4,128)S(1)}, u32[]{:S(2)}, u32[]{:S(2)}) collective-permute-start(f32[3,512]{1,0:T(4,128)S(1)} %get-tuple-element.18), channel_id=1, source_target_pairs={{2,0},{0,2},{8,4},{10,6},{4,8},{6,10},{14,12},{12,14},{9,1},{11,3}... | collective-permute-start | bytes 18440 | tf_op jit(solution)/shard_map/ppermute | solution.py:318
  14.7 1.7 %collective-permute-done.3.after_ref.token_ref.refs_1_ = f32[3,512]{1,0:T(4,128)S(1)} collective-permute-done((f32[3,512]{1,0:T(4,128)S(1)}, f32[3,512]{1,0:T(4,128)S(1)}, u32[]{:S(2)}, u32[]{:S(2)}) %collective-permute-start.3) | collective-permute-done | bytes 6176 | tf_op jit(solution)/shard_map/ppermute | solution.py:318
  16.4 0.3 collective-permute-start.4
  16.8 0.0 copy-done
  16.8 0.6 %split.1 = (bf16[256,4096]{1,0:T(8,128)(2,1)S(1)}, bf16[256,4096]{1,0:T(8,128)(2,1)S(1)}) custom-call(f32[3,512]{1,0:T(4,128)S(1)} %collective-permute-done.3.after_ref.token_ref.refs_1_, f32[256,4096]{1,0:T(8,128)S(1)} %copy-done), custom_call_target="tpu_custom_call" | custom-call | bytes 8388608 | tf_op jit(solution)/shard_map/split/pallas_call | solution.py:240
  17.3 0.3 collective-permute-done.4.refs_2_
  17.6 0.0 copy-start.1
  17.6 0.7 %precondition.1.mine_ref = f32[8,4224]{1,0:T(8,128)S(1)} custom-call(f32[3,512]{1,0:T(4,128)S(1)} %collective-permute-done.3.after_ref.token_ref.refs_1_, f32[3,512]{1,0:T(4,128)S(1)} %get-tuple-element.19.refs_0_, f32[3,512]{1,0:T(4,128)S(1)} %collective-permute-done.3.after_ref.token_ref.refs_1_, f32[3,512]{1,0:T(4,128)S(1)} %collective-permute-done.4.refs_2_, ...), custom_call_target="tpu_custom_call" | custom-call | flops 16777216 | bytes 4194304 | tf_op jit(solution)/shard_map/precondition/pallas_call | solution.py:286
  18.3 0.3 %collective-permute-start.5 = (f32[8,4224]{1,0:T(8,128)S(1)}, f32[8,4224]{1,0:T(8,128)S(1)}, u32[]{:S(2)}, u32[]{:S(2)}) collective-permute-start(f32[8,4224]{1,0:T(8,128)S(1)} %precondition.1.mine_ref), channel_id=1, source_target_pairs={{0,1},{1,0},{2,3},{3,2},{4,5},{5,4},{6,7},{7,6},{8,9},{9,8},{10,11... | collective-permute-start | bytes 405512 | tf_op jit(solution)/shard_map/ppermute | solution.py:309
  18.7 1.0 %collective-permute-done.5.other_ref = f32[8,4224]{1,0:T(8,128)S(1)} collective-permute-done((f32[8,4224]{1,0:T(8,128)S(1)}, f32[8,4224]{1,0:T(8,128)S(1)}, u32[]{:S(2)}, u32[]{:S(2)}) %collective-permute-start.5) | collective-permute-done | bytes 135200 | tf_op jit(solution)/shard_map/ppermute | solution.py:309
  19.8 1.8 %collective-permute-start.6 = (f16[8,4224]{1,0:T(8,128)(2,1)S(1)}, f16[8,4224]{1,0:T(8,128)(2,1)S(1)}, u32[]{:S(2)}, u32[]{:S(2)}) collective-permute-start(f16[8,4224]{1,0:T(8,128)(2,1)S(1)} %convert_element_type.18), channel_id=1, source_target_pairs={{9,0},{11,2},{3,4},{1,6},{15,8},{13,10},{5,12},{7,14},{4,1},{6,3},... | collective-permute-start | bytes 202760 | tf_op jit(solution)/shard_map/ppermute | solution.py:318
  21.6 3.1 %collective-permute-done.6 = f16[8,4224]{1,0:T(8,128)(2,1)S(1)} collective-permute-done((f16[8,4224]{1,0:T(8,128)(2,1)S(1)}, f16[8,4224]{1,0:T(8,128)(2,1)S(1)}, u32[]{:S(2)}, u32[]{:S(2)}) %collective-permute-start.6) | collective-permute-done | bytes 67616 | tf_op jit(solution)/shard_map/ppermute | solution.py:318
  24.7 0.0 collective-permute-start.7
  24.7 1.2 %collective-permute-done.7 = f16[8,4224]{1,0:T(8,128)(2,1)S(1)} collective-permute-done((f16[8,4224]{1,0:T(8,128)(2,1)S(1)}, f16[8,4224]{1,0:T(8,128)(2,1)S(1)}, u32[]{:S(2)}, u32[]{:S(2)}) %collective-permute-start.7) | collective-permute-done | bytes 67616 | tf_op jit(solution)/shard_map/ppermute | solution.py:309
  26.1 1.8 %collective-permute-start.8 = (f16[8,4224]{1,0:T(8,128)(2,1)S(1)}, f16[8,4224]{1,0:T(8,128)(2,1)S(1)}, u32[]{:S(2)}, u32[]{:S(2)}) collective-permute-start(f16[8,4224]{1,0:T(8,128)(2,1)S(1)} %convert_element_type.21), channel_id=1, source_target_pairs={{2,0},{0,2},{8,4},{10,6},{4,8},{6,10},{14,12},{12,14},{9,1},{11,3}... | collective-permute-start | bytes 202760 | tf_op jit(solution)/shard_map/ppermute | solution.py:318
  27.9 2.5 %collective-permute-done.8 = f16[8,4224]{1,0:T(8,128)(2,1)S(1)} collective-permute-done((f16[8,4224]{1,0:T(8,128)(2,1)S(1)}, f16[8,4224]{1,0:T(8,128)(2,1)S(1)}, u32[]{:S(2)}, u32[]{:S(2)}) %collective-permute-start.8) | collective-permute-done | bytes 67616 | tf_op jit(solution)/shard_map/ppermute | solution.py:318
  30.4 0.5 %collective-permute-start.9 = (f16[8,4224]{1,0:T(8,128)(2,1)S(1)}, f16[8,4224]{1,0:T(8,128)(2,1)S(1)}, u32[]{:S(2)}, u32[]{:S(2)}) collective-permute-start(f16[8,4224]{1,0:T(8,128)(2,1)S(1)} %collective-permute-done.8), channel_id=1, source_target_pairs={{0,1},{1,0},{2,3},{3,2},{4,5},{5,4},{6,7},{7,6},{8,9},{9,8},{10,11... | collective-permute-start | bytes 202760 | tf_op jit(solution)/shard_map/ppermute | solution.py:309
  30.9 0.9 %collective-permute-done.9 = f16[8,4224]{1,0:T(8,128)(2,1)S(1)} collective-permute-done((f16[8,4224]{1,0:T(8,128)(2,1)S(1)}, f16[8,4224]{1,0:T(8,128)(2,1)S(1)}, u32[]{:S(2)}, u32[]{:S(2)}) %collective-permute-start.9) | collective-permute-done | bytes 67616 | tf_op jit(solution)/shard_map/ppermute | solution.py:309
  31.8 0.0 copy-done.1
  31.8 0.9 %score.1 = f32[8,64]{1,0:T(8,128)} custom-call(f32[8,4096]{1,0:T(8,128)S(1)} %get-tuple-element.25.sum_ref, f32[8,4224]{1,0:T(8,128)S(1)} %convert_element_type.22.got_ref, f32[8,4224]{1,0:T(8,128)S(1)} %convert_element_type.23.swapped_ref, bf16[64,4096]{1,0:T(8,128)(2,1)S(1)} %copy-done.1), custom_call_target="tpu_custom_call" | custom-call | tf_op jit(solution)/shard_map/score/pallas_call | solution.py:390
  (9 shorter events, 0.2 us)
Async XLA Ops:
  0.0 16.8 %copy-start = (f32[256,4096]{1,0:T(8,128)S(1)}, f32[256,4096]{1,0:T(8,128)}, u32[]{:S(2)}) copy-start(f32[256,4096]{1,0:T(8,128)} %refs_0_) | copy-start | bytes 12582916
  4.9 1.7 %collective-permute-start = (f32[512,128]{1,0:T(8,128)S(1)}, f32[512,128]{1,0:T(8,128)S(1)}, u32[]{:S(2)}, u32[]{:S(2)}) collective-permute-start(f32[512,128]{1,0:T(8,128)S(1)} %project.1.mine_ref), channel_id=1, source_target_pairs={{0,1},{1,0},{2,3},{3,2},{4,5},{5,4},{6,7},{7,6},{8,9},{9,8},{10,11... | collective-permute-start | bytes 786440 | tf_op jit(solution)/shard_map/ppermute | solution.py:309
  7.0 4.6 %collective-permute-start.1 = (f32[3,512]{1,0:T(4,128)S(1)}, f32[3,512]{1,0:T(4,128)S(1)}, u32[]{:S(2)}, u32[]{:S(2)}) collective-permute-start(f32[3,512]{1,0:T(4,128)S(1)} %get-tuple-element.17), channel_id=1, source_target_pairs={{4,0},{6,2},{0,4},{2,6},{12,8},{14,10},{8,12},{10,14},{9,1},{11,3}... | collective-permute-start | bytes 18440 | tf_op jit(solution)/shard_map/ppermute | solution.py:318
  11.6 1.2 %collective-permute-start.2 = (f32[3,512]{1,0:T(4,128)S(1)}, f32[3,512]{1,0:T(4,128)S(1)}, u32[]{:S(2)}, u32[]{:S(2)}) collective-permute-start(f32[3,512]{1,0:T(4,128)S(1)} %collective-permute-done.1.refs_1_), channel_id=1, source_target_pairs={{0,1},{1,0},{2,3},{3,2},{4,5},{5,4},{6,7},{7,6},{8,9},{9,8},{10,11... | collective-permute-start | bytes 18440 | tf_op jit(solution)/shard_map/ppermute | solution.py:309
  12.8 3.7 %collective-permute-start.3 = (f32[3,512]{1,0:T(4,128)S(1)}, f32[3,512]{1,0:T(4,128)S(1)}, u32[]{:S(2)}, u32[]{:S(2)}) collective-permute-start(f32[3,512]{1,0:T(4,128)S(1)} %get-tuple-element.18), channel_id=1, source_target_pairs={{2,0},{0,2},{8,4},{10,6},{4,8},{6,10},{14,12},{12,14},{9,1},{11,3}... | collective-permute-start | bytes 18440 | tf_op jit(solution)/shard_map/ppermute | solution.py:318
  16.4 1.2 %collective-permute-start.4 = (f32[3,512]{1,0:T(4,128)S(1)}, f32[3,512]{1,0:T(4,128)S(1)}, u32[]{:S(2)}, u32[]{:S(2)}) collective-permute-start(f32[3,512]{1,0:T(4,128)S(1)} %collective-permute-done.3.after_ref.token_ref.refs_1_), channel_id=1, source_target_pairs={{0,1},{1,0},{2,3},{3,2},{4,5},{5,4},{6,7},{7,6},{8,9},{9,8},{10,11... | collective-permute-start | bytes 18440 | tf_op jit(solution)/shard_map/ppermute | solution.py:309
  17.6 14.2 %copy-start.1 = (bf16[64,4096]{1,0:T(8,128)(2,1)S(1)}, bf16[64,4096]{1,0:T(8,128)(2,1)}, u32[]{:S(2)}) copy-start(bf16[64,4096]{1,0:T(8,128)(2,1)} %query_ref.1) | copy-start | bytes 1572868
  18.3 1.4 %collective-permute-start.5 = (f32[8,4224]{1,0:T(8,128)S(1)}, f32[8,4224]{1,0:T(8,128)S(1)}, u32[]{:S(2)}, u32[]{:S(2)}) collective-permute-start(f32[8,4224]{1,0:T(8,128)S(1)} %precondition.1.mine_ref), channel_id=1, source_target_pairs={{0,1},{1,0},{2,3},{3,2},{4,5},{5,4},{6,7},{7,6},{8,9},{9,8},{10,11... | collective-permute-start | bytes 405512 | tf_op jit(solution)/shard_map/ppermute | solution.py:309
  19.8 4.9 %collective-permute-start.6 = (f16[8,4224]{1,0:T(8,128)(2,1)S(1)}, f16[8,4224]{1,0:T(8,128)(2,1)S(1)}, u32[]{:S(2)}, u32[]{:S(2)}) collective-permute-start(f16[8,4224]{1,0:T(8,128)(2,1)S(1)} %convert_element_type.18), channel_id=1, source_target_pairs={{9,0},{11,2},{3,4},{1,6},{15,8},{13,10},{5,12},{7,14},{4,1},{6,3},... | collective-permute-start | bytes 202760 | tf_op jit(solution)/shard_map/ppermute | solution.py:318
  24.7 1.3 %collective-permute-start.7 = (f16[8,4224]{1,0:T(8,128)(2,1)S(1)}, f16[8,4224]{1,0:T(8,128)(2,1)S(1)}, u32[]{:S(2)}, u32[]{:S(2)}) collective-permute-start(f16[8,4224]{1,0:T(8,128)(2,1)S(1)} %collective-permute-done.6), channel_id=1, source_target_pairs={{0,1},{1,0},{2,3},{3,2},{4,5},{5,4},{6,7},{7,6},{8,9},{9,8},{10,11... | collective-permute-start | bytes 202760 | tf_op jit(solution)/shard_map/ppermute | solution.py:309
  26.1 4.3 %collective-permute-start.8 = (f16[8,4224]{1,0:T(8,128)(2,1)S(1)}, f16[8,4224]{1,0:T(8,128)(2,1)S(1)}, u32[]{:S(2)}, u32[]{:S(2)}) collective-permute-start(f16[8,4224]{1,0:T(8,128)(2,1)S(1)} %convert_element_type.21), channel_id=1, source_target_pairs={{2,0},{0,2},{8,4},{10,6},{4,8},{6,10},{14,12},{12,14},{9,1},{11,3}... | collective-permute-start | bytes 202760 | tf_op jit(solution)/shard_map/ppermute | solution.py:318
  30.4 1.4 %collective-permute-start.9 = (f16[8,4224]{1,0:T(8,128)(2,1)S(1)}, f16[8,4224]{1,0:T(8,128)(2,1)S(1)}, u32[]{:S(2)}, u32[]{:S(2)}) collective-permute-start(f16[8,4224]{1,0:T(8,128)(2,1)S(1)} %collective-permute-done.8), channel_id=1, source_target_pairs={{0,1},{1,0},{2,3},{3,2},{4,5},{5,4},{6,7},{7,6},{8,9},{9,8},{10,11... | collective-permute-start | bytes 202760 | tf_op jit(solution)/shard_map/ppermute | solution.py:309

commit v9 on v8

--- a/solution.py
+++ b/solution.py
@@ -410,7 +410,7 @@
     mine, code = small_kernel(
         add_cores_kernel, "add_cores", (partial, other), (wide, wide)
     )
-    heard_first = heard(code, ROUNDS_OF_8[0][::-1], 1)
+    heard_first = heard(code, ROUNDS_OF_8[0], 0)
     total, code = small_kernel(
         add_first_kernel, "add_first", (mine, *heard_first), (narrow, wide)
     )

time: 32.8 us -> 32.8 us (level)
    ppermute x4, starting transfers between devices: 8.59 us -> 8.98 us  [receive(): return lax.ppermute(value, ('dp', 'tensor'), pairs)]
where the time goes in v9:
time: 32.8 us; the launch traced here: 32.7 us
  waiting for transfers between devices  14.3 us (44%)
  starting transfers between devices  10.6 us (32%)
  Pallas kernels  7.56 us (23%)
    ppermute x4, starting transfers between devices, receive(): return lax.ppermute(value, ('dp', 'tensor'), pairs)  8.98 us
    ppermute x4, waiting for transfers between devices, receive(): return lax.ppermute(value, ('dp', 'tensor'), pairs)  8.65 us
    ppermute x6, waiting for transfers between devices, swap(): return lax.ppermute(value, axis, [(i, i ^ bit) for i in range(size)])  5.69 us
    pallas_call x1, Pallas kernels, project(): pl.pallas_call(project_kernel, out_shape=jax.ShapeDtypeStruct((tokens, 2...  4.93 us
    ppermute x6, starting transfers between devices, swap(): return lax.ppermute(value, axis, [(i, i ^ bit) for i in range(size)])  1.64 us
    pallas_call x3, Pallas kernels, small_kernel(): pl.pallas_call(kernel, out_shape=[jax.ShapeDtypeStruct(shape, jnp.float32...  0.93 us
    pallas_call x1, Pallas kernels, precondition_rows(): pl.pallas_call(precondition_kernel, out_shape=jax.ShapeDtypeStruct((seqs,...  0.72 us
  transfers between devices with their start and end apart: 10, of which 10 were waited for; matrix products, arithmetic and copies ran while one was open for 0% of the time, Pallas kernels for 2%

profile of v9, /device:TPU:0, one launch (start us, length us, event | category | flops | bytes accessed | tf_op | source)
XLA Modules:
  0.0 32.7 jit_solution(12323135613025693596)
XLA Ops:
  0.0 0.0 copy-start
  0.0 4.9 %project.1.mine_ref = f32[512,128]{1,0:T(8,128)S(1)} custom-call(bf16[512,2048]{1,0:T(8,128)(2,1)} %layer_ref.1, bf16[512,7168]{1,0:T(8,128)(2,1)} %gate_ref.1, bf16[64,2048]{1,0:T(8,128)(2,1)} %in_ref.1, bf16[64,7168]{1,0:T(8,128)(2,1)} %out_ref.1), custom_call_target="tpu_custom_call" | custom-call | flops 603979776 | bytes 10616832 | tf_op jit(solution)/shard_map/project/pallas_call | solution.py:132
  4.9 0.5 %collective-permute-start = (f32[512,128]{1,0:T(8,128)S(1)}, f32[512,128]{1,0:T(8,128)S(1)}, u32[]{:S(2)}, u32[]{:S(2)}) collective-permute-start(f32[512,128]{1,0:T(8,128)S(1)} %project.1.mine_ref), channel_id=1, source_target_pairs={{0,1},{1,0},{2,3},{3,2},{4,5},{5,4},{6,7},{7,6},{8,9},{9,8},{10,11... | collective-permute-start | bytes 786440 | tf_op jit(solution)/shard_map/ppermute | solution.py:309
  5.5 1.2 %collective-permute-done.other_ref = f32[512,128]{1,0:T(8,128)S(1)} collective-permute-done((f32[512,128]{1,0:T(8,128)S(1)}, f32[512,128]{1,0:T(8,128)S(1)}, u32[]{:S(2)}, u32[]{:S(2)}) %collective-permute-start) | collective-permute-done | bytes 262176 | tf_op jit(solution)/shard_map/ppermute | solution.py:309
  6.6 0.4 %gradient.1 = (f32[8,512]{1,0:T(8,128)S(1)}, f32[3,512]{1,0:T(4,128)S(1)}) custom-call(f32[512,128]{1,0:T(8,128)S(1)} %project.1.mine_ref, f32[512,128]{1,0:T(8,128)S(1)} %collective-permute-done.other_ref), custom_call_target="tpu_custom_call" | custom-call | flops 4194304 | bytes 524288 | tf_op jit(solution)/shard_map/gradient/pallas_call | solution.py:180
  7.0 2.9 %collective-permute-start.1 = (f32[3,512]{1,0:T(4,128)S(1)}, f32[3,512]{1,0:T(4,128)S(1)}, u32[]{:S(2)}, u32[]{:S(2)}) collective-permute-start(f32[3,512]{1,0:T(4,128)S(1)} %get-tuple-element.17), channel_id=1, source_target_pairs={{4,0},{6,2},{0,4},{2,6},{12,8},{14,10},{8,12},{10,14},{9,1},{11,3}... | collective-permute-start | bytes 18440 | tf_op jit(solution)/shard_map/ppermute | solution.py:318
  10.0 1.6 %collective-permute-done.1.refs_1_ = f32[3,512]{1,0:T(4,128)S(1)} collective-permute-done((f32[3,512]{1,0:T(4,128)S(1)}, f32[3,512]{1,0:T(4,128)S(1)}, u32[]{:S(2)}, u32[]{:S(2)}) %collective-permute-start.1) | collective-permute-done | bytes 6176 | tf_op jit(solution)/shard_map/ppermute | solution.py:318
  11.6 0.3 collective-permute-start.2
  11.9 0.9 %collective-permute-done.2.refs_2_ = f32[3,512]{1,0:T(4,128)S(1)} collective-permute-done((f32[3,512]{1,0:T(4,128)S(1)}, f32[3,512]{1,0:T(4,128)S(1)}, u32[]{:S(2)}, u32[]{:S(2)}) %collective-permute-start.2) | collective-permute-done | bytes 6176 | tf_op jit(solution)/shard_map/ppermute | solution.py:309
  12.8 2.0 %collective-permute-start.3 = (f32[3,512]{1,0:T(4,128)S(1)}, f32[3,512]{1,0:T(4,128)S(1)}, u32[]{:S(2)}, u32[]{:S(2)}) collective-permute-start(f32[3,512]{1,0:T(4,128)S(1)} %get-tuple-element.18), channel_id=1, source_target_pairs={{2,0},{0,2},{8,4},{10,6},{4,8},{6,10},{14,12},{12,14},{9,1},{11,3}... | collective-permute-start | bytes 18440 | tf_op jit(solution)/shard_map/ppermute | solution.py:318
  14.7 1.7 %collective-permute-done.3.after_ref.token_ref.refs_1_ = f32[3,512]{1,0:T(4,128)S(1)} collective-permute-done((f32[3,512]{1,0:T(4,128)S(1)}, f32[3,512]{1,0:T(4,128)S(1)}, u32[]{:S(2)}, u32[]{:S(2)}) %collective-permute-start.3) | collective-permute-done | bytes 6176 | tf_op jit(solution)/shard_map/ppermute | solution.py:318
  16.4 0.3 collective-permute-start.4
  16.8 0.0 copy-done
  16.8 0.6 %split.1 = (bf16[256,4096]{1,0:T(8,128)(2,1)S(1)}, bf16[256,4096]{1,0:T(8,128)(2,1)S(1)}) custom-call(f32[3,512]{1,0:T(4,128)S(1)} %collective-permute-done.3.after_ref.token_ref.refs_1_, f32[256,4096]{1,0:T(8,128)S(1)} %copy-done), custom_call_target="tpu_custom_call" | custom-call | bytes 8388608 | tf_op jit(solution)/shard_map/split/pallas_call | solution.py:240
  17.3 0.3 collective-permute-done.4.refs_2_
  17.6 0.0 copy-start.1
  17.6 0.7 %precondition.1.mine_ref = f32[8,4224]{1,0:T(8,128)S(1)} custom-call(f32[3,512]{1,0:T(4,128)S(1)} %collective-permute-done.3.after_ref.token_ref.refs_1_, f32[3,512]{1,0:T(4,128)S(1)} %get-tuple-element.19.refs_0_, f32[3,512]{1,0:T(4,128)S(1)} %collective-permute-done.3.after_ref.token_ref.refs_1_, f32[3,512]{1,0:T(4,128)S(1)} %collective-permute-done.4.refs_2_, ...), custom_call_target="tpu_custom_call" | custom-call | flops 16777216 | bytes 4194304 | tf_op jit(solution)/shard_map/precondition/pallas_call | solution.py:286
  18.3 0.3 %collective-permute-start.5 = (f32[8,4224]{1,0:T(8,128)S(1)}, f32[8,4224]{1,0:T(8,128)S(1)}, u32[]{:S(2)}, u32[]{:S(2)}) collective-permute-start(f32[8,4224]{1,0:T(8,128)S(1)} %precondition.1.mine_ref), channel_id=1, source_target_pairs={{0,1},{1,0},{2,3},{3,2},{4,5},{5,4},{6,7},{7,6},{8,9},{9,8},{10,11... | collective-permute-start | bytes 405512 | tf_op jit(solution)/shard_map/ppermute | solution.py:309
  18.7 1.0 %collective-permute-done.5.other_ref = f32[8,4224]{1,0:T(8,128)S(1)} collective-permute-done((f32[8,4224]{1,0:T(8,128)S(1)}, f32[8,4224]{1,0:T(8,128)S(1)}, u32[]{:S(2)}, u32[]{:S(2)}) %collective-permute-start.5) | collective-permute-done | bytes 135200 | tf_op jit(solution)/shard_map/ppermute | solution.py:309
  19.8 2.1 %collective-permute-start.6 = (f16[8,4224]{1,0:T(8,128)(2,1)S(1)}, f16[8,4224]{1,0:T(8,128)(2,1)S(1)}, u32[]{:S(2)}, u32[]{:S(2)}) collective-permute-start(f16[8,4224]{1,0:T(8,128)(2,1)S(1)} %convert_element_type.18), channel_id=1, source_target_pairs={{4,0},{6,2},{0,4},{2,6},{12,8},{14,10},{8,12},{10,14},{9,1},{11,3}... | collective-permute-start | bytes 202760 | tf_op jit(solution)/shard_map/ppermute | solution.py:318
  21.9 3.0 %collective-permute-done.6 = f16[8,4224]{1,0:T(8,128)(2,1)S(1)} collective-permute-done((f16[8,4224]{1,0:T(8,128)(2,1)S(1)}, f16[8,4224]{1,0:T(8,128)(2,1)S(1)}, u32[]{:S(2)}, u32[]{:S(2)}) %collective-permute-start.6) | collective-permute-done | bytes 67616 | tf_op jit(solution)/shard_map/ppermute | solution.py:318
  24.8 0.0 collective-permute-start.7
  24.9 1.2 %collective-permute-done.7 = f16[8,4224]{1,0:T(8,128)(2,1)S(1)} collective-permute-done((f16[8,4224]{1,0:T(8,128)(2,1)S(1)}, f16[8,4224]{1,0:T(8,128)(2,1)S(1)}, u32[]{:S(2)}, u32[]{:S(2)}) %collective-permute-start.7) | collective-permute-done | bytes 67616 | tf_op jit(solution)/shard_map/ppermute | solution.py:309
  26.2 2.0 %collective-permute-start.8 = (f16[8,4224]{1,0:T(8,128)(2,1)S(1)}, f16[8,4224]{1,0:T(8,128)(2,1)S(1)}, u32[]{:S(2)}, u32[]{:S(2)}) collective-permute-start(f16[8,4224]{1,0:T(8,128)(2,1)S(1)} %convert_element_type.21), channel_id=1, source_target_pairs={{2,0},{0,2},{8,4},{10,6},{4,8},{6,10},{14,12},{12,14},{9,1},{11,3}... | collective-permute-start | bytes 202760 | tf_op jit(solution)/shard_map/ppermute | solution.py:318
  28.2 2.3 %collective-permute-done.8 = f16[8,4224]{1,0:T(8,128)(2,1)S(1)} collective-permute-done((f16[8,4224]{1,0:T(8,128)(2,1)S(1)}, f16[8,4224]{1,0:T(8,128)(2,1)S(1)}, u32[]{:S(2)}, u32[]{:S(2)}) %collective-permute-start.8) | collective-permute-done | bytes 67616 | tf_op jit(solution)/shard_map/ppermute | solution.py:318
  30.5 0.2 collective-permute-start.9
  30.7 1.1 %collective-permute-done.9 = f16[8,4224]{1,0:T(8,128)(2,1)S(1)} collective-permute-done((f16[8,4224]{1,0:T(8,128)(2,1)S(1)}, f16[8,4224]{1,0:T(8,128)(2,1)S(1)}, u32[]{:S(2)}, u32[]{:S(2)}) %collective-permute-start.9) | collective-permute-done | bytes 67616 | tf_op jit(solution)/shard_map/ppermute | solution.py:309
  31.8 0.0 copy-done.1
  31.8 0.9 %score.1 = f32[8,64]{1,0:T(8,128)} custom-call(f32[8,4096]{1,0:T(8,128)S(1)} %get-tuple-element.25.sum_ref, f32[8,4224]{1,0:T(8,128)S(1)} %convert_element_type.22.got_ref, f32[8,4224]{1,0:T(8,128)S(1)} %convert_element_type.23.swapped_ref, bf16[64,4096]{1,0:T(8,128)(2,1)S(1)} %copy-done.1), custom_call_target="tpu_custom_call" | custom-call | tf_op jit(solution)/shard_map/score/pallas_call | solution.py:390
  (9 shorter events, 0.2 us)
Async XLA Ops:
  0.0 16.8 %copy-start = (f32[256,4096]{1,0:T(8,128)S(1)}, f32[256,4096]{1,0:T(8,128)}, u32[]{:S(2)}) copy-start(f32[256,4096]{1,0:T(8,128)} %refs_0_) | copy-start | bytes 12582916
  4.9 1.7 %collective-permute-start = (f32[512,128]{1,0:T(8,128)S(1)}, f32[512,128]{1,0:T(8,128)S(1)}, u32[]{:S(2)}, u32[]{:S(2)}) collective-permute-start(f32[512,128]{1,0:T(8,128)S(1)} %project.1.mine_ref), channel_id=1, source_target_pairs={{0,1},{1,0},{2,3},{3,2},{4,5},{5,4},{6,7},{7,6},{8,9},{9,8},{10,11... | collective-permute-start | bytes 786440 | tf_op jit(solution)/shard_map/ppermute | solution.py:309
  7.0 4.6 %collective-permute-start.1 = (f32[3,512]{1,0:T(4,128)S(1)}, f32[3,512]{1,0:T(4,128)S(1)}, u32[]{:S(2)}, u32[]{:S(2)}) collective-permute-start(f32[3,512]{1,0:T(4,128)S(1)} %get-tuple-element.17), channel_id=1, source_target_pairs={{4,0},{6,2},{0,4},{2,6},{12,8},{14,10},{8,12},{10,14},{9,1},{11,3}... | collective-permute-start | bytes 18440 | tf_op jit(solution)/shard_map/ppermute | solution.py:318
  11.6 1.2 %collective-permute-start.2 = (f32[3,512]{1,0:T(4,128)S(1)}, f32[3,512]{1,0:T(4,128)S(1)}, u32[]{:S(2)}, u32[]{:S(2)}) collective-permute-start(f32[3,512]{1,0:T(4,128)S(1)} %collective-permute-done.1.refs_1_), channel_id=1, source_target_pairs={{0,1},{1,0},{2,3},{3,2},{4,5},{5,4},{6,7},{7,6},{8,9},{9,8},{10,11... | collective-permute-start | bytes 18440 | tf_op jit(solution)/shard_map/ppermute | solution.py:309
  12.8 3.7 %collective-permute-start.3 = (f32[3,512]{1,0:T(4,128)S(1)}, f32[3,512]{1,0:T(4,128)S(1)}, u32[]{:S(2)}, u32[]{:S(2)}) collective-permute-start(f32[3,512]{1,0:T(4,128)S(1)} %get-tuple-element.18), channel_id=1, source_target_pairs={{2,0},{0,2},{8,4},{10,6},{4,8},{6,10},{14,12},{12,14},{9,1},{11,3}... | collective-permute-start | bytes 18440 | tf_op jit(solution)/shard_map/ppermute | solution.py:318
  16.4 1.2 %collective-permute-start.4 = (f32[3,512]{1,0:T(4,128)S(1)}, f32[3,512]{1,0:T(4,128)S(1)}, u32[]{:S(2)}, u32[]{:S(2)}) collective-permute-start(f32[3,512]{1,0:T(4,128)S(1)} %collective-permute-done.3.after_ref.token_ref.refs_1_), channel_id=1, source_target_pairs={{0,1},{1,0},{2,3},{3,2},{4,5},{5,4},{6,7},{7,6},{8,9},{9,8},{10,11... | collective-permute-start | bytes 18440 | tf_op jit(solution)/shard_map/ppermute | solution.py:309
  17.6 14.2 %copy-start.1 = (bf16[64,4096]{1,0:T(8,128)(2,1)S(1)}, bf16[64,4096]{1,0:T(8,128)(2,1)}, u32[]{:S(2)}) copy-start(bf16[64,4096]{1,0:T(8,128)(2,1)} %query_ref.1) | copy-start | bytes 1572868
  18.3 1.4 %collective-permute-start.5 = (f32[8,4224]{1,0:T(8,128)S(1)}, f32[8,4224]{1,0:T(8,128)S(1)}, u32[]{:S(2)}, u32[]{:S(2)}) collective-permute-start(f32[8,4224]{1,0:T(8,128)S(1)} %precondition.1.mine_ref), channel_id=1, source_target_pairs={{0,1},{1,0},{2,3},{3,2},{4,5},{5,4},{6,7},{7,6},{8,9},{9,8},{10,11... | collective-permute-start | bytes 405512 | tf_op jit(solution)/shard_map/ppermute | solution.py:309
  19.8 5.1 %collective-permute-start.6 = (f16[8,4224]{1,0:T(8,128)(2,1)S(1)}, f16[8,4224]{1,0:T(8,128)(2,1)S(1)}, u32[]{:S(2)}, u32[]{:S(2)}) collective-permute-start(f16[8,4224]{1,0:T(8,128)(2,1)S(1)} %convert_element_type.18), channel_id=1, source_target_pairs={{4,0},{6,2},{0,4},{2,6},{12,8},{14,10},{8,12},{10,14},{9,1},{11,3}... | collective-permute-start | bytes 202760 | tf_op jit(solution)/shard_map/ppermute | solution.py:318
  24.8 1.3 %collective-permute-start.7 = (f16[8,4224]{1,0:T(8,128)(2,1)S(1)}, f16[8,4224]{1,0:T(8,128)(2,1)S(1)}, u32[]{:S(2)}, u32[]{:S(2)}) collective-permute-start(f16[8,4224]{1,0:T(8,128)(2,1)S(1)} %collective-permute-done.6), channel_id=1, source_target_pairs={{0,1},{1,0},{2,3},{3,2},{4,5},{5,4},{6,7},{7,6},{8,9},{9,8},{10,11... | collective-permute-start | bytes 202760 | tf_op jit(solution)/shard_map/ppermute | solution.py:309
  26.2 4.3 %collective-permute-start.8 = (f16[8,4224]{1,0:T(8,128)(2,1)S(1)}, f16[8,4224]{1,0:T(8,128)(2,1)S(1)}, u32[]{:S(2)}, u32[]{:S(2)}) collective-permute-start(f16[8,4224]{1,0:T(8,128)(2,1)S(1)} %convert_element_type.21), channel_id=1, source_target_pairs={{2,0},{0,2},{8,4},{10,6},{4,8},{6,10},{14,12},{12,14},{9,1},{11,3}... | collective-permute-start | bytes 202760 | tf_op jit(solution)/shard_map/ppermute | solution.py:318
  30.5 1.3 %collective-permute-start.9 = (f16[8,4224]{1,0:T(8,128)(2,1)S(1)}, f16[8,4224]{1,0:T(8,128)(2,1)S(1)}, u32[]{:S(2)}, u32[]{:S(2)}) collective-permute-start(f16[8,4224]{1,0:T(8,128)(2,1)S(1)} %collective-permute-done.8), channel_id=1, source_target_pairs={{0,1},{1,0},{2,3},{3,2},{4,5},{5,4},{6,7},{7,6},{8,9},{9,8},{10,11... | collective-permute-start | bytes 202760 | tf_op jit(solution)/shard_map/ppermute | solution.py:309
